TPU v7x, 128 devices: a whole 4x4x4 slice. The times are simulated.
128 devices in a mesh: row: 8 (over y, z_lo), col: 16 (over z_hi, x, core).
Axes of the slice: x: 4, y: 4, z: 4 (z_hi: 2, z_lo: 2; z = z_hi * 2 + z_lo), core: 2. Of those that a mesh axis runs over, the one named last changes fastest.
Arguments:
- image: bfloat16 [128, 1024, 256], P('row', 'col'), may hold values from -7 to 7
- out_cotangent: bfloat16 [128, 1024, 256], P('row', 'col'), may hold values from -6 to 6
- norm0_gain: bfloat16 [256], replicated, may hold values from 0.099609375 to 1.8984375
- w_expand: bfloat16 [256, 1024], replicated, may hold values from -0.375 to 0.375
- w_depth: bfloat16 [3, 3, 1024], replicated, may hold values from -2 to 2
- w_squeeze: bfloat16 [1024, 64], replicated, may hold values from -0.75 to 0.75
- w_excite: bfloat16 [64, 1024], replicated, may hold values from -3 to 3
- w_project: bfloat16 [1024, 256], replicated, may hold values from -0.1875 to 0.1875
- norm1_gain: bfloat16 [256], replicated, may hold values from 0.099609375 to 1.8984375
- w_qkv: bfloat16 [256, 768], replicated, may hold values from -0.375 to 0.375
- w_out: bfloat16 [256, 256], replicated, may hold values from -0.375 to 0.375
- attn_bias: float32 [8, 64, 64], replicated, may hold values from -2 to 250
Outputs:
- block_out: bfloat16 [128, 1024, 256], P('row', 'col')
- grad_image: bfloat16 [128, 1024, 256], P('row', 'col')
- grad_norm0: float32 [256], replicated
- grad_expand: float32 [256, 1024], replicated
- grad_depth: float32 [3, 3, 1024], replicated
- grad_squeeze: float32 [1024, 64], replicated
- grad_excite: float32 [64, 1024], replicated
- grad_project: float32 [1024, 256], replicated
- grad_norm1: float32 [256], replicated
- grad_qkv: float32 [256, 768], replicated
- grad_out_proj: float32 [256, 256], replicated
- grad_bias: float32 [8, 64, 64], replicated
All inputs are finite; a program needn't handle non-finite values.
Results may differ from a plain program's by a relative error of at most 0.015.
Values may be sent and summed in bfloat16 or wider, within the bound.
A program may use at most 128 MiB of HBM per device.

v0:
```python
import jax
import jax.numpy as jnp
from jax import lax
from jax.sharding import PartitionSpec as P

GRID = 8


def with_halo(cells, sides, width):
    for axis, dim in sides:
        count = lax.axis_size(axis)
        ends = count - 1
        head = lax.slice_in_dim(cells, 0, width, axis=dim)
        tail = lax.slice_in_dim(cells, cells.shape[dim] - width, cells.shape[dim], axis=dim)
        cells = jnp.concatenate(
            [
                lax.ppermute(tail, axis, [(i, (i + 1) % count) for i in range(ends)]),
                cells,
                lax.ppermute(head, axis, [((i + 1) % count, i) for i in range(ends)]),
            ],
            axis=dim,
        )
    return cells


def norm_tokens(values, scale_gain):
    average = jnp.mean(values, axis=-1, keepdims=True)
    centered = values - average
    variance = jnp.mean(centered * centered, axis=-1, keepdims=True)
    return centered * lax.rsqrt(variance + 1e-05) * scale_gain


def matmul_last(left_side, right_side):
    flat_rows = left_side.reshape(-1, left_side.shape[-1])
    product = jnp.dot(flat_rows, right_side, preferred_element_type=jnp.float32)
    return product.reshape(left_side.shape[:-1] + (right_side.shape[-1],))


def smooth_gelu(values):
    return jax.nn.gelu(values, approximate=True)


def depthwise(padded, kernel, row_count, col_count):
    accumulated = jnp.zeros((row_count, col_count, padded.shape[-1]), jnp.float32)
    for shift_row in range(3):
        for shift_col in range(3):
            window = padded[
                shift_row : shift_row + row_count, shift_col : shift_col + col_count
            ].astype(jnp.float32)
            accumulated = accumulated + window * kernel[shift_row, shift_col].astype(jnp.float32)
    return accumulated


def depthwise_back(padded_grad, kernel, row_count, col_count):
    accumulated = jnp.zeros((row_count, col_count, padded_grad.shape[-1]), jnp.float32)
    for shift_row in range(3):
        for shift_col in range(3):
            window = padded_grad[
                2 - shift_row : 2 - shift_row + row_count, 2 - shift_col : 2 - shift_col + col_count
            ].astype(jnp.float32)
            accumulated = accumulated + window * kernel[shift_row, shift_col].astype(jnp.float32)
    return accumulated


def kernel_grad(padded, grad_pre, row_count, col_count):
    kernel_terms = []
    for shift_row in range(3):
        for shift_col in range(3):
            window = padded[
                shift_row : shift_row + row_count, shift_col : shift_col + col_count
            ].astype(jnp.float32)
            kernel_terms.append(jnp.sum(window * grad_pre.astype(jnp.float32), axis=(0, 1)))
    return jnp.stack(kernel_terms).reshape(3, 3, padded.shape[-1])


def excite_gate(pooled, squeeze_wide, excite_wide):
    hidden = jax.nn.silu(jnp.dot(pooled[None, :], squeeze_wide, precision=lax.Precision.HIGHEST))
    return jax.nn.sigmoid(jnp.dot(hidden, excite_wide, precision=lax.Precision.HIGHEST))[0]


def into_groups(values):
    row_count, col_count, channels = values.shape
    parted = values.reshape(GRID, row_count // GRID, GRID, col_count // GRID, channels).transpose(
        1, 3, 0, 2, 4
    )
    return parted.reshape(-1, GRID * GRID, channels)


def from_groups(values, row_count, col_count):
    channels = values.shape[-1]
    parted = values.reshape(row_count // GRID, col_count // GRID, GRID, GRID, channels).transpose(
        2, 0, 3, 1, 4
    )
    return parted.reshape(row_count, col_count, channels)


def flat_order_out(values):
    row_count, col_count, channels = values.shape
    row_devices = lax.axis_size("row")
    col_devices = lax.axis_size("col")
    ordered = values.reshape(
        row_count // row_devices, row_devices, col_count // col_devices, col_devices, channels
    )
    return ordered.transpose(1, 3, 0, 2, 4).reshape(
        row_devices * col_devices, row_count // row_devices, col_count // col_devices, channels
    )


def flat_order_in(arrived, row_count, col_count):
    channels = arrived.shape[-1]
    row_devices = lax.axis_size("row")
    col_devices = lax.axis_size("col")
    arrived = arrived.reshape(
        row_devices, col_devices, row_count // row_devices, col_count // col_devices, channels
    )
    return arrived.transpose(0, 2, 1, 3, 4).reshape(row_count, col_count, channels)


def flat_back_out(values):
    row_count, col_count, channels = values.shape
    row_devices = lax.axis_size("row")
    col_devices = lax.axis_size("col")
    ordered = values.reshape(
        row_devices, row_count // row_devices, col_devices, col_count // col_devices, channels
    )
    return ordered.transpose(0, 2, 1, 3, 4).reshape(
        row_devices * col_devices, row_count // row_devices, col_count // col_devices, channels
    )


def flat_back_in(arrived, row_count, col_count):
    channels = arrived.shape[-1]
    row_devices = lax.axis_size("row")
    col_devices = lax.axis_size("col")
    arrived = arrived.reshape(
        row_devices, col_devices, row_count // row_devices, col_count // col_devices, channels
    )
    return arrived.transpose(2, 0, 3, 1, 4).reshape(row_count, col_count, channels)


def to_grid(values):
    row_count, col_count, channels = values.shape
    arrived = lax.all_to_all(
        flat_order_out(values), ("row", "col"), split_axis=0, concat_axis=0, tiled=True
    )
    return flat_order_in(arrived, row_count, col_count)


def from_grid(values):
    row_count, col_count, channels = values.shape
    arrived = lax.all_to_all(
        flat_back_out(values), ("row", "col"), split_axis=0, concat_axis=0, tiled=True
    )
    return flat_back_in(arrived, row_count, col_count)


def attention_core(normed_groups, w_qkv, attn_bias):
    groups, members, channels = normed_groups.shape
    head_count = attn_bias.shape[0]
    head_dim = channels // head_count
    packed = (
        matmul_last(normed_groups, w_qkv)
        .astype(jnp.bfloat16)
        .reshape(groups, members, 3, head_count, head_dim)
    )
    queries = packed[:, :, 0]
    key_rows = packed[:, :, 1]
    values = packed[:, :, 2]
    scores = jnp.einsum(
        "gihd,gjhd->ghij", queries, key_rows, preferred_element_type=jnp.float32
    ) * head_dim ** (-0.5)
    scores = scores + attn_bias[None]
    row_max = jnp.max(scores, axis=-1, keepdims=True)
    lifted = jnp.exp(scores - row_max)
    softmaxed = lifted / jnp.sum(lifted, axis=-1, keepdims=True)
    attended = jnp.einsum(
        "ghij,gjhd->gihd",
        softmaxed.astype(jnp.bfloat16),
        values,
        preferred_element_type=jnp.float32,
    ).astype(jnp.bfloat16)
    return (attended.reshape(groups, members, channels), queries, key_rows, values, softmaxed)


def attention_back(grad_att, queries, key_rows, values, softmaxed):
    groups, members, channels = grad_att.shape
    head_count = queries.shape[2]
    head_dim = channels // head_count
    grad_heads = grad_att.reshape(groups, members, head_count, head_dim)
    grad_values = jnp.einsum(
        "ghij,gihd->gjhd",
        softmaxed.astype(jnp.bfloat16),
        grad_heads,
        preferred_element_type=jnp.float32,
    ).astype(jnp.bfloat16)
    grad_probs = jnp.einsum(
        "gihd,gjhd->ghij", grad_heads, values, preferred_element_type=jnp.float32
    )
    grad_scores = softmaxed * (grad_probs - jnp.sum(grad_probs * softmaxed, axis=-1, keepdims=True))
    bias_part = jnp.sum(grad_scores, axis=0)
    scaled = (grad_scores * head_dim ** (-0.5)).astype(jnp.bfloat16)
    grad_queries = jnp.einsum(
        "ghij,gjhd->gihd", scaled, key_rows, preferred_element_type=jnp.float32
    ).astype(jnp.bfloat16)
    grad_keys = jnp.einsum(
        "ghij,gihd->gjhd", scaled, queries, preferred_element_type=jnp.float32
    ).astype(jnp.bfloat16)
    stacked = jnp.stack([grad_queries, grad_keys, grad_values], axis=2)
    return (stacked.reshape(groups, members, 3 * channels), bias_part)


def on_device(
    image,
    out_cotangent,
    norm0_gain,
    w_expand,
    w_depth,
    w_squeeze,
    w_excite,
    w_project,
    norm1_gain,
    w_qkv,
    w_out,
    attn_bias,
):
    row_count, col_count, channels = image.shape
    cells_total = row_count * lax.axis_size("row") * col_count * lax.axis_size("col")
    image_float = image.astype(jnp.float32)
    gain_first = norm0_gain.astype(jnp.float32)
    gain_second = norm1_gain.astype(jnp.float32)
    normed_first = norm_tokens(image_float, gain_first).astype(jnp.bfloat16)
    expanded = matmul_last(normed_first, w_expand)
    spread = smooth_gelu(expanded).astype(jnp.bfloat16)
    padded = with_halo(spread, (("row", 0), ("col", 1)), 1)
    depth_pre = depthwise(padded, w_depth, row_count, col_count)
    activated = smooth_gelu(depth_pre)
    pooled = lax.psum(jnp.sum(activated, axis=(0, 1)), ("row", "col")) / cells_total
    squeeze_wide = w_squeeze.astype(jnp.float32)
    excite_wide = w_excite.astype(jnp.float32)
    channel_gate = excite_gate(pooled, squeeze_wide, excite_wide)
    gated_act = (activated * channel_gate).astype(jnp.bfloat16)
    mixed_map = (image_float + matmul_last(gated_act, w_project)).astype(jnp.bfloat16)
    mixed_float = mixed_map.astype(jnp.float32)
    normed_second = norm_tokens(mixed_float, gain_second).astype(jnp.bfloat16)
    grad_att = matmul_last(out_cotangent, w_out.T).astype(jnp.bfloat16)
    grid_normed = into_groups(to_grid(normed_second))
    attended_groups, queries, key_rows, values, softmaxed = attention_core(
        grid_normed, w_qkv, attn_bias
    )
    attended_map = from_grid(from_groups(attended_groups, row_count, col_count))
    grid_grad = into_groups(to_grid(grad_att))
    grad_packed, grad_bias = attention_back(grid_grad, queries, key_rows, values, softmaxed)
    grad_qkv = jnp.dot(
        grid_normed.reshape(-1, channels).T,
        grad_packed.reshape(-1, 3 * channels),
        preferred_element_type=jnp.float32,
    )
    grad_normed_grid = matmul_last(grad_packed, w_qkv.T).astype(jnp.bfloat16)
    grad_normed = from_grid(from_groups(grad_normed_grid, row_count, col_count))
    block_out = (mixed_float + matmul_last(attended_map, w_out)).astype(jnp.bfloat16)
    grad_out_proj = jnp.dot(
        attended_map.reshape(-1, channels).T,
        out_cotangent.reshape(-1, channels),
        preferred_element_type=jnp.float32,
    )
    unused_second, norm_second_vjp = jax.vjp(norm_tokens, mixed_float, gain_second)
    grad_mixed_norm, grad_norm1 = norm_second_vjp(grad_normed.astype(jnp.float32))
    grad_mixed = out_cotangent.astype(jnp.float32) + grad_mixed_norm
    grad_mixed_b = grad_mixed.astype(jnp.bfloat16)
    grad_project = jnp.dot(
        gated_act.reshape(-1, gated_act.shape[-1]).T,
        grad_mixed_b.reshape(-1, channels),
        preferred_element_type=jnp.float32,
    )
    grad_gated = matmul_last(grad_mixed_b, w_project.T)
    grad_gate = lax.psum(jnp.sum(grad_gated * activated, axis=(0, 1)), ("row", "col"))
    unused_gate, gate_vjp = jax.vjp(excite_gate, pooled, squeeze_wide, excite_wide)
    grad_pooled, grad_squeeze, grad_excite = gate_vjp(grad_gate)
    grad_activated = grad_gated * channel_gate + grad_pooled / cells_total
    unused_act, gelu_depth_vjp = jax.vjp(smooth_gelu, depth_pre)
    grad_depth_pre = gelu_depth_vjp(grad_activated)[0].astype(jnp.bfloat16)
    grad_pad = with_halo(grad_depth_pre, (("row", 0), ("col", 1)), 1)
    grad_spread = depthwise_back(grad_pad, w_depth, row_count, col_count)
    grad_depth = kernel_grad(padded, grad_depth_pre, row_count, col_count)
    unused_spread, gelu_expand_vjp = jax.vjp(smooth_gelu, expanded)
    grad_expanded = gelu_expand_vjp(grad_spread)[0].astype(jnp.bfloat16)
    grad_expand = jnp.dot(
        normed_first.reshape(-1, channels).T,
        grad_expanded.reshape(-1, grad_expanded.shape[-1]),
        preferred_element_type=jnp.float32,
    )
    grad_first = matmul_last(grad_expanded, w_expand.T)
    unused_first, norm_first_vjp = jax.vjp(norm_tokens, image_float, gain_first)
    grad_image_norm, grad_norm0 = norm_first_vjp(grad_first)
    grad_image = (grad_mixed + grad_image_norm).astype(jnp.bfloat16)
    summed = lax.psum(
        (
            grad_norm0,
            grad_expand,
            grad_depth,
            grad_project,
            grad_norm1,
            grad_qkv,
            grad_out_proj,
            grad_bias,
        ),
        ("row", "col"),
    )
    return (
        block_out,
        grad_image,
        summed[0],
        summed[1],
        summed[2],
        grad_squeeze,
        grad_excite,
        summed[3],
        summed[4],
        summed[5],
        summed[6],
        summed[7],
    )


def solution(mesh):
    placed = (
        P("row", "col", None),
        P("row", "col", None),
        P(),
        P(),
        P(),
        P(),
        P(),
        P(),
        P(),
        P(),
        P(),
        P(),
    )
    return jax.shard_map(
        on_device,
        mesh=mesh,
        in_specs=placed,
        out_specs=(
            P("row", "col", None),
            P("row", "col", None),
            P(),
            P(),
            P(),
            P(),
            P(),
            P(),
            P(),
            P(),
            P(),
            P(),
        ),
        check_vma=False,
    )
```

profile of v0, /device:TPU:1, one launch (start us, length us, event | category | flops | bytes accessed | tf_op | source)
XLA Modules:
  0.0 525.6 jit_solution(3804619641046596437)
XLA Ops:
  10.7 4.6 multiply_convert_fusion.2
  16.0 4.4 collective-permute-start
  23.2 12.9 %all-to-all-start.2 = ((bf16[128,2,4,256]{3,2,1,0:T(4,128)(2,1)}), bf16[128,2,4,256]{3,2,1,0:T(4,128)(2,1)}, u32[]{:S(2)}, u32[]{:S(2)}) async-start(bf16[128,2,4,256]{3,2,1,0:T(4,128)(2,1)} %copy.140), calls=%async_computation.2 | async-start | bytes 1048576 | tf_op jit(solution)/shard_map/all_to_all | solution.py:143
  36.3 3.5 collective-permute-start.2
  39.8 1.9 collective-permute-start.3
  41.9 3.9 collective-permute-done.3
  45.9 3.3 maximum_maximum_fusion
  49.2 7.5 %fusion.104 = (f32[1024]{0:T(1024)S(1)}, f32[16,64,1024]{2,1,0:T(8,128)}) fusion(f32[1024]{0:T(1024)S(1)} %bitcast.218, bf16[18,65,1024]{2,1,0:T(8,128)(2,1)S(1)} %get-tuple-element.71, f32[1024]{0:T(1024)S(1)} %bitcast.220, bf16[1,64,1024]{2,1,0:T(8,128)(2,1)S(1)} %collective-permute-done.1, bf16[16,64,1024]{2,1,0:T(8,128)(2,1)S(1)} %copy-done.3, ...), kind=kLoop, calls=%fused_computation.197 | loop fusion | flops 38796288 | bytes 19177472 | tf_op jit(solution)/shard_map/reduce_sum | solution.py:237
  56.8 69.6 %psum.70 = f32[1024]{0:T(1024)S(1)} all-reduce(f32[1024]{0:T(1024)S(1)} %get-tuple-element.64), channel_id=1, replica_groups=mesh['row'=8,'col'=16] {'row','col'}, use_global_device_ids=true, to_apply=%region_3.0 | all-reduce | flops 1024 | bytes 8192 | tf_op jit(solution)/shard_map/psum | solution.py:237
  126.4 1.7 fusion.101
  129.2 4.2 convert_reduce_fusion
  135.8 6.6 %all-to-all-start = ((bf16[128,2,4,256]{3,2,1,0:T(4,128)(2,1)}), bf16[128,2,4,256]{3,2,1,0:T(4,128)(2,1)}, u32[]{:S(2)}, u32[]{:S(2)}) async-start(bf16[128,2,4,256]{3,2,1,0:T(4,128)(2,1)} %copy.123), calls=%async_computation | async-start | bytes 1048576 | tf_op jit(solution)/shard_map/all_to_all | solution.py:143
  142.4 1.8 copy.131
  146.6 3.5 reshape_reshape.34
  150.1 3.0 copy.144
  153.1 2.6 all-to-all-done
  158.1 2.7 convolution_convert_fusion
  160.8 4.1 copy.127
  164.9 2.4 fusion.73
  172.1 5.8 %fusion.110 = (f32[8,64,64]{1,2,0:T(8,128)}, f32[16,8,64,64]{2,3,1,0:T(8,128)S(1)}) fusion(f32[16,8,64,64]{2,3,1,0:T(8,128)S(1)} %fusion.72, f32[16,8,64,64]{2,3,1,0:T(8,128)S(1)} %get-tuple-element.92, f32[16,8,64]{2,1,0:T(8,128)S(1)} %get-tuple-element.91), kind=kOutput, calls=%fused_computation.201 | output fusion | flops 3121215 | bytes 6455296 | tf_op jit(solution)/shard_map/sub | solution.py:199
  184.5 8.0 %all-to-all-start.3 = ((bf16[128,2,4,256]{3,2,1,0:T(4,128)(2,1)}), bf16[128,2,4,256]{3,2,1,0:T(4,128)(2,1)}, u32[]{:S(2)}, u32[]{:S(2)}) async-start(bf16[128,2,4,256]{3,2,1,0:T(4,128)(2,1)} %copy.153), calls=%async_computation.3 | async-start | bytes 1048576 | tf_op jit(solution)/shard_map/all_to_all | solution.py:151
  192.6 4.3 fusion.52
  196.9 3.8 copy.157
  200.7 3.0 copy.133
  203.7 3.8 reshape_reshape.31
  210.2 5.4 %reshape_reshape.37 = bf16[1024,768]{0,1:T(8,128)(2,1)} reshape(bf16[16,64,3,8,32]{1,0,4,3,2:T(8,128)(2,1)} %copy.157) | data formatting | bytes 3145728 | tf_op jit(solution)/shard_map/reshape;reshape | solution.py:34
  215.6 3.1 fusion.111
  218.7 10.2 %all-to-all-start.1 = ((bf16[128,2,4,256]{3,2,1,0:T(4,128)(2,1)}), bf16[128,2,4,256]{3,2,1,0:T(4,128)(2,1)}, u32[]{:S(2)}, u32[]{:S(2)}) async-start(bf16[128,2,4,256]{3,2,1,0:T(4,128)(2,1)} %copy.136), calls=%async_computation.1 | async-start | bytes 1048576 | tf_op jit(solution)/shard_map/all_to_all | solution.py:151
  232.9 2.7 convolution_bitcast_fusion
  235.6 3.1 multiply_reduce_fusion
  238.7 3.6 all-to-all-done.1
  244.3 63.8 %psum.71 = f32[1024]{0:T(1024)S(1)} all-reduce(f32[1024]{0:T(1024)S(1)} %get-tuple-element.93), channel_id=1, replica_groups=mesh['row'=8,'col'=16] {'row','col'}, use_global_device_ids=true, to_apply=%region_12.13 | all-reduce | flops 1024 | bytes 8192 | tf_op jit(solution)/shard_map/psum | solution.py:276
  310.3 12.4 %fusion.37 = (f32[1024]{0:T(1024)S(1)}, f32[1024]{0:T(1024)S(1)}, f32[1024]{0:T(1024)S(1)}, f32[1024]{0:T(1024)}, f32[1024]{0:T(1024)}, /*index=5*/f32[1024]{0:T...) fusion(bf16[18,65,1024]{2,1,0:T(8,128)(2,1)} %copy-done.1, ...), kind=kLoop, calls=%fused_computation.60 | loop fusion | flops 54516736 | bytes 25473024 | tf_op jit(solution)/shard_map/reduce_sum | solution.py:72
  322.7 1.7 collective-permute-start.4
  326.8 3.3 collective-permute-done.5
  330.3 4.3 collective-permute-start.6
  334.6 2.2 collective-permute-start.7
  338.2 1.5 pad_maximum_fusion.2
  339.8 7.8 %fusion.16 = bf16[16,64,1024]{2,1,0:T(8,128)(2,1)S(1)} fusion(f32[16,64,1024]{2,1,0:T(8,128)S(1)} %copy-done.24, bf16[16,64,1024]{2,1,0:T(8,128)(2,1)S(1)} %get-tuple-element.63, bf16[18,65,1024]{2,1,0:T(8,128)(2,1)S(1)} %get-tuple-element.67, bf16[1,64,1024]{2,1,0:T(8,128)(2,1)S(1)} %collective-permute-done.4, ...), kind=kLoop, calls=%fused_computation.39 | loop fusion | flops 50331648 | bytes 21270528 | tf_op jit(solution)/shard_map/convert_element_type | solution.py:286
  349.0 2.0 convolution_bitcast_fusion.1
  352.0 2.2 fusion.57
  354.3 2.4 fusion.67
  358.3 71.3 %all-reduce = (f32[256]{0:T(256)}, f32[3,3,1024]{2,1,0:T(4,128)}, f32[256]{0:T(256)}) all-reduce(f32[256]{0:T(256)S(1)} %get-tuple-element.53, f32[3,3,1024]{2,1,0:T(4,128)S(1)} %reshape.218, f32[256]{0:T(256)S(1)} %copy-done.44), channel_id=1, replica_groups=mesh['row'=8,'col'=16] {'row','col'}, use_global_device_ids=true, to_apply=%region_16.17 | all-reduce | flops 9728 | bytes 77824 | tf_op jit(solution)/shard_map/psum | solution.py:296
  429.7 3.0 add_convert_fusion
  432.7 77.8 %all-reduce.4.cloned.1.call-done = (f32[256,1024]{1,0:T(8,128)}, f32[1024,256]{1,0:T(8,128)}, f32[256,768]{1,0:T(8,128)}, f32[256,256]{1,0:T(8,128)}, f32[8,64,64]{1,2,0:T(8,128)}) async-done(((f32[256,1024]{1,0:T(8,128)}, f32[1024,256]{1,0:T(8,128)}, f32[256,768]{1,0:T(8,128)}, f32[256,256]{1,0:T(8,128)}, f32[8,64,64]{1,2,0:T(8,128)}), (f32[256,1024]{1,0:T(8,128)}, f32[1024,256]{1,0:T(8,128)}, ...) | async-done | bytes 3276816 | tf_op jit(solution)/shard_map/psum | solution.py:296
  510.5 1.9 copy.159
  512.4 2.3 copy.173
  514.7 2.3 copy.174
  (175 shorter events, 47.0 us)
Async XLA Ops:
  7.2 3.5 copy-start
  7.9 2.7 copy-start.42
  10.6 11.0 %copy-start.15 = (bf16[16,64,256]{2,1,0:T(8,128)(2,1)S(1)}, bf16[16,64,256]{2,1,0:T(8,128)(2,1)}, u32[]{:S(2)}) copy-start(bf16[16,64,256]{2,1,0:T(8,128)(2,1)} %param.13) | copy-start | bytes 1572868
  10.7 11.0 %copy-start.28 = (bf16[256,256]{1,0:T(8,128)(2,1)S(1)}, bf16[256,256]{1,0:T(8,128)(2,1)}, u32[]{:S(2)}) copy-start(bf16[256,256]{1,0:T(8,128)(2,1)} %param.22) | copy-start | bytes 393220
  15.2 26.7 %copy-start.2 = (bf16[16,64,1024]{2,1,0:T(8,128)(2,1)}, bf16[16,64,1024]{2,1,0:T(8,128)(2,1)S(1)}, u32[]{:S(2)}) copy-start(bf16[16,64,1024]{2,1,0:T(8,128)(2,1)S(1)} %get-tuple-element.87) | copy-start | bytes 6291460
  15.2 26.5 %copy-start.32 = (bf16[3,3,1024]{2,1,0:T(4,128)(2,1)S(1)}, bf16[3,3,1024]{2,1,0:T(4,128)(2,1)}, u32[]{:S(2)}) copy-start(bf16[3,3,1024]{2,1,0:T(4,128)(2,1)} %param.16) | copy-start | bytes 55300
  15.3 26.5 %copy-start.47 = (bf16[256]{0:T(256)(128)(2,1)S(1)}, bf16[256]{0:T(256)(128)(2,1)}, u32[]{:S(2)}) copy-start(bf16[256]{0:T(256)(128)(2,1)} %param.20) | copy-start | bytes 1540
  16.0 20.2 %collective-permute-start = (bf16[1,64,1024]{2,1,0:T(8,128)(2,1)}, bf16[1,64,1024]{2,1,0:T(8,128)(2,1)S(1)}, u32[]{:S(2)}, u32[]{:S(2)}) collective-permute-start(bf16[1,64,1024]{2,1,0:T(8,128)(2,1)} %get-tuple-element.76), channel_id=1, source_target_pairs={{0,16},{16,32},{32,48},{48,64},{64,80},{80,96},{96,112},{1,17},{17... | collective-permute-start | bytes 393224 | tf_op jit(solution)/shard_map/ppermute | solution.py:17
  20.3 15.8 %collective-permute-start.1 = (bf16[1,64,1024]{2,1,0:T(8,128)(2,1)}, bf16[1,64,1024]{2,1,0:T(8,128)(2,1)S(1)}, u32[]{:S(2)}, u32[]{:S(2)}) collective-permute-start(bf16[1,64,1024]{2,1,0:T(8,128)(2,1)} %get-tuple-element.77), channel_id=1, source_target_pairs={{16,0},{32,16},{48,32},{64,48},{80,64},{96,80},{112,96},{17,1},{33... | collective-permute-start | bytes 393224 | tf_op jit(solution)/shard_map/ppermute | solution.py:19
  23.2 112.6 %all-to-all-start.2 = ((bf16[128,2,4,256]{3,2,1,0:T(4,128)(2,1)}), bf16[128,2,4,256]{3,2,1,0:T(4,128)(2,1)}, u32[]{:S(2)}, u32[]{:S(2)}) async-start(bf16[128,2,4,256]{3,2,1,0:T(4,128)(2,1)} %copy.140), calls=%async_computation.2 | async-start | bytes 1048576 | tf_op jit(solution)/shard_map/all_to_all | solution.py:143
  36.3 5.7 %collective-permute-start.2 = (bf16[18,1,1024]{2,1,0:T(2,128)(2,1)S(1)}, bf16[18,1,1024]{2,1,0:T(2,128)(2,1)S(1)}, u32[]{:S(2)}, u32[]{:S(2)}) collective-permute-start(bf16[18,1,1024]{2,1,0:T(2,128)(2,1)S(1)} %get-tuple-element.72), channel_id=1, source_target_pairs={{0,1},{1,2},{2,3},{3,4},{4,5},{5,6},{6,7},{7,8},{8,9},{9,10},{10,1... | collective-permute-start | bytes 110600 | tf_op jit(solution)/shard_map/ppermute | solution.py:17
  39.8 6.1 %collective-permute-start.3 = (bf16[18,1,1024]{2,1,0:T(2,128)(2,1)S(1)}, bf16[18,1,1024]{2,1,0:T(2,128)(2,1)S(1)}, u32[]{:S(2)}, u32[]{:S(2)}) collective-permute-start(bf16[18,1,1024]{2,1,0:T(2,128)(2,1)S(1)} %get-tuple-element.73), channel_id=1, source_target_pairs={{1,0},{2,1},{3,2},{4,3},{5,4},{6,5},{7,6},{8,7},{9,8},{10,9},{11,1... | collective-permute-start | bytes 110600 | tf_op jit(solution)/shard_map/ppermute | solution.py:19
  45.9 3.3 copy-start.3
  49.2 7.6 %copy-start.1 = (bf16[18,65,1024]{2,1,0:T(8,128)(2,1)}, bf16[18,65,1024]{2,1,0:T(8,128)(2,1)S(1)}, u32[]{:S(2)}) copy-start(bf16[18,65,1024]{2,1,0:T(8,128)(2,1)S(1)} %get-tuple-element.71) | copy-start | bytes 7188484
  129.2 103.6 %copy-start.41 = (f32[1024]{0:T(1024)}, f32[1024]{0:T(1024)S(1)}, u32[]{:S(2)}) copy-start(f32[1024]{0:T(1024)S(1)} %add_divide_fusion) | copy-start | bytes 12292
  135.8 19.8 %all-to-all-start = ((bf16[128,2,4,256]{3,2,1,0:T(4,128)(2,1)}), bf16[128,2,4,256]{3,2,1,0:T(4,128)(2,1)}, u32[]{:S(2)}, u32[]{:S(2)}) async-start(bf16[128,2,4,256]{3,2,1,0:T(4,128)(2,1)} %copy.123), calls=%async_computation | async-start | bytes 1048576 | tf_op jit(solution)/shard_map/all_to_all | solution.py:143
  164.9 2.5 copy-start.11
  164.9 2.8 copy-start.22
  184.5 34.1 %all-to-all-start.3 = ((bf16[128,2,4,256]{3,2,1,0:T(4,128)(2,1)}), bf16[128,2,4,256]{3,2,1,0:T(4,128)(2,1)}, u32[]{:S(2)}, u32[]{:S(2)}) async-start(bf16[128,2,4,256]{3,2,1,0:T(4,128)(2,1)} %copy.153), calls=%async_computation.3 | async-start | bytes 1048576 | tf_op jit(solution)/shard_map/all_to_all | solution.py:151
  192.6 4.3 copy-start.5
  218.7 23.6 %all-to-all-start.1 = ((bf16[128,2,4,256]{3,2,1,0:T(4,128)(2,1)}), bf16[128,2,4,256]{3,2,1,0:T(4,128)(2,1)}, u32[]{:S(2)}, u32[]{:S(2)}) async-start(bf16[128,2,4,256]{3,2,1,0:T(4,128)(2,1)} %copy.136), calls=%async_computation.1 | async-start | bytes 1048576 | tf_op jit(solution)/shard_map/all_to_all | solution.py:151
  228.9 281.6 %all-reduce.4.cloned.1.call-start = ((), (), s32[]{:S(2)}) async-start(), calls=%async_computation.4 | async-start | bytes 6815744 | tf_op jit(solution)/shard_map/psum | solution.py:296
  229.0 3.1 copy-start.16
  230.3 2.6 copy-start.12
  232.9 2.7 copy-start.46
  310.3 15.5 %copy-start.17 = (bf16[16,64,256]{2,1,0:T(8,128)(2,1)S(1)}, bf16[16,64,256]{2,1,0:T(8,128)(2,1)}, u32[]{:S(2)}) copy-start(bf16[16,64,256]{2,1,0:T(8,128)(2,1)} %param.13) | copy-start | bytes 1572868
  310.3 15.5 %copy-start.19 = (bf16[2,8,4,16,256]{4,3,2,1,0:T(8,128)(2,1)S(1)}, bf16[2,8,4,16,256]{4,3,2,1,0:T(8,128)(2,1)}, u32[]{:S(2)}) copy-start(bf16[2,8,4,16,256]{4,3,2,1,0:T(8,128)(2,1)} %copy.138) | copy-start | bytes 1572868
  322.7 14.1 %copy-start.40 = (f32[1024]{0:T(1024)S(1)}, f32[1024]{0:T(1024)}, u32[]{:S(2)}) copy-start(f32[1024]{0:T(1024)} %copy-done.39) | copy-start | bytes 12292
  322.7 4.1 collective-permute-start.4
  324.4 5.7 %collective-permute-start.5 = (bf16[1,64,1024]{2,1,0:T(8,128)(2,1)S(1)}, bf16[1,64,1024]{2,1,0:T(8,128)(2,1)S(1)}, u32[]{:S(2)}, u32[]{:S(2)}) collective-permute-start(bf16[1,64,1024]{2,1,0:T(8,128)(2,1)S(1)} %get-tuple-element.75), channel_id=1, source_target_pairs={{16,0},{32,16},{48,32},{64,48},{80,64},{96,80},{112,96},{17,1},{33... | collective-permute-start | bytes 393224 | tf_op jit(solution)/shard_map/ppermute | solution.py:19
  330.3 9.4 %copy-start.24 = (f32[16,64,1024]{2,1,0:T(8,128)S(1)}, f32[16,64,1024]{2,1,0:T(8,128)}, u32[]{:S(2)}) copy-start(f32[16,64,1024]{2,1,0:T(8,128)} %get-tuple-element.88) | copy-start | bytes 12582916
  330.3 7.4 %collective-permute-start.6 = (bf16[18,1,1024]{2,1,0:T(2,128)(2,1)S(1)}, bf16[18,1,1024]{2,1,0:T(2,128)(2,1)S(1)}, u32[]{:S(2)}, u32[]{:S(2)}) collective-permute-start(bf16[18,1,1024]{2,1,0:T(2,128)(2,1)S(1)} %get-tuple-element.68), channel_id=1, source_target_pairs={{1,0},{2,1},{3,2},{4,3},{5,4},{6,5},{7,6},{8,7},{9,8},{10,9},{11,1... | collective-permute-start | bytes 110600 | tf_op jit(solution)/shard_map/ppermute | solution.py:19
  334.6 3.6 collective-permute-start.7
  339.7 9.2 %copy-start.13 = (bf16[16,64,256]{2,1,0:T(8,128)(2,1)S(1)}, bf16[16,64,256]{2,1,0:T(8,128)(2,1)}, u32[]{:S(2)}) copy-start(bf16[16,64,256]{2,1,0:T(8,128)(2,1)} %param.12) | copy-start | bytes 1572868
  339.7 9.2 %copy-start.43 = (f32[256]{0:T(256)S(1)}, f32[256]{0:T(256)}, u32[]{:S(2)}) copy-start(f32[256]{0:T(256)} %copy-done.42) | copy-start | bytes 3076
  348.9 2.9 copy-start.33
  349.0 2.9 copy-start.34
  349.0 2.9 copy-start.35
  349.0 2.9 copy-start.36
  349.0 2.9 copy-start.37
  349.0 2.9 copy-start.38
  349.0 3.0 copy-start.10
  349.0 3.0 copy-start.29
  351.9 6.5 %copy-start.44 = (f32[256]{0:T(256)S(1)}, f32[256]{0:T(256)}, u32[]{:S(2)}) copy-start(f32[256]{0:T(256)} %get-tuple-element.51) | copy-start | bytes 3076
  351.9 77.8 %copy-start.7 = (f32[2,8,4,16,256]{4,3,2,1,0:T(8,128)S(1)}, f32[2,8,4,16,256]{4,3,2,1,0:T(8,128)}, u32[]{:S(2)}) copy-start(f32[2,8,4,16,256]{4,3,2,1,0:T(8,128)} %copy-done.6) | copy-start | bytes 3145732
  351.9 77.8 %copy-start.18 = (bf16[16,64,256]{2,1,0:T(8,128)(2,1)S(1)}, bf16[16,64,256]{2,1,0:T(8,128)(2,1)}, u32[]{:S(2)}) copy-start(bf16[16,64,256]{2,1,0:T(8,128)(2,1)} %param.13) | copy-start | bytes 1572868
  510.5 6.4 %copy-start.27 = (f32[256,768]{1,0:T(8,128)S(1)}, f32[256,768]{1,0:T(8,128)}, u32[]{:S(2)}) copy-start(f32[256,768]{1,0:T(8,128)} %get-tuple-element.110) | copy-start | bytes 2359300
  510.5 7.3 %copy-start.30 = (f32[256,256]{1,0:T(8,128)S(1)}, f32[256,256]{1,0:T(8,128)}, u32[]{:S(2)}) copy-start(f32[256,256]{1,0:T(8,128)} %get-tuple-element.111) | copy-start | bytes 786436
  (13 other events, 19.4 us)
Sparse Core Ops, SparseCore 0:
  351.2 159.2 all-reduce.3
where the time goes:
time: 536 us; the launch traced here: 526 us
  blocking collectives  205 us (38%)
  waiting for transfers between devices  92 us (17%)
  starting transfers between devices  58.4 us (11%)
  local copies, waits for them, and re-layouts  57.7 us (11%)
  other arithmetic  52.7 us (10%)
  matrix products  45 us (8%)
  between operations  15.2 us (3%)
    psum x1, waiting for transfers between devices, on_device(): lax.psum((grad_norm0, grad_expand, grad_depth, grad_project, grad_norm1,...  77.8 us
    psum x1, blocking collectives, on_device(): lax.psum((grad_norm0, grad_expand, grad_depth, grad_project, grad_norm1,...  71.3 us
    psum x1, blocking collectives, on_device(): lax.psum(jnp.sum(activated, axis=(0, 1)), ('row', 'col')) / cells_total  69.6 us
    psum x1, blocking collectives, on_device(): lax.psum(jnp.sum(grad_gated * activated, axis=(0, 1)), ('row', 'col'))  63.8 us
    dot_general x8, matrix products, matmul_last(): product = jnp.dot(flat_rows, right_side, preferred_element_type=jnp.float32)  20.6 us
    all_to_all x2, starting transfers between devices, to_grid(): lax.all_to_all(flat_order_out(values), ('row', 'col'), split_axis=0, conc...  19.5 us
    all_to_all x2, starting transfers between devices, from_grid(): lax.all_to_all(flat_back_out(values), ('row', 'col'), split_axis=0, conca...  18.2 us
    unnamed x102, local copies, waits for them, and re-layouts  15.2 us
  transfers between devices with their start and end apart: 13, of which 7 were waited for; matrix products, arithmetic and copies ran while one was open for 15% of the time, Pallas kernels for 0%

commit v1 on v0

v1 whole, which is shorter than its diff:
```python
import functools

import jax
import jax.numpy as jnp
from jax import lax
from jax.experimental import pallas as pl
from jax.experimental.pallas import tpu as pltpu
from jax.sharding import PartitionSpec as P

F32 = jnp.float32
BF16 = jnp.bfloat16
MESH = pl.DeviceIdType.MESH
ROWS = 8
COLS = 16
CHIPS = 64
HEADS = 8
MEMBERS = 64
GROUPS = 16
CH = 256
ANY = pl.BlockSpec(memory_space=pl.ANY)
VMEM = pl.BlockSpec(memory_space=pltpu.VMEM)


def nn(a, b):
    return jnp.dot(a, b, preferred_element_type=F32)


def nt(a, b):
    return lax.dot_general(a, b, (((1,), (1,)), ((), ())), preferred_element_type=F32)


def tn(a, b):
    return lax.dot_general(a, b, (((0,), (0,)), ((), ())), preferred_element_type=F32)


def place():
    row = lax.axis_index("row")
    col = lax.axis_index("col")
    core = lax.rem(col, 2)
    chip = row * 8 + lax.div(col, 2)
    return row, col, core, chip


def chip_device(chip, core):
    return (lax.div(chip, 8), lax.rem(chip, 8) * 2 + core)


def each_chip(chip, body):
    def step(k, carry):
        body(k, lax.rem(chip + k, CHIPS))
        return carry

    lax.fori_loop(1, CHIPS, step, 0)


def tile_sum_kernel(x_ref, o_ref, col_slots, row_slots, send_a, recv_a, send_b, recv_b):
    row, col, _, _ = place()
    barrier = pltpu.get_barrier_semaphore()
    for k in range(1, COLS):
        pl.semaphore_signal(
            barrier, inc=1, device_id=(row, lax.rem(col + k, COLS)), device_id_type=MESH
        )
    for k in range(1, ROWS):
        pl.semaphore_signal(
            barrier, inc=1, device_id=(lax.rem(row + k, ROWS), col), device_id_type=MESH
        )
    col_slots[col] = x_ref[...]
    pl.semaphore_wait(barrier, COLS + ROWS - 2)
    copies = []
    for k in range(1, COLS):
        copy = pltpu.make_async_remote_copy(
            src_ref=x_ref,
            dst_ref=col_slots.at[col],
            send_sem=send_a.at[k],
            recv_sem=recv_a.at[k],
            device_id=(row, lax.rem(col + k, COLS)),
            device_id_type=MESH,
        )
        copy.start()
        copies.append(copy)
    for copy in copies:
        copy.wait()
    total = col_slots[0]
    for k in range(1, COLS):
        total = total + col_slots[k]
    row_slots[row] = total
    copies = []
    for k in range(1, ROWS):
        copy = pltpu.make_async_remote_copy(
            src_ref=row_slots.at[row],
            dst_ref=row_slots.at[row],
            send_sem=send_b.at[k],
            recv_sem=recv_b.at[k],
            device_id=(lax.rem(row + k, ROWS), col),
            device_id_type=MESH,
        )
        copy.start()
        copies.append(copy)
    for copy in copies:
        copy.wait()
    total = row_slots[0]
    for k in range(1, ROWS):
        total = total + row_slots[k]
    o_ref[...] = total


def tile_sum(x, collective_id):
    out = pl.pallas_call(
        tile_sum_kernel,
        out_shape=jax.ShapeDtypeStruct((8, 128), F32),
        in_specs=[VMEM],
        out_specs=VMEM,
        scratch_shapes=[
            pltpu.VMEM((COLS, 8, 128), F32),
            pltpu.VMEM((ROWS, 8, 128), F32),
            pltpu.SemaphoreType.DMA((COLS,)),
            pltpu.SemaphoreType.DMA((COLS,)),
            pltpu.SemaphoreType.DMA((ROWS,)),
            pltpu.SemaphoreType.DMA((ROWS,)),
        ],
        compiler_params=pltpu.CompilerParams(collective_id=collective_id, has_side_effects=True),
        name="tile_sum",
    )(x.reshape(8, 128))
    return out.reshape(1024)


def exchange_kernel(count, *refs):
    sources, outs = refs[:count], refs[count : 2 * count]
    send_sem, recv_sem, own_sem = refs[2 * count :]
    _, _, core, chip = place()
    barrier = pltpu.get_barrier_semaphore()

    def greet(k, peer):
        pl.semaphore_signal(
            barrier, inc=1, device_id=chip_device(peer, core), device_id_type=MESH
        )

    each_chip(chip, greet)
    own = []
    for n in range(count):
        copy = pltpu.make_async_copy(sources[n].at[chip], outs[n].at[chip], own_sem.at[n])
        copy.start()
        own.append(copy)
    pl.semaphore_wait(barrier, CHIPS - 1)

    def send(k, peer):
        for n in range(count):
            pltpu.make_async_remote_copy(
                src_ref=sources[n].at[peer],
                dst_ref=outs[n].at[chip],
                send_sem=send_sem.at[n],
                recv_sem=recv_sem.at[n],
                device_id=chip_device(peer, core),
                device_id_type=MESH,
            ).start()

    each_chip(chip, send)
    for n in range(count):
        own[n].wait()
        most = pl.ds(0, CHIPS - 1)
        pltpu.make_async_copy(sources[n].at[most], outs[n].at[most], send_sem.at[n]).wait()
        pltpu.make_async_copy(sources[n].at[most], outs[n].at[most], recv_sem.at[n]).wait()


def exchange(arrays, collective_id):
    count = len(arrays)
    shape = jax.ShapeDtypeStruct((CHIPS, GROUPS, CH), BF16)
    return pl.pallas_call(
        functools.partial(exchange_kernel, count),
        out_shape=[shape] * count,
        in_specs=[ANY] * count,
        out_specs=[ANY] * count,
        scratch_shapes=[
            pltpu.SemaphoreType.DMA((count,)),
            pltpu.SemaphoreType.DMA((count,)),
            pltpu.SemaphoreType.DMA((count,)),
        ],
        compiler_params=pltpu.CompilerParams(collective_id=collective_id, has_side_effects=True),
        name="exchange",
    )(*[a.reshape(CHIPS, GROUPS, CH) for a in arrays])


def chunk_of(ref, core, chip):
    height, width = ref.shape
    across = width // 128
    first = core * (height // 2) + lax.div(chip, across) * 16
    return ref.at[
        pl.ds(pl.multiple_of(first, 16), 16),
        pl.ds(pl.multiple_of(lax.rem(chip, across) * 128, 128), 128),
    ]


def half_of(ref, core):
    half = ref.shape[0] // 2
    return ref.at[pl.ds(pl.multiple_of(core * half, half), half)]


def weight_sum_kernel(count, *refs):
    xs = refs[:count]
    small_x = refs[count]
    outs = refs[count + 1 : 2 * count + 1]
    small_o = refs[2 * count + 1]
    rest = refs[2 * count + 2 :]
    pair_in = rest[:count]
    small_pair = rest[count]
    summed = rest[count + 1 : 2 * count + 1]
    small_summed = rest[2 * count + 1]
    slots = rest[2 * count + 2 : 3 * count + 2]
    small_slots = rest[3 * count + 2]
    pair_send, pair_recv, send_sem, recv_sem, back_send, back_recv, last_send, last_recv = rest[
        3 * count + 3 :
    ]
    _, _, core, chip = place()
    other = 1 - core
    partner = chip_device(chip, other)
    barrier = pltpu.get_barrier_semaphore()

    def greet(k, peer):
        pl.semaphore_signal(
            barrier, inc=1, device_id=chip_device(peer, core), device_id_type=MESH
        )

    pl.semaphore_signal(barrier, inc=1, device_id=partner, device_id_type=MESH)
    each_chip(chip, greet)
    pl.semaphore_wait(barrier, CHIPS)

    copies = []
    for n in range(count + 1):
        src = half_of(xs[n], other) if n < count else small_x.at[other]
        dst = pair_in[n] if n < count else small_pair
        copy = pltpu.make_async_remote_copy(
            src_ref=src,
            dst_ref=dst,
            send_sem=pair_send.at[n],
            recv_sem=pair_recv.at[n],
            device_id=partner,
            device_id_type=MESH,
        )
        copy.start()
        copies.append(copy)
    for copy in copies:
        copy.wait()
    for n in range(count):
        mine = half_of(xs[n], core)
        summed[n][...] = (mine[...].astype(F32) + pair_in[n][...].astype(F32)).astype(BF16)
    small_summed[...] = small_x[core] + small_pair[...]

    def scatter(k, peer):
        for n in range(count + 1):
            if n < count:
                src, dst = chunk_of(summed[n], 0, peer), slots[n].at[chip]
            else:
                src, dst = small_summed.at[peer], small_slots.at[chip]
            pltpu.make_async_remote_copy(
                src_ref=src,
                dst_ref=dst,
                send_sem=send_sem.at[n],
                recv_sem=recv_sem.at[n],
                device_id=chip_device(peer, core),
                device_id_type=MESH,
            ).start()

    each_chip(chip, scatter)
    most = pl.ds(0, CHIPS - 1)
    for n in range(count):
        slots[n][chip] = chunk_of(summed[n], 0, chip)[...]
    small_slots[chip] = small_summed[chip]
    for n in range(count + 1):
        buf = slots[n] if n < count else small_slots
        pltpu.make_async_copy(buf.at[most], buf.at[most], recv_sem.at[n]).wait()

    for n in range(count):
        total = jnp.sum(slots[n][...].astype(F32), axis=0)
        chunk_of(outs[n], core, chip)[...] = total.astype(BF16)
    small_o[core, chip] = jnp.sum(small_slots[...], axis=0)

    def gather(k, peer):
        for n in range(count + 1):
            piece = chunk_of(outs[n], core, chip) if n < count else small_o.at[core, chip]
            pltpu.make_async_remote_copy(
                src_ref=piece,
                dst_ref=piece,
                send_sem=back_send.at[n],
                recv_sem=back_recv.at[n],
                device_id=chip_device(peer, core),
                device_id_type=MESH,
            ).start()

    each_chip(chip, gather)
    for n in range(count + 1):
        buf = slots[n] if n < count else small_slots
        pltpu.make_async_copy(buf.at[most], buf.at[most], send_sem.at[n]).wait()
        pltpu.make_async_copy(buf.at[most], buf.at[most], back_recv.at[n]).wait()
    copies = []
    for n in range(count + 1):
        piece = half_of(outs[n], core) if n < count else small_o.at[core]
        copy = pltpu.make_async_remote_copy(
            src_ref=piece,
            dst_ref=piece,
            send_sem=last_send.at[n],
            recv_sem=last_recv.at[n],
            device_id=partner,
            device_id_type=MESH,
        )
        copy.start()
        copies.append(copy)
    for n in range(count + 1):
        buf = slots[n] if n < count else small_slots
        pltpu.make_async_copy(buf.at[most], buf.at[most], back_send.at[n]).wait()
    for copy in copies:
        copy.wait()


def weight_sum(arrays, small, collective_id):
    count = len(arrays)
    width = small.shape[-1]
    sems = [pltpu.SemaphoreType.DMA((count + 1,))] * 8
    halves = [pltpu.VMEM((a.shape[0] // 2, a.shape[1]), BF16) for a in arrays]
    half_small = pltpu.VMEM((CHIPS, 1, width), F32)
    return pl.pallas_call(
        functools.partial(weight_sum_kernel, count),
        out_shape=[jax.ShapeDtypeStruct(a.shape, BF16) for a in arrays]
        + [jax.ShapeDtypeStruct((2, CHIPS, 1, width), F32)],
        in_specs=[VMEM] * (count + 1),
        out_specs=[VMEM] * (count + 1),
        scratch_shapes=halves
        + [half_small]
        + halves
        + [half_small]
        + [pltpu.VMEM((CHIPS, 16, 128), BF16)] * count
        + [half_small]
        + sems,
        compiler_params=pltpu.CompilerParams(
            collective_id=collective_id, has_side_effects=True, vmem_limit_bytes=40 * 2**20
        ),
        name="weight_sum",
    )(*arrays, small)


def attention_kernel(
    x_ref, dy_ref, w_qkv, w_out, bias_ref, att_ref, gn_ref, gw_ref, gb_ref, qkv_s, g_s, att_s, gp_s
):
    rows = MEMBERS * GROUPS
    tile = 256
    scale = 32 ** (-0.5)

    @pl.loop(0, rows // tile)
    def _(t):
        members = tile // GROUPS
        at = pl.ds(pl.multiple_of(t * tile, tile), tile)
        x = x_ref[pl.ds(t * members, members)].reshape(tile, CH)
        dy = dy_ref[pl.ds(t * members, members)].reshape(tile, CH)
        qkv = nn(x, w_qkv[...])
        for n in range(6):
            qkv_s[n, at, :] = qkv[:, n * 128 : (n + 1) * 128]
        g = nt(dy, w_out[...])
        for n in range(2):
            g_s[n, at, :] = g[:, n * 128 : (n + 1) * 128]

    gb_ref[...] = jnp.zeros_like(gb_ref)
    head_of = lax.div(lax.broadcasted_iota(jnp.int32, (1, CH), 1), 32)
    masks_f = [(head_of == h).astype(F32) for h in range(HEADS)]
    masks = [m.astype(BF16) for m in masks_f]

    def spread_heads(a):
        return jnp.concatenate([a * m for m in masks], axis=0)

    def own_heads(r):
        total = r[0:MEMBERS] * masks_f[0]
        for h in range(1, HEADS):
            total = total + r[h * MEMBERS : (h + 1) * MEMBERS] * masks_f[h]
        return total

    @pl.loop(0, GROUPS)
    def _(group):
        at = pl.ds(group, MEMBERS, stride=GROUPS)

        def take(ref, first):
            return jnp.concatenate([ref[first, at, :], ref[first + 1, at, :]], axis=1).astype(BF16)

        def put(ref, first, value):
            value = value.astype(BF16).astype(F32)
            ref[first, at, :] = value[:, :128]
            ref[first + 1, at, :] = value[:, 128:]

        q, k, v, g = take(qkv_s, 0), take(qkv_s, 2), take(qkv_s, 4), take(g_s, 0)
        q_heads, g_heads = spread_heads(q), spread_heads(g)
        scores = nt(k, q_heads) * scale + bias_ref[...]
        lifted = jnp.exp(scores - jnp.max(scores, axis=0, keepdims=True))
        probs = lifted / jnp.sum(lifted, axis=0, keepdims=True)
        low = probs.astype(BF16)
        put(att_s, 0, own_heads(tn(low, v)))
        put(gp_s, 4, nn(low, g_heads))
        grad_probs = nt(v, g_heads)
        grad_scores = probs * (grad_probs - jnp.sum(grad_probs * probs, axis=0, keepdims=True))
        gb_ref[...] += grad_scores
        scaled = (grad_scores * scale).astype(BF16)
        put(gp_s, 0, own_heads(tn(scaled, k)))
        put(gp_s, 2, nn(scaled, q_heads))

    gw_ref[...] = jnp.zeros_like(gw_ref)

    @pl.loop(0, rows // tile)
    def _(t):
        members = tile // GROUPS
        at = pl.ds(pl.multiple_of(t * tile, tile), tile)
        x = x_ref[pl.ds(t * members, members)].reshape(tile, CH)
        dy = dy_ref[pl.ds(t * members, members)].reshape(tile, CH)
        att = jnp.concatenate([att_s[n, at, :] for n in range(2)], axis=1).astype(BF16)
        gp = jnp.concatenate([gp_s[n, at, :] for n in range(6)], axis=1).astype(BF16)
        att_ref[pl.ds(t * members, members)] = att.reshape(members, GROUPS, CH)
        gn = nt(gp, w_qkv[...]).astype(BF16)
        gn_ref[pl.ds(t * members, members)] = gn.reshape(members, GROUPS, CH)
        gw_ref[:, : 3 * CH] += tn(x, gp)
        gw_ref[:, 3 * CH :] += tn(att, dy)


def attention(x, dy, w_qkv, w_out, bias_rows):
    rows = MEMBERS * GROUPS
    grid_shape = jax.ShapeDtypeStruct((MEMBERS, GROUPS, CH), BF16)
    return pl.pallas_call(
        attention_kernel,
        out_shape=[
            grid_shape,
            grid_shape,
            jax.ShapeDtypeStruct((CH, 4 * CH), F32),
            jax.ShapeDtypeStruct((MEMBERS, HEADS * MEMBERS), F32),
        ],
        in_specs=[VMEM] * 5,
        out_specs=[VMEM] * 4,
        scratch_shapes=[
            pltpu.VMEM((6, rows, 128), F32),
            pltpu.VMEM((2, rows, 128), F32),
            pltpu.VMEM((2, rows, 128), F32),
            pltpu.VMEM((6, rows, 128), F32),
        ],
        compiler_params=pltpu.CompilerParams(vmem_limit_bytes=40 * 2**20),
        name="attention",
    )(x, dy, w_qkv, w_out, bias_rows)


def with_halo(cells, sides, width):
    for axis, dim in sides:
        count = lax.axis_size(axis)
        ends = count - 1
        head = lax.slice_in_dim(cells, 0, width, axis=dim)
        tail = lax.slice_in_dim(cells, cells.shape[dim] - width, cells.shape[dim], axis=dim)
        cells = jnp.concatenate(
            [
                lax.ppermute(tail, axis, [(i, (i + 1) % count) for i in range(ends)]),
                cells,
                lax.ppermute(head, axis, [((i + 1) % count, i) for i in range(ends)]),
            ],
            axis=dim,
        )
    return cells


def norm_tokens(values, scale_gain):
    average = jnp.mean(values, axis=-1, keepdims=True)
    centered = values - average
    variance = jnp.mean(centered * centered, axis=-1, keepdims=True)
    return centered * lax.rsqrt(variance + 1e-05) * scale_gain


def matmul_last(left_side, right_side):
    flat_rows = left_side.reshape(-1, left_side.shape[-1])
    product = jnp.dot(flat_rows, right_side, preferred_element_type=F32)
    return product.reshape(left_side.shape[:-1] + (right_side.shape[-1],))


def smooth_gelu(values):
    return jax.nn.gelu(values, approximate=True)


def depthwise(padded, kernel, row_count, col_count):
    accumulated = jnp.zeros((row_count, col_count, padded.shape[-1]), F32)
    for shift_row in range(3):
        for shift_col in range(3):
            window = padded[
                shift_row : shift_row + row_count, shift_col : shift_col + col_count
            ].astype(F32)
            accumulated = accumulated + window * kernel[shift_row, shift_col].astype(F32)
    return accumulated


def depthwise_back(padded_grad, kernel, row_count, col_count):
    accumulated = jnp.zeros((row_count, col_count, padded_grad.shape[-1]), F32)
    for shift_row in range(3):
        for shift_col in range(3):
            window = padded_grad[
                2 - shift_row : 2 - shift_row + row_count, 2 - shift_col : 2 - shift_col + col_count
            ].astype(F32)
            accumulated = accumulated + window * kernel[shift_row, shift_col].astype(F32)
    return accumulated


def kernel_grad(padded, grad_pre, row_count, col_count):
    kernel_terms = []
    for shift_row in range(3):
        for shift_col in range(3):
            window = padded[
                shift_row : shift_row + row_count, shift_col : shift_col + col_count
            ].astype(F32)
            kernel_terms.append(jnp.sum(window * grad_pre.astype(F32), axis=(0, 1)))
    return jnp.stack(kernel_terms).reshape(3, 3, padded.shape[-1])


def excite_gate(pooled, squeeze_wide, excite_wide):
    hidden = jax.nn.silu(jnp.dot(pooled[None, :], squeeze_wide, precision=lax.Precision.HIGHEST))
    return jax.nn.sigmoid(jnp.dot(hidden, excite_wide, precision=lax.Precision.HIGHEST))[0]


def on_device(
    image,
    out_cotangent,
    norm0_gain,
    w_expand,
    w_depth,
    w_squeeze,
    w_excite,
    w_project,
    norm1_gain,
    w_qkv,
    w_out,
    attn_bias,
):
    row_count, col_count, channels = image.shape
    map_shape = image.shape
    cells_total = row_count * lax.axis_size("row") * col_count * lax.axis_size("col")
    (grid_cot,) = exchange([out_cotangent], 0)
    image_float = image.astype(F32)
    gain_first = norm0_gain.astype(F32)
    gain_second = norm1_gain.astype(F32)
    normed_first = norm_tokens(image_float, gain_first).astype(BF16)
    expanded = matmul_last(normed_first, w_expand)
    spread = smooth_gelu(expanded).astype(BF16)
    padded = with_halo(spread, (("row", 0), ("col", 1)), 1)
    depth_pre = depthwise(padded, w_depth, row_count, col_count)
    activated = smooth_gelu(depth_pre)
    pooled = tile_sum(jnp.sum(activated, axis=(0, 1)), 1) / cells_total
    squeeze_wide = w_squeeze.astype(F32)
    excite_wide = w_excite.astype(F32)
    channel_gate = excite_gate(pooled, squeeze_wide, excite_wide)
    gated_act = (activated * channel_gate).astype(BF16)
    mixed_map = (image_float + matmul_last(gated_act, w_project)).astype(BF16)
    mixed_float = mixed_map.astype(F32)
    normed_second = norm_tokens(mixed_float, gain_second).astype(BF16)
    (grid_normed,) = exchange([normed_second], 2)
    bias_rows = attn_bias.transpose(2, 0, 1).reshape(MEMBERS, HEADS * MEMBERS)
    grid_att, grid_grad, grad_pair, bias_grad = attention(
        grid_normed, grid_cot, w_qkv, w_out, bias_rows
    )
    attended_map, grad_normed = exchange([grid_att, grid_grad], 3)
    attended_map = attended_map.reshape(map_shape)
    grad_normed = grad_normed.reshape(map_shape)
    block_out = (mixed_float + matmul_last(attended_map, w_out)).astype(BF16)
    unused_second, norm_second_vjp = jax.vjp(norm_tokens, mixed_float, gain_second)
    grad_mixed_norm, grad_norm1 = norm_second_vjp(grad_normed.astype(F32))
    grad_mixed = out_cotangent.astype(F32) + grad_mixed_norm
    grad_mixed_b = grad_mixed.astype(BF16)
    grad_project = jnp.dot(
        gated_act.reshape(-1, gated_act.shape[-1]).T,
        grad_mixed_b.reshape(-1, channels),
        preferred_element_type=F32,
    )
    grad_gated = matmul_last(grad_mixed_b, w_project.T)
    grad_gate = tile_sum(jnp.sum(grad_gated * activated, axis=(0, 1)), 4)
    unused_gate, gate_vjp = jax.vjp(excite_gate, pooled, squeeze_wide, excite_wide)
    grad_pooled, grad_squeeze, grad_excite = gate_vjp(grad_gate)
    grad_activated = grad_gated * channel_gate + grad_pooled / cells_total
    unused_act, gelu_depth_vjp = jax.vjp(smooth_gelu, depth_pre)
    grad_depth_pre = gelu_depth_vjp(grad_activated)[0].astype(BF16)
    grad_pad = with_halo(grad_depth_pre, (("row", 0), ("col", 1)), 1)
    grad_spread = depthwise_back(grad_pad, w_depth, row_count, col_count)
    grad_depth = kernel_grad(padded, grad_depth_pre, row_count, col_count)
    unused_spread, gelu_expand_vjp = jax.vjp(smooth_gelu, expanded)
    grad_expanded = gelu_expand_vjp(grad_spread)[0].astype(BF16)
    grad_expand = jnp.dot(
        normed_first.reshape(-1, channels).T,
        grad_expanded.reshape(-1, grad_expanded.shape[-1]),
        preferred_element_type=F32,
    )
    grad_first = matmul_last(grad_expanded, w_expand.T)
    unused_first, norm_first_vjp = jax.vjp(norm_tokens, image_float, gain_first)
    grad_image_norm, grad_norm0 = norm_first_vjp(grad_first)
    grad_image = (grad_mixed + grad_image_norm).astype(BF16)

    small = jnp.concatenate(
        [grad_norm0, grad_norm1, grad_depth.reshape(-1), bias_grad.reshape(-1)]
    )
    small = jnp.pad(small, (0, 2 * CHIPS * 384 - small.shape[0])).reshape(2, CHIPS, 1, 384)
    sum_expand, sum_project, sum_pair, sum_small = weight_sum(
        [grad_expand.astype(BF16), grad_project.astype(BF16), grad_pair.astype(BF16)], small, 5
    )
    sum_small = sum_small.reshape(-1)
    depth_end = 2 * channels + w_depth.size
    sum_bias = sum_small[depth_end : depth_end + attn_bias.size]
    return (
        block_out,
        grad_image,
        sum_small[:channels],
        sum_expand.astype(F32),
        sum_small[2 * channels : depth_end].reshape(w_depth.shape),
        grad_squeeze,
        grad_excite,
        sum_project.astype(F32),
        sum_small[channels : 2 * channels],
        sum_pair[:, : 3 * channels].astype(F32),
        sum_pair[:, 3 * channels :].astype(F32),
        sum_bias.reshape(MEMBERS, HEADS, MEMBERS).transpose(1, 2, 0),
    )


def solution(mesh):
    mapped = P("row", "col", None)
    return jax.shard_map(
        on_device,
        mesh=mesh,
        in_specs=(mapped, mapped) + (P(),) * 10,
        out_specs=(mapped, mapped) + (P(),) * 10,
        check_vma=False,
    )
```

time: 536 us -> 267 us (0.50); the launches traced: 526 us -> 266 us
  blocking collectives: 205 us -> 0 us
  Pallas kernels: 0 us -> 142 us
  waiting for transfers between devices: 92 us -> 8.03 us
  local copies, waits for them, and re-layouts: 57.7 us -> 10.8 us
  starting transfers between devices: 58.4 us -> 23.9 us
  matrix products: 45 us -> 19.6 us
  between operations: 15.2 us -> 1.88 us
  other arithmetic: 52.7 us -> 59.9 us
    psum x3 -> x0, blocking collectives: 205 us -> none  [the longest x1 71.3 us: on_device(): lax.psum((grad_norm0, grad_expand, grad_depth, grad_project, grad_norm1,...]
    pallas_call x0 -> x7, Pallas kernels: none -> 142 us  [the longest x3 47 us: exchange(): pl.pallas_call(functools.partial(exchange_kernel, count), out_shape=[shap...]
    psum x1 -> x0, waiting for transfers between devices: 77.8 us -> none  [on_device(): lax.psum((grad_norm0, grad_expand, grad_depth, grad_project, grad_norm1,...]
    all_to_all x4 -> x0, starting transfers between devices: 37.7 us -> none  [the longest x2 19.5 us: to_grid(): lax.all_to_all(flat_order_out(values), ('row', 'col'), split_axis=0, conc...]
    dot_general x16 -> x5, matrix products: 35.3 us -> 14.6 us  [matmul_last(): product = jnp.dot(flat_rows, right_side, preferred_element_type=F32)]
    another operation x6 -> x1, local copies, waits for them, and re-layouts: 20.4 us -> 0.02 us  [on_device(): grad_depth.reshape(-1)]
    unnamed x102 -> x152, local copies, waits for them, and re-layouts: 15.2 us -> 5.16 us
    sub x2 -> x0, other arithmetic: 7.25 us -> none  [the longest x1 5.81 us: attention_back(): grad_probs - jnp.sum(grad_probs * softmaxed, axis=-1, keepdims=True)]
  transfers between devices with their start and end apart: 13 -> 8, of which waited for: 7 -> 3; matrix products, arithmetic and copies ran while one was open for 15% -> 1% of each run, Pallas kernels for 0% -> 6%
where the time goes in v1:
time: 267 us; the launch traced here: 266 us
  Pallas kernels  142 us (53%)
  other arithmetic  59.9 us (22%)
  starting transfers between devices  23.9 us (9%)
  matrix products  19.6 us (7%)
  local copies, waits for them, and re-layouts  10.8 us (4%)
  waiting for transfers between devices  8.03 us (3%)
    pallas_call x3, Pallas kernels, exchange(): pl.pallas_call(functools.partial(exchange_kernel, count), out_shape=[shap...  47 us
    pallas_call x1, Pallas kernels, weight_sum(): pl.pallas_call(functools.partial(weight_sum_kernel, count), out_shape=[ja...  44.3 us
    pallas_call x2, Pallas kernels, tile_sum(): pl.pallas_call(tile_sum_kernel, out_shape=jax.ShapeDtypeStruct((8, 128),...  32.2 us
    pallas_call x1, Pallas kernels, attention(): pl.pallas_call(attention_kernel, out_shape=[grid_shape, grid_shape, jax.S...  18 us
    ppermute x4, starting transfers between devices, with_halo(): lax.ppermute(tail, axis, [(i, (i + 1) % count) for i in range(ends)])  14.6 us
    dot_general x5, matrix products, matmul_last(): product = jnp.dot(flat_rows, right_side, preferred_element_type=F32)  14.6 us
    reduce_sum x1, other arithmetic, kernel_grad(): kernel_terms.append(jnp.sum(window * grad_pre.astype(F32), axis=(0, 1)))  13.3 us
    ppermute x4, starting transfers between devices, with_halo(): lax.ppermute(head, axis, [((i + 1) % count, i) for i in range(ends)])  9.27 us
  transfers between devices with their start and end apart: 8, of which 3 were waited for; matrix products, arithmetic and copies ran while one was open for 1% of the time, Pallas kernels for 6%

profile of v1, /device:TPU:1, one launch (start us, length us, event | category | flops | bytes accessed | tf_op | source)
XLA Modules:
  0.0 265.7 jit_solution(2301292825243007769)
XLA Ops:
  1.4 1.3 convert_reduce_fusion.1
  2.6 1.4 fusion.56
  4.2 4.6 %multiply_convert_fusion.1 = (bf16[16,64,1024]{2,1,0:T(8,128)(2,1)S(1)}, f32[16,64,1024]{2,1,0:T(8,128)}) fusion(bf16[256,1024]{1,0:T(8,128)(2,1)S(1)} %copy-done, bf16[16,64,256]{2,1,0:T(8,128)(2,1)} %param.12, f32[256]{0:T(256)S(1)} %convert_element_type.176, f32[16,64]{1,0:T(8,128)S(1)} %fusion.73, f32[16,64]{1,0:T(8,128)S(1)} %broadcast_multiply_fusion.3), kind=kOutput, calls=%fused_computation.61 | convolution fusion | flops 547618816 | bytes 7349248 | tf_op jit(solution)/shard_map/dot_general | solution.py:468
  8.8 4.4 %collective-permute-start = (bf16[1,64,1024]{2,1,0:T(8,128)(2,1)S(1)}, bf16[1,64,1024]{2,1,0:T(8,128)(2,1)S(1)}, u32[]{:S(2)}, u32[]{:S(2)}) collective-permute-start(bf16[1,64,1024]{2,1,0:T(8,128)(2,1)S(1)} %get-tuple-element.76), channel_id=1, source_target_pairs={{0,16},{16,32},{32,48},{48,64},{64,80},{80,96},{96,112},{1,17},{17... | collective-permute-start | bytes 393224 | tf_op jit(solution)/shard_map/ppermute | solution.py:450
  13.2 1.3 collective-permute-start.1
  14.5 0.8 collective-permute-done
  15.3 3.6 %collective-permute-done.1 = bf16[1,64,1024]{2,1,0:T(8,128)(2,1)S(1)} collective-permute-done((bf16[1,64,1024]{2,1,0:T(8,128)(2,1)S(1)}, bf16[1,64,1024]{2,1,0:T(8,128)(2,1)S(1)}, u32[]{:S(2)}, u32[]{:S(2)}) %collective-permute-start.1) | collective-permute-done | bytes 131104 | tf_op jit(solution)/shard_map/ppermute | solution.py:452
  19.0 5.1 %collective-permute-start.2 = (bf16[18,1,1024]{2,1,0:T(2,128)(2,1)S(1)}, bf16[18,1,1024]{2,1,0:T(2,128)(2,1)S(1)}, u32[]{:S(2)}, u32[]{:S(2)}) collective-permute-start(bf16[18,1,1024]{2,1,0:T(2,128)(2,1)S(1)} %get-tuple-element.72), channel_id=1, source_target_pairs={{0,1},{1,2},{2,3},{3,4},{4,5},{5,6},{6,7},{7,8},{8,9},{9,10},{10,1... | collective-permute-start | bytes 110600 | tf_op jit(solution)/shard_map/ppermute | solution.py:450
  24.1 2.1 collective-permute-start.3
  27.1 16.3 %exchange.4.dy_ref = bf16[64,16,256]{2,1,0:T(8,128)(2,1)} custom-call(bf16[64,16,256]{2,1,0:T(8,128)(2,1)} %bitcast.115), custom_call_target="tpu_custom_call" | custom-call | tf_op jit(solution)/shard_map/exchange/pallas_call | solution.py:168
  43.4 2.3 maximum_maximum_fusion
  45.8 8.1 %fusion.85 = (f32[1024]{0:T(1024)}, f32[16,64,1024]{2,1,0:T(8,128)}) fusion(f32[1024]{0:T(1024)S(1)} %bitcast.134, bf16[18,65,1024]{2,1,0:T(8,128)(2,1)S(1)} %get-tuple-element.71, f32[1024]{0:T(1024)S(1)} %bitcast.136, bf16[1,64,1024]{2,1,0:T(8,128)(2,1)S(1)} %collective-permute-done.1, bf16[16,64,1024]{2,1,0:T(8,128)(2,1)S(1)} %get-tuple-element.91, ...), kind=kLoop, calls=%fused_computation.171 | loop fusion | flops 38796288 | bytes 19177472 | tf_op jit(solution)/shard_map/reduce_sum | solution.py:541
  54.0 16.1 %tile_sum.2 = f32[8,128]{1,0:T(8,128)} custom-call(f32[8,128]{1,0:T(8,128)} %bitcast.150), custom_call_target="tpu_custom_call" | custom-call | tf_op jit(solution)/shard_map/tile_sum/pallas_call | solution.py:108
  70.1 1.3 fusion.82
  72.7 4.3 %convert_reduce_fusion = (f32[16,64]{1,0:T(8,128)S(1)}, bf16[16,64,256]{2,1,0:T(8,128)(2,1)S(1)}) fusion(bf16[1024,256]{1,0:T(8,128)(2,1)} %param.19, f32[1024]{0:T(1024)S(1)} %add_divide_fusion, f32[16,64,1024]{2,1,0:T(8,128)} %get-tuple-element.65, bf16[16,64,256]{2,1,0:T(8,128)(2,1)} %param.12), kind=kOutput, calls=%fused_computation.75 | convolution fusion | flops 548666368 | bytes 5775360 | tf_op jit(solution)/shard_map/dot_general | solution.py:468
  77.4 1.1 fusion.52
  78.6 12.8 %exchange.3.x_ref = bf16[64,16,256]{2,1,0:T(8,128)(2,1)} custom-call(bf16[64,16,256]{2,1,0:T(8,128)(2,1)} %bitcast.116), custom_call_target="tpu_custom_call" | custom-call | tf_op jit(solution)/shard_map/exchange/pallas_call | solution.py:168
  91.4 1.0 copy-done.2
  92.5 18.0 %attention.1 = (bf16[64,16,256]{2,1,0:T(8,128)(2,1)S(1)}, bf16[64,16,256]{2,1,0:T(8,128)(2,1)S(1)}, f32[256,1024]{1,0:T(8,128)S(1)}, f32[64,512]{1,0:T(8,128)S(1)}) custom-call(bf16[64,16,256]{2,1,0:T(8,128)(2,1)S(1)} %copy-done.2, bf16[64,16,256]{2,1,0:T(8,128)(2,1)S(1)} %copy-done.1, bf16[256,768]{1,0:T(8,128)(2,1)S(1)} %copy-done.6, ...), custom_call_target="tpu_custom_call" | custom-call | tf_op jit(solution)/shard_map/attention/pallas_call | solution.py:421
  111.3 0.8 copy-done.4
  112.1 17.8 %exchange.5 = (bf16[64,16,256]{2,1,0:T(8,128)(2,1)}, bf16[64,16,256]{2,1,0:T(8,128)(2,1)}) custom-call(bf16[64,16,256]{2,1,0:T(8,128)(2,1)} %copy-done.3, bf16[64,16,256]{2,1,0:T(8,128)(2,1)} %copy-done.4), custom_call_target="tpu_custom_call" | custom-call | tf_op jit(solution)/shard_map/exchange/pallas_call | solution.py:168
  129.9 1.6 fusion.59
  132.2 2.3 fusion.55
  134.5 1.8 fusion.71
  136.3 2.7 %fusion.47.refs_1_ = bf16[1024,256]{1,0:T(8,128)(2,1)S(1)} fusion(bf16[16,64,256]{2,1,0:T(8,128)(2,1)S(1)} %fusion.71, f32[1024]{0:T(1024)} %copy-done.64, f32[16,64,1024]{2,1,0:T(8,128)S(1)} %copy-done.12), kind=kOutput, calls=%fused_computation.94 | convolution fusion | flops 547618816 | bytes 5246976 | tf_op jit(solution)/shard_map/dot_general | solution.py:562
  139.1 3.8 %multiply_reduce_fusion = (f32[1024]{0:T(1024)}, f32[16,64,1024]{2,1,0:T(8,128)}) fusion(f32[16,64,1024]{2,1,0:T(8,128)S(1)} %copy-done.12, bf16[16,64,256]{2,1,0:T(8,128)(2,1)S(1)} %fusion.71, bf16[1024,256]{1,0:T(8,128)(2,1)S(1)} %copy-done.73), kind=kOutput, calls=%fused_computation.59 | convolution fusion | flops 547355648 | bytes 9441280 | tf_op jit(solution)/shard_map/dot_general | solution.py:468
  142.9 1.1 fusion.45
  144.0 16.2 %tile_sum.3 = f32[8,128]{1,0:T(8,128)} custom-call(f32[8,128]{1,0:T(8,128)} %bitcast.153), custom_call_target="tpu_custom_call" | custom-call | tf_op jit(solution)/shard_map/tile_sum/pallas_call | solution.py:108
  161.3 13.3 %fusion.35 = (f32[1024]{0:T(1024)}, f32[1024]{0:T(1024)}, f32[1024]{0:T(1024)}, f32[1024]{0:T(1024)}, f32[1024]{0:T(1024)}, /*index=5*/f32[1024]{0:T(1024)}, f32...) fusion(bf16[18,65,1024]{2,1,0:T(8,128)(2,1)} %copy-done.8, ...), kind=kLoop, calls=%fused_computation.58 | loop fusion | flops 54516736 | bytes 25473024 | tf_op jit(solution)/shard_map/reduce_sum | solution.py:505
  174.6 2.8 %collective-permute-start.4 = (bf16[1,64,1024]{2,1,0:T(8,128)(2,1)S(1)}, bf16[1,64,1024]{2,1,0:T(8,128)(2,1)S(1)}, u32[]{:S(2)}, u32[]{:S(2)}) collective-permute-start(bf16[1,64,1024]{2,1,0:T(8,128)(2,1)S(1)} %get-tuple-element.74), channel_id=1, source_target_pairs={{0,16},{16,32},{32,48},{48,64},{64,80},{80,96},{96,112},{1,17},{17... | collective-permute-start | bytes 393224 | tf_op jit(solution)/shard_map/ppermute | solution.py:450
  177.4 1.3 collective-permute-start.5
  179.5 3.6 %collective-permute-done.5 = bf16[1,64,1024]{2,1,0:T(8,128)(2,1)S(1)} collective-permute-done((bf16[1,64,1024]{2,1,0:T(8,128)(2,1)S(1)}, bf16[1,64,1024]{2,1,0:T(8,128)(2,1)S(1)}, u32[]{:S(2)}, u32[]{:S(2)}) %collective-permute-start.5) | collective-permute-done | bytes 131104 | tf_op jit(solution)/shard_map/ppermute | solution.py:452
  183.9 4.6 %collective-permute-start.6 = (bf16[18,1,1024]{2,1,0:T(2,128)(2,1)}, bf16[18,1,1024]{2,1,0:T(2,128)(2,1)}, u32[]{:S(2)}, u32[]{:S(2)}) collective-permute-start(bf16[18,1,1024]{2,1,0:T(2,128)(2,1)} %get-tuple-element.68), channel_id=1, source_target_pairs={{1,0},{2,1},{3,2},{4,3},{5,4},{6,5},{7,6},{8,7},{9,8},{10,9},{11,1... | collective-permute-start | bytes 110600 | tf_op jit(solution)/shard_map/ppermute | solution.py:452
  188.5 2.4 collective-permute-start.7
  191.9 1.5 stack.39
  193.5 3.3 %pad_maximum_fusion.1 = (bf16[18,65,1024]{2,1,0:T(8,128)(2,1)S(1)}, bf16[18,65,1024]{2,1,0:T(8,128)(2,1)S(1)}) fusion(bf16[18,1,1024]{2,1,0:T(2,128)(2,1)} %collective-permute-done.6, bf16[1,64,1024]{2,1,0:T(8,128)(2,1)S(1)} %collective-permute-done.5, bf16[16,64,1024]{2,1,0:T(8,128)(2,1)} %copy-done.10, bf16[1,64,1024]{2,1,0:T(8,128)(2,1)S(1)} %collective-permute-done.4, ...), kind=kLoop, calls=%fused_computation.65 | loop fusion | flops 19169280 | bytes 7225344 | tf_op jit(solution)/shard_map/concatenate | solution.py:448
  197.6 7.8 %fusion.14 = bf16[16,64,1024]{2,1,0:T(8,128)(2,1)S(1)} fusion(f32[16,64,1024]{2,1,0:T(8,128)S(1)} %copy-done.17, bf16[16,64,1024]{2,1,0:T(8,128)(2,1)S(1)} %copy-done.11, bf16[18,65,1024]{2,1,0:T(8,128)(2,1)S(1)} %get-tuple-element.67, bf16[1,64,1024]{2,1,0:T(8,128)(2,1)S(1)} %collective-permute-done.4, bf16[18,65,1024]{2,1,0:T(8,128)(2,1)S(1)} %get-tuple-element.66, ...), kind=kLoop, calls=%fused_computation.37 | loop fusion | flops 50331648 | bytes 21270528 | tf_op jit(solution)/shard_map/convert_element_type | solution.py:578
  205.5 1.0 fusion.46.refs_0_
  206.5 0.8 fusion.57
  208.4 44.3 %weight_sum.1 = (bf16[256,1024]{1,0:T(8,128)(2,1)S(1)}, bf16[1024,256]{1,0:T(8,128)(2,1)S(1)}, bf16[256,1024]{1,0:T(8,128)(2,1)S(1)}, f32[2,64,1,384]{3,2,1,0:T(1,128)S(1)}) custom-call(bf16[256,1024]{1,0:T(8,128)(2,1)S(1)} %fusion.46.refs_0_, bf16[1024,256]{1,0:T(8,128)(2,1)S(1)} %fusion.47.refs_1_, bf16[256,1024]{1,0:T(8,128)(2,1)S(1)} %convert_element_type.212.refs_2_, ...), custom_call_target="tpu_custom_call" | custom-call | tf_op jit(solution)/shard_map/weight_sum/pallas_call | solution.py:320
  254.0 0.9 slice_convert_fusion
  255.6 1.2 reduce
  256.8 1.8 slice.191
  258.6 1.0 slice_bitcast_fusion
  259.5 0.9 copy.27
  260.4 1.1 convert_element_type.213
  261.5 1.0 convert_element_type.214
  262.6 3.1 %add_convert_fusion = bf16[16,64,256]{2,1,0:T(8,128)(2,1)} fusion(f32[16,64]{1,0:T(8,128)S(1)} %negate_multiply_fusion, f32[16,64]{1,0:T(8,128)S(1)} %copy-done.34, f32[16,64]{1,0:T(8,128)S(1)} %broadcast_multiply_fusion.3, bf16[16,64,256]{2,1,0:T(8,128)(2,1)S(1)} %copy-done.14, f32[16,64]{1,0:T(8,128)S(1)} %copy-done.24, f32[16,64,256]{2,1,0:T(8,128)} %copy-done.16, ...), kind=kLoop, calls=%fused_computation.109 | loop fusion | flops 5505024 | bytes 3704832 | tf_op jit(solution)/shard_map/convert_element_type | solution.py:587
  (188 shorter events, 12.2 us)
Async XLA Ops:
  4.1 22.1 %copy-start.40 = (bf16[3,3,1024]{2,1,0:T(4,128)(2,1)S(1)}, bf16[3,3,1024]{2,1,0:T(4,128)(2,1)}, u32[]{:S(2)}) copy-start(bf16[3,3,1024]{2,1,0:T(4,128)(2,1)} %param.16) | copy-start | bytes 55300
  4.1 22.2 %copy-start.74 = (bf16[256]{0:T(256)(128)(2,1)S(1)}, bf16[256]{0:T(256)(128)(2,1)}, u32[]{:S(2)}) copy-start(bf16[256]{0:T(256)(128)(2,1)} %param.20) | copy-start | bytes 1540
  4.1 22.8 %copy-start.21 = (f32[8,64,64]{2,1,0:T(8,128)S(1)}, f32[8,64,64]{2,1,0:T(8,128)}, u32[]{:S(2)}) copy-start(f32[8,64,64]{2,1,0:T(8,128)} %param.23) | copy-start | bytes 393220
  8.8 36.9 %copy-start.9 = (bf16[16,64,1024]{2,1,0:T(8,128)(2,1)}, bf16[16,64,1024]{2,1,0:T(8,128)(2,1)S(1)}, u32[]{:S(2)}) copy-start(bf16[16,64,1024]{2,1,0:T(8,128)(2,1)S(1)} %get-tuple-element.91) | copy-start | bytes 6291460
  8.8 6.5 %collective-permute-start = (bf16[1,64,1024]{2,1,0:T(8,128)(2,1)S(1)}, bf16[1,64,1024]{2,1,0:T(8,128)(2,1)S(1)}, u32[]{:S(2)}, u32[]{:S(2)}) collective-permute-start(bf16[1,64,1024]{2,1,0:T(8,128)(2,1)S(1)} %get-tuple-element.76), channel_id=1, source_target_pairs={{0,16},{16,32},{32,48},{48,64},{64,80},{80,96},{96,112},{1,17},{17... | collective-permute-start | bytes 393224 | tf_op jit(solution)/shard_map/ppermute | solution.py:450
  13.2 5.7 %collective-permute-start.1 = (bf16[1,64,1024]{2,1,0:T(8,128)(2,1)S(1)}, bf16[1,64,1024]{2,1,0:T(8,128)(2,1)S(1)}, u32[]{:S(2)}, u32[]{:S(2)}) collective-permute-start(bf16[1,64,1024]{2,1,0:T(8,128)(2,1)S(1)} %get-tuple-element.77), channel_id=1, source_target_pairs={{16,0},{32,16},{48,32},{64,48},{80,64},{96,80},{112,96},{17,1},{33... | collective-permute-start | bytes 393224 | tf_op jit(solution)/shard_map/ppermute | solution.py:452
  18.9 26.8 %copy-start.18 = (bf16[1,64,1024]{2,1,0:T(8,128)(2,1)}, bf16[1,64,1024]{2,1,0:T(8,128)(2,1)S(1)}, u32[]{:S(2)}) copy-start(bf16[1,64,1024]{2,1,0:T(8,128)(2,1)S(1)} %collective-permute-done.1) | copy-start | bytes 393220
  19.0 24.4 %collective-permute-start.2 = (bf16[18,1,1024]{2,1,0:T(2,128)(2,1)S(1)}, bf16[18,1,1024]{2,1,0:T(2,128)(2,1)S(1)}, u32[]{:S(2)}, u32[]{:S(2)}) collective-permute-start(bf16[18,1,1024]{2,1,0:T(2,128)(2,1)S(1)} %get-tuple-element.72), channel_id=1, source_target_pairs={{0,1},{1,2},{2,3},{3,4},{4,5},{5,6},{6,7},{7,8},{8,9},{9,10},{10,1... | collective-permute-start | bytes 110600 | tf_op jit(solution)/shard_map/ppermute | solution.py:450
  24.1 19.3 %collective-permute-start.3 = (bf16[18,1,1024]{2,1,0:T(2,128)(2,1)S(1)}, bf16[18,1,1024]{2,1,0:T(2,128)(2,1)}, u32[]{:S(2)}, u32[]{:S(2)}) collective-permute-start(bf16[18,1,1024]{2,1,0:T(2,128)(2,1)S(1)} %get-tuple-element.73), channel_id=1, source_target_pairs={{1,0},{2,1},{3,2},{4,3},{5,4},{6,5},{7,6},{8,7},{9,8},{10,9},{11,1... | collective-permute-start | bytes 110600 | tf_op jit(solution)/shard_map/ppermute | solution.py:452
  26.3 19.4 %copy-start.41 = (f32[1,1,1024]{2,1,0:T(1,128)}, f32[1,1,1024]{2,1,0:T(1,128)S(1)}, u32[]{:S(2)}) copy-start(f32[1,1,1024]{2,1,0:T(1,128)S(1)} %get-tuple-element.80) | copy-start | bytes 12292
  26.3 19.4 %copy-start.43 = (f32[1,1,1024]{2,1,0:T(1,128)}, f32[1,1,1024]{2,1,0:T(1,128)S(1)}, u32[]{:S(2)}) copy-start(f32[1,1,1024]{2,1,0:T(1,128)S(1)} %get-tuple-element.81) | copy-start | bytes 12292
  26.3 19.4 %copy-start.45 = (f32[1,1,1024]{2,1,0:T(1,128)}, f32[1,1,1024]{2,1,0:T(1,128)S(1)}, u32[]{:S(2)}) copy-start(f32[1,1,1024]{2,1,0:T(1,128)S(1)} %get-tuple-element.82) | copy-start | bytes 12292
  26.3 19.4 %copy-start.47 = (f32[1,1,1024]{2,1,0:T(1,128)}, f32[1,1,1024]{2,1,0:T(1,128)S(1)}, u32[]{:S(2)}) copy-start(f32[1,1,1024]{2,1,0:T(1,128)S(1)} %get-tuple-element.83) | copy-start | bytes 12292
  26.3 19.4 %copy-start.49 = (f32[1,1,1024]{2,1,0:T(1,128)}, f32[1,1,1024]{2,1,0:T(1,128)S(1)}, u32[]{:S(2)}) copy-start(f32[1,1,1024]{2,1,0:T(1,128)S(1)} %get-tuple-element.84) | copy-start | bytes 12292
  26.4 19.4 %copy-start.51 = (f32[1,1,1024]{2,1,0:T(1,128)}, f32[1,1,1024]{2,1,0:T(1,128)S(1)}, u32[]{:S(2)}) copy-start(f32[1,1,1024]{2,1,0:T(1,128)S(1)} %get-tuple-element.85) | copy-start | bytes 12292
  26.4 19.4 %copy-start.53 = (f32[1,1,1024]{2,1,0:T(1,128)}, f32[1,1,1024]{2,1,0:T(1,128)S(1)}, u32[]{:S(2)}) copy-start(f32[1,1,1024]{2,1,0:T(1,128)S(1)} %get-tuple-element.86) | copy-start | bytes 12292
  26.4 19.4 %copy-start.55 = (f32[1,1,1024]{2,1,0:T(1,128)}, f32[1,1,1024]{2,1,0:T(1,128)S(1)}, u32[]{:S(2)}) copy-start(f32[1,1,1024]{2,1,0:T(1,128)S(1)} %get-tuple-element.87) | copy-start | bytes 12292
  26.4 19.4 %copy-start.57 = (f32[1,1,1024]{2,1,0:T(1,128)}, f32[1,1,1024]{2,1,0:T(1,128)S(1)}, u32[]{:S(2)}) copy-start(f32[1,1,1024]{2,1,0:T(1,128)S(1)} %get-tuple-element.88) | copy-start | bytes 12292
  45.7 8.3 %copy-start.7 = (bf16[18,65,1024]{2,1,0:T(8,128)(2,1)}, bf16[18,65,1024]{2,1,0:T(8,128)(2,1)S(1)}, u32[]{:S(2)}) copy-start(bf16[18,65,1024]{2,1,0:T(8,128)(2,1)S(1)} %get-tuple-element.70) | copy-start | bytes 7188484
  45.7 8.3 %copy-start.8 = (bf16[18,65,1024]{2,1,0:T(8,128)(2,1)}, bf16[18,65,1024]{2,1,0:T(8,128)(2,1)S(1)}, u32[]{:S(2)}) copy-start(bf16[18,65,1024]{2,1,0:T(8,128)(2,1)S(1)} %get-tuple-element.71) | copy-start | bytes 7188484
  45.8 25.5 %copy-start.31 = (bf16[1024,64]{0,1:T(8,128)(2,1)S(1)}, bf16[1024,64]{0,1:T(8,128)(2,1)}, u32[]{:S(2)}) copy-start(bf16[1024,64]{0,1:T(8,128)(2,1)} %param.17) | copy-start | bytes 393220
  45.8 26.3 %copy-start.29 = (bf16[64,1024]{1,0:T(8,128)(2,1)S(1)}, bf16[64,1024]{1,0:T(8,128)(2,1)}, u32[]{:S(2)}) copy-start(bf16[64,1024]{1,0:T(8,128)(2,1)} %param.18) | copy-start | bytes 393220
  72.6 18.8 %copy-start.1 = (bf16[64,16,256]{2,1,0:T(8,128)(2,1)S(1)}, bf16[64,16,256]{2,1,0:T(8,128)(2,1)}, u32[]{:S(2)}) copy-start(bf16[64,16,256]{2,1,0:T(8,128)(2,1)} %exchange.4.dy_ref) | copy-start | bytes 1572868
  72.7 18.8 %copy-start.5 = (bf16[256,256]{1,0:T(8,128)(2,1)S(1)}, bf16[256,256]{1,0:T(8,128)(2,1)}, u32[]{:S(2)}) copy-start(bf16[256,256]{1,0:T(8,128)(2,1)} %w_out.1) | copy-start | bytes 393220
  72.7 18.8 %copy-start.6 = (bf16[256,768]{1,0:T(8,128)(2,1)S(1)}, bf16[256,768]{1,0:T(8,128)(2,1)}, u32[]{:S(2)}) copy-start(bf16[256,768]{1,0:T(8,128)(2,1)} %w_qkv.1) | copy-start | bytes 1179652
  139.0 21.1 %copy-start.60 = (f32[1,1024]{1,0:T(1,128)S(1)}, f32[1,1024]{1,0:T(1,128)}, u32[]{:S(2)}) copy-start(f32[1,1024]{1,0:T(1,128)} %copy-done.59) | copy-start | bytes 12292
  139.1 21.8 %copy-start.30 = (bf16[64,1024]{1,0:T(8,128)(2,1)S(1)}, bf16[64,1024]{1,0:T(8,128)(2,1)}, u32[]{:S(2)}) copy-start(bf16[64,1024]{1,0:T(8,128)(2,1)} %param.18) | copy-start | bytes 393220
  139.1 21.8 %copy-start.72 = (f32[64]{0:T(128)S(1)}, f32[64]{0:T(128)}, u32[]{:S(2)}) copy-start(f32[64]{0:T(128)} %copy-done.71) | copy-start | bytes 772
  139.1 21.9 %copy-start.32 = (bf16[1024,64]{0,1:T(8,128)(2,1)S(1)}, bf16[1024,64]{0,1:T(8,128)(2,1)}, u32[]{:S(2)}) copy-start(bf16[1024,64]{0,1:T(8,128)(2,1)} %param.17) | copy-start | bytes 393220
  139.1 22.2 %copy-start.19 = (bf16[1,64,1024]{2,1,0:T(8,128)(2,1)S(1)}, bf16[1,64,1024]{2,1,0:T(8,128)(2,1)}, u32[]{:S(2)}) copy-start(bf16[1,64,1024]{2,1,0:T(8,128)(2,1)} %copy-done.18) | copy-start | bytes 393220
  139.1 22.2 %copy-start.65 = (f32[1024]{0:T(1024)S(1)}, f32[1024]{0:T(1024)}, u32[]{:S(2)}) copy-start(f32[1024]{0:T(1024)} %copy-done.64) | copy-start | bytes 12292
  161.3 17.4 %copy-start.63 = (f32[1024]{0:T(1024)S(1)}, f32[1024]{0:T(1024)}, u32[]{:S(2)}) copy-start(f32[1024]{0:T(1024)} %get-tuple-element.89) | copy-start | bytes 12292
  161.3 29.6 %copy-start.70 = (f32[64]{0:T(128)S(1)}, f32[64]{0:T(128)}, u32[]{:S(2)}) copy-start(f32[64]{0:T(128)} %get-tuple-element.99) | copy-start | bytes 772
  174.6 17.2 %copy-start.10 = (bf16[16,64,1024]{2,1,0:T(8,128)(2,1)}, bf16[16,64,1024]{2,1,0:T(8,128)(2,1)S(1)}, u32[]{:S(2)}) copy-start(bf16[16,64,1024]{2,1,0:T(8,128)(2,1)S(1)} %get-tuple-element.63) | copy-start | bytes 6291460
  174.6 4.9 %collective-permute-start.4 = (bf16[1,64,1024]{2,1,0:T(8,128)(2,1)S(1)}, bf16[1,64,1024]{2,1,0:T(8,128)(2,1)S(1)}, u32[]{:S(2)}, u32[]{:S(2)}) collective-permute-start(bf16[1,64,1024]{2,1,0:T(8,128)(2,1)S(1)} %get-tuple-element.74), channel_id=1, source_target_pairs={{0,16},{16,32},{32,48},{48,64},{64,80},{80,96},{96,112},{1,17},{17... | collective-permute-start | bytes 393224 | tf_op jit(solution)/shard_map/ppermute | solution.py:450
  177.4 5.7 %collective-permute-start.5 = (bf16[1,64,1024]{2,1,0:T(8,128)(2,1)S(1)}, bf16[1,64,1024]{2,1,0:T(8,128)(2,1)S(1)}, u32[]{:S(2)}, u32[]{:S(2)}) collective-permute-start(bf16[1,64,1024]{2,1,0:T(8,128)(2,1)S(1)} %get-tuple-element.75), channel_id=1, source_target_pairs={{16,0},{32,16},{48,32},{64,48},{80,64},{96,80},{112,96},{17,1},{33... | collective-permute-start | bytes 393224 | tf_op jit(solution)/shard_map/ppermute | solution.py:452
  183.9 9.5 %collective-permute-start.6 = (bf16[18,1,1024]{2,1,0:T(2,128)(2,1)}, bf16[18,1,1024]{2,1,0:T(2,128)(2,1)}, u32[]{:S(2)}, u32[]{:S(2)}) collective-permute-start(bf16[18,1,1024]{2,1,0:T(2,128)(2,1)} %get-tuple-element.68), channel_id=1, source_target_pairs={{1,0},{2,1},{3,2},{4,3},{5,4},{6,5},{7,6},{8,7},{9,8},{10,9},{11,1... | collective-permute-start | bytes 110600 | tf_op jit(solution)/shard_map/ppermute | solution.py:452
  188.5 5.0 %collective-permute-start.7 = (bf16[18,1,1024]{2,1,0:T(2,128)(2,1)}, bf16[18,1,1024]{2,1,0:T(2,128)(2,1)}, u32[]{:S(2)}, u32[]{:S(2)}) collective-permute-start(bf16[18,1,1024]{2,1,0:T(2,128)(2,1)} %get-tuple-element.69), channel_id=1, source_target_pairs={{0,1},{1,2},{2,3},{3,4},{4,5},{5,6},{6,7},{7,8},{8,9},{9,10},{10,1... | collective-permute-start | bytes 110600 | tf_op jit(solution)/shard_map/ppermute | solution.py:450
  197.6 7.8 %copy-start.67 = (f32[256]{0:T(256)S(1)}, f32[256]{0:T(256)}, u32[]{:S(2)}) copy-start(f32[256]{0:T(256)} %copy-done.66) | copy-start | bytes 3076
  208.3 54.2 %copy-start.24 = (f32[16,64]{1,0:T(8,128)S(1)}, f32[16,64]{1,0:T(8,128)}, u32[]{:S(2)}) copy-start(f32[16,64]{1,0:T(8,128)} %copy-done.22) | copy-start | bytes 12292
  208.3 54.2 %copy-start.26 = (f32[16,64]{1,0:T(8,128)S(1)}, f32[16,64]{1,0:T(8,128)}, u32[]{:S(2)}) copy-start(f32[16,64]{1,0:T(8,128)} %copy-done.25) | copy-start | bytes 12292
  208.3 54.2 %copy-start.28 = (f32[16,64]{1,0:T(8,128)S(1)}, f32[16,64]{1,0:T(8,128)}, u32[]{:S(2)}) copy-start(f32[16,64]{1,0:T(8,128)} %copy-done.27) | copy-start | bytes 12292
  208.3 54.2 %copy-start.34 = (f32[16,64]{1,0:T(8,128)S(1)}, f32[16,64]{1,0:T(8,128)}, u32[]{:S(2)}) copy-start(f32[16,64]{1,0:T(8,128)} %copy-done.33) | copy-start | bytes 12292
  208.3 54.2 %copy-start.36 = (f32[16,64]{1,0:T(8,128)S(1)}, f32[16,64]{1,0:T(8,128)}, u32[]{:S(2)}) copy-start(f32[16,64]{1,0:T(8,128)} %copy-done.35) | copy-start | bytes 12292
  208.4 54.2 %copy-start.62 = (f32[256]{0:T(256)S(1)}, f32[256]{0:T(256)}, u32[]{:S(2)}) copy-start(f32[256]{0:T(256)} %convert_element_type.191) | copy-start | bytes 3076
  208.4 54.2 %copy-start.68 = (f32[256]{0:T(256)S(1)}, f32[256]{0:T(256)}, u32[]{:S(2)}) copy-start(f32[256]{0:T(256)} %copy-done.66) | copy-start | bytes 3076
  252.7 9.8 %copy-start.14 = (bf16[16,64,256]{2,1,0:T(8,128)(2,1)S(1)}, bf16[16,64,256]{2,1,0:T(8,128)(2,1)}, u32[]{:S(2)}) copy-start(bf16[16,64,256]{2,1,0:T(8,128)(2,1)} %param.12) | copy-start | bytes 1572868
  252.7 9.8 %copy-start.15 = (bf16[64,16,256]{2,1,0:T(8,128)(2,1)S(1)}, bf16[64,16,256]{2,1,0:T(8,128)(2,1)}, u32[]{:S(2)}) copy-start(bf16[64,16,256]{2,1,0:T(8,128)(2,1)} %get-tuple-element.25) | copy-start | bytes 1572868
  (35 other events, 132.0 us)

commit v2 on v0

v2 whole, which is shorter than its diff:
```python
import functools

import jax
import jax.numpy as jnp
from jax import lax
from jax.experimental import pallas as pl
from jax.experimental.pallas import tpu as pltpu
from jax.sharding import PartitionSpec as P

F32 = jnp.float32
BF16 = jnp.bfloat16
MESH = pl.DeviceIdType.MESH
ROWS = 8
COLS = 16
CHIPS = 64
HEADS = 8
MEMBERS = 64
GROUPS = 16
CH = 256
MAP_ROWS = 16
MAP_COLS = 64
CELLS = MAP_ROWS * MAP_COLS
CELLS_TOTAL = 131072
LANES = 8
PAD = 80
PADDED = (MAP_ROWS + 2) * PAD
TILE = 256
SCALE = 32 ** (-0.5)
GELU_A = 0.7978845608028654
GELU_B = 0.044715


def nn(a, b):
    return jnp.dot(a, b, preferred_element_type=F32)


def nt(a, b):
    return lax.dot_general(a, b, (((1,), (1,)), ((), ())), preferred_element_type=F32)


def tn(a, b):
    return lax.dot_general(a, b, (((0,), (0,)), ((), ())), preferred_element_type=F32)


def gelu(x):
    return 0.5 * x * (1.0 + jnp.tanh(GELU_A * (x + GELU_B * (x * x * x))))


def gelu_slope(x):
    square = x * x
    t = jnp.tanh(GELU_A * (x + GELU_B * (square * x)))
    return 0.5 * (1.0 + t) + (0.5 * GELU_A) * x * (1.0 - t * t) * (1.0 + (3 * GELU_B) * square)


def centre(x):
    centered = x - jnp.mean(x, axis=-1, keepdims=True)
    rstd = lax.rsqrt(jnp.mean(centered * centered, axis=-1, keepdims=True) + 1e-05)
    return centered * rstd, rstd


def norm_back(unit, rstd, grad_unit):
    first = jnp.mean(grad_unit, axis=-1, keepdims=True)
    second = jnp.mean(grad_unit * unit, axis=-1, keepdims=True)
    return rstd * (grad_unit - first - unit * second)


def fold(x):
    return jnp.sum(x.reshape(x.shape[0] // 8, 8, x.shape[1]), axis=0)


def thirds(x):
    one = x.astype(BF16).astype(F32)
    two = (x - one).astype(BF16).astype(F32)
    three = (x - one - two).astype(BF16).astype(F32)
    return one, two, three


def stack_rows(rows):
    width = rows[0].shape[1]
    rows = list(rows) + [jnp.zeros((8 - len(rows), width), F32)]
    return jnp.concatenate(rows, axis=0).astype(BF16)


def wide_product(x, w, product):
    return jnp.sum(product(stack_rows(thirds(x)), w), axis=0, keepdims=True)


def outer(a, b):
    a1, a2, a3 = thirds(a)
    b1, b2, b3 = thirds(b)
    return tn(stack_rows([a1, a1, a2, a2, a1, a3]), stack_rows([b1, b2, b1, b2, b3, b1]))


def aligned(start, size, unit=8):
    return pl.ds(pl.multiple_of(start, unit), size)


class Place:
    def __init__(self):
        self.row = lax.axis_index("row")
        self.col = lax.axis_index("col")
        self.core = lax.rem(self.col, 2)
        self.q = lax.div(self.col, 2)
        self.chip = self.row * 8 + self.q
        self.qs = [lax.rem(self.q + k, 8) for k in range(8)]
        self.cols = [q * 2 + self.core for q in self.qs]

    def partner(self):
        return (self.row, self.q * 2 + 1 - self.core)

    def q_peer(self, k):
        return self.qs[k], (self.row, self.cols[k])

    def row_peer(self, k):
        row = lax.rem(self.row + k, ROWS)
        return row, (row, self.col)

    def beside(self, up, right):
        return (lax.rem(self.row + ROWS + up, ROWS), lax.rem(self.col + COLS + right, COLS))

    def every_peer(self, body):
        def others(k, carry):
            row = lax.rem(self.row + k, ROWS)
            for n in range(1, 8):
                body(row, self.qs[n], (row, self.cols[n]))
            return carry

        def same(k, carry):
            row = lax.rem(self.row + k, ROWS)
            body(row, self.q, (row, self.col))
            return carry

        lax.fori_loop(0, ROWS, others, 0)
        lax.fori_loop(1, ROWS, same, 0)


class Links:
    def __init__(self, sems):
        self.sems = sems
        self.used = 0
        self.sent = []

    def pair(self):
        at = self.used
        self.used += 2
        return self.sems.at[at], self.sems.at[at + 1]

    def finish(self):
        for sem, buf in self.sent:
            pltpu.make_async_copy(buf, buf, sem).wait()


def push(src, dst, send, recv, device):
    pltpu.make_async_remote_copy(
        src_ref=src,
        dst_ref=dst,
        send_sem=send,
        recv_sem=recv,
        device_id=device,
        device_id_type=MESH,
    ).start()


def arrived(buf, sem):
    pltpu.make_async_copy(buf, buf, sem).wait()


class TileSum:
    def __init__(self, me, links, x, pair_slot, slots):
        self.me, self.links = me, links
        self.x, self.pair_slot, self.slots = x, pair_slot, slots
        self.s0, self.s1 = links.pair(), links.pair()

    def start(self):
        push(self.x, self.pair_slot, *self.s0, self.me.partner())
        self.links.sent.append((self.s0[0], self.x))
        arrived(self.pair_slot, self.s0[1])
        self.slots[self.me.chip] = self.x[...] + self.pair_slot[...]
        mine = self.slots.at[self.me.chip]
        self.me.every_peer(lambda row, q, device: push(mine, mine, *self.s1, device))
        self.links.sent.append((self.s1[0], self.slots.at[pl.ds(0, CHIPS - 1)]))

    def end(self):
        arrived(self.slots.at[pl.ds(0, CHIPS - 1)], self.s1[1])
        return jnp.sum(self.slots[...], axis=0)


class BigSum:
    def __init__(self, me, links, x, pair_in, summed, slots_a, total_a, slots_b, out):
        self.me, self.links = me, links
        self.x, self.pair_in, self.summed, self.out = x, pair_in, summed, out
        self.slots_a, self.total_a, self.slots_b = slots_a, total_a, slots_b
        self.half = x.shape[0] // 2
        self.across = x.shape[1] // 128
        self.sems = [links.pair() for _ in range(6)]

    def half_of(self, ref, core):
        return ref.at[aligned(core * self.half, self.half, 128)]

    def block(self, ref, base, q, row=None):
        first = base + lax.div(q, self.across) * 128
        size = 128
        if row is not None:
            first, size = first + row * 16, 16
        lane = aligned(lax.rem(q, self.across) * 128, 128, 128)
        return ref.at[aligned(first, size, 16), lane]

    def start(self):
        push(
            self.half_of(self.x, 1 - self.me.core),
            self.pair_in,
            *self.sems[0],
            self.me.partner(),
        )
        self.links.sent.append((self.sems[0][0], self.pair_in))

    def to_q(self):
        arrived(self.pair_in, self.sems[0][1])
        mine = self.half_of(self.x, self.me.core)
        for n in range(self.half // 128):
            at = pl.ds(n * 128, 128)
            self.summed[at] = (mine[at].astype(F32) + self.pair_in[at].astype(F32)).astype(BF16)
        for k in range(1, 8):
            q, device = self.me.q_peer(k)
            push(
                self.block(self.summed, 0, q), self.slots_a.at[self.me.q], *self.sems[1], device
            )
        self.links.sent.append((self.sems[1][0], self.slots_a.at[pl.ds(0, 7)]))

    def to_rows(self):
        self.slots_a[self.me.q] = self.block(self.summed, 0, self.me.q)[...]
        arrived(self.slots_a.at[pl.ds(0, 7)], self.sems[1][1])
        self.total_a[...] = jnp.sum(self.slots_a[...].astype(F32), axis=0).astype(BF16)
        for k in range(1, 8):
            row, device = self.me.row_peer(k)
            piece = self.total_a.at[aligned(row * 16, 16, 16)]
            push(piece, self.slots_b.at[self.me.row], *self.sems[2], device)
        self.links.sent.append((self.sems[2][0], self.slots_b.at[pl.ds(0, 7)]))

    def back_rows(self):
        me = self.me
        self.slots_b[me.row] = self.total_a[aligned(me.row * 16, 16, 16)]
        arrived(self.slots_b.at[pl.ds(0, 7)], self.sems[2][1])
        total = jnp.sum(self.slots_b[...].astype(F32), axis=0).astype(BF16)
        piece = self.block(self.out, me.core * self.half, me.q, me.row)
        piece[...] = total
        for k in range(1, 8):
            _, device = me.row_peer(k)
            push(piece, piece, *self.sems[3], device)
        self.links.sent.append((self.sems[3][0], self.slots_b.at[pl.ds(0, 7)]))

    def back_q(self):
        me = self.me
        arrived(self.slots_b.at[pl.ds(0, 7)], self.sems[3][1])
        piece = self.block(self.out, me.core * self.half, me.q)
        for k in range(1, 8):
            _, device = me.q_peer(k)
            push(piece, piece, *self.sems[4], device)
        self.links.sent.append((self.sems[4][0], self.slots_a.at[pl.ds(0, 7)]))

    def back_pair(self):
        me = self.me
        arrived(self.slots_a.at[pl.ds(0, 7)], self.sems[4][1])
        piece = self.half_of(self.out, me.core)
        push(piece, piece, *self.sems[5], me.partner())
        self.links.sent.append((self.sems[5][0], self.pair_in))

    def end(self):
        arrived(self.pair_in, self.sems[5][1])


class DirectSum(BigSum):
    def __init__(self, me, links, x, pair_in, summed, slots, out):
        super().__init__(me, links, x, pair_in, summed, None, None, None, out)
        self.slots = slots

    def scatter(self):
        me = self.me
        arrived(self.pair_in, self.sems[0][1])
        mine = self.half_of(self.x, me.core)
        for n in range(self.half // 128):
            at = pl.ds(n * 128, 128)
            self.summed[at] = (mine[at].astype(F32) + self.pair_in[at].astype(F32)).astype(BF16)

        def send(row, q, device):
            push(
                self.block(self.summed, 0, q, row), self.slots.at[me.chip], *self.sems[1], device
            )

        me.every_peer(send)
        self.slots[me.chip] = self.block(self.summed, 0, me.q, me.row)[...]
        self.links.sent.append((self.sems[1][0], self.slots.at[pl.ds(0, CHIPS - 1)]))

    def gather(self):
        me = self.me
        arrived(self.slots.at[pl.ds(0, CHIPS - 1)], self.sems[1][1])
        piece = self.block(self.out, me.core * self.half, me.q, me.row)
        piece[...] = jnp.sum(self.slots[...].astype(F32), axis=0).astype(BF16)
        me.every_peer(lambda row, q, device: push(piece, piece, *self.sems[2], device))
        self.links.sent.append((self.sems[2][0], self.slots.at[pl.ds(0, CHIPS - 1)]))

    def back_pair(self):
        me = self.me
        arrived(self.slots.at[pl.ds(0, CHIPS - 1)], self.sems[2][1])
        piece = self.half_of(self.out, me.core)
        push(piece, piece, *self.sems[5], me.partner())
        self.links.sent.append((self.sems[5][0], self.pair_in))


class SmallSum:
    def __init__(self, me, links, x, pair_in, summed, slots_a, slots_b, out):
        self.me, self.links = me, links
        self.x, self.pair_in, self.summed, self.out = x, pair_in, summed, out
        self.slots_a, self.slots_b = slots_a, slots_b
        self.sems = [links.pair() for _ in range(4)]

    def start(self):
        push(self.x, self.pair_in, *self.sems[0], self.me.partner())
        self.links.sent.append((self.sems[0][0], self.pair_in))

    def to_q(self):
        arrived(self.pair_in, self.sems[0][1])
        self.summed[...] = self.x[...] + self.pair_in[...]
        for k in range(1, 8):
            q, device = self.me.q_peer(k)
            piece = self.summed.at[aligned(q * 8, 8)]
            push(piece, self.slots_a.at[self.me.q], *self.sems[1], device)
        self.links.sent.append((self.sems[1][0], self.slots_a.at[pl.ds(0, 7)]))

    def to_rows(self):
        me = self.me
        self.slots_a[me.q] = self.summed[aligned(me.q * 8, 8)]
        arrived(self.slots_a.at[pl.ds(0, 7)], self.sems[1][1])
        self.slots_b[me.row] = jnp.sum(self.slots_a[...], axis=0)
        for k in range(1, 8):
            _, device = me.row_peer(k)
            piece = self.slots_b.at[me.row]
            push(piece, piece, *self.sems[2], device)
        self.links.sent.append((self.sems[2][0], self.slots_b.at[pl.ds(0, 7)]))

    def back_q(self):
        me = self.me
        arrived(self.slots_b.at[pl.ds(0, 7)], self.sems[2][1])
        piece = self.out.at[aligned(me.q * 8, 8)]
        piece[...] = jnp.sum(self.slots_b[...], axis=0)
        for k in range(1, 8):
            _, device = me.q_peer(k)
            push(piece, piece, *self.sems[3], device)
        self.links.sent.append((self.sems[3][0], self.slots_a.at[pl.ds(0, 7)]))

    def end(self):
        arrived(self.slots_a.at[pl.ds(0, 7)], self.sems[3][1])


class Exchange:
    def __init__(self, me, links, src, dst):
        self.me, self.links, self.src, self.dst = me, links, src, dst
        self.sems = links.pair()

    def send(self, row, k):
        q, col = self.me.qs[k], self.me.cols[k]
        push(self.src.at[row * 8 + q], self.dst.at[self.me.chip], *self.sems, (row, col))

    def send_row(self, row):
        for k in range(1, 8):
            self.send(row, k)

        @pl.when(row != self.me.row)
        def _():
            self.send(row, 0)

    def send_tile(self, t):
        for k in range(2):
            self.send_row(t * 2 + lax.rem(self.me.row + k, 2))

    def end(self):
        self.dst[self.me.chip] = self.src[self.me.chip]
        arrived(self.dst.at[pl.ds(0, CHIPS - 1)], self.sems[1])
        self.links.sent.append((self.sems[0], self.dst.at[pl.ds(0, CHIPS - 1)]))


class Halo:
    def __init__(
        self, me, links, rows_out, cols_out, corners_out, rows_in, cols_in, corners_in
    ):
        self.me, self.links = me, links
        self.rows_out, self.cols_out, self.corners_out = rows_out, cols_out, corners_out
        self.rows_in, self.cols_in, self.corners_in = rows_in, cols_in, corners_in
        self.sems = [links.pair() for _ in range(3)]

    def start(self):
        me = self.me
        for side, up in ((0, -1), (1, 1)):
            push(
                self.rows_out[side],
                self.rows_in.at[1 - side],
                *self.sems[0],
                me.beside(up, 0),
            )
        for side, right in ((0, -1), (1, 1)):
            strip = self.cols_out.at[side]
            push(strip, self.cols_in.at[1 - side], *self.sems[1], me.beside(0, right))
            for end, up in ((0, -1), (1, 1)):
                push(
                    self.corners_out[end * 2 + side],
                    self.corners_in.at[(1 - end) * 2 + 1 - side],
                    *self.sems[2],
                    me.beside(up, right),
                )

    def end(self):
        for n, buf in enumerate((self.rows_in, self.cols_in, self.corners_in)):
            arrived(buf, self.sems[n][1])
            self.links.sent.append((self.sems[n][0], buf))


IN_NAMES = ["image", "norm0_gain", "norm1_gain", "w_depth", "w_expand"]
LATE = dict(
    dy=((MEMBERS, GROUPS, CH), BF16),
    w_out=((CH, CH), BF16),
    bias=((HEADS, MEMBERS, MEMBERS), F32),
    w_squeeze_t=((64, 1024), BF16),
    w_excite=((64, 1024), BF16),
    w_project=((1024, CH), BF16),
    w_qkv=((CH, 768), BF16),
)
OUTS = dict(
    out_map=((MAP_ROWS, MAP_COLS, CH), BF16),
    grad_map=((MAP_ROWS, MAP_COLS, CH), BF16),
    sum_expand=((CH, 1024), BF16),
    sum_project=((1024, CH), BF16),
    sum_pair=((CH, 1024), BF16),
    sum_bias=((MEMBERS, 512), F32),
    sum_small=((64, 256), F32),
    gate_rows=((8, 1024), F32),
)


def big_scratch(name, rows, width):
    return {
        name + "_x": ((rows, width), BF16),
        name + "_pair": ((rows // 2, width), BF16),
        name + "_summed": ((rows // 2, width), BF16),
        name + "_a": ((8, 128, 128), BF16),
        name + "_total": ((128, 128), BF16),
        name + "_b": ((8, 16, 128), BF16),
    }


def small_scratch(name, width):
    return {
        name + "_x": ((64, width), F32),
        name + "_pair": ((64, width), F32),
        name + "_summed": ((64, width), F32),
        name + "_a": ((8, 8, width), F32),
        name + "_b": ((8, 8, width), F32),
    }


def tile_scratch(name):
    return {
        name + "_x": ((8, 128), F32),
        name + "_pair": ((8, 128), F32),
        name + "_slots": ((CHIPS, 8, 128), F32),
    }


SCRATCH = dict(
    taps=((16, 1024), F32),
    normed=((CELLS, CH), BF16),
    normed_t=((CH, CELLS), BF16),
    spread=((LANES, PADDED, 128), F32),
    expanded=((LANES, CELLS, 128), F32),
    depth=((LANES, CELLS, 128), F32),
    act=((LANES, CELLS, 128), BF16),
    pool_acc=((LANES, 8, 128), F32),
    edge_cols=((2, 16, CH), BF16),
    edge_rows_in=((2, MAP_COLS, CH), BF16),
    edge_cols_in=((2, 16, CH), BF16),
    edge_corners_in=((4, 16, CH), BF16),
    gate=((1, 1024), F32),
    gate_back=((1, 1024), F32),
    mixed=((CELLS, CH), BF16),
    normed_two=((MEMBERS, GROUPS, CH), BF16),
    grid_x=((MEMBERS, GROUPS, CH), BF16),
    grid_dy=((MEMBERS, GROUPS, CH), BF16),
    qkv=((6, CELLS, 128), F32),
    grid_g=((2, CELLS, 128), F32),
    att_rows=((2, CELLS, 128), F32),
    packed_back=((6, CELLS, 128), F32),
    probs=((GROUPS, MEMBERS, 512), F32),
    bias_t=((MEMBERS, 512), F32),
    att_out=((MEMBERS, GROUPS, CH), BF16),
    att_in=((MEMBERS, GROUPS, CH), BF16),
    gn_out=((MEMBERS, GROUPS, CH), BF16),
    gn_in=((MEMBERS, GROUPS, CH), BF16),
    grad_mixed=((CELLS, CH), F32),
    grad_mixed_b=((CELLS, CH), BF16),
    grad_gated=((LANES, CELLS, 128), F32),
    gate_acc=((LANES, 8, 128), F32),
    grad_pre=((LANES, PADDED, 128), F32),
    pre_rows=((2, LANES, MAP_COLS, 128), BF16),
    pre_cols=((2, LANES, 16, 128), BF16),
    pre_rows_in=((2, LANES, MAP_COLS, 128), BF16),
    pre_cols_in=((2, LANES, 16, 128), BF16),
    pre_corners=((4, 16, 128), BF16),
    pre_corners_in=((4, 16, 128), BF16),
    tap_acc=((LANES, 9, 8, 128), F32),
    grad_exp=((LANES, CELLS, 128), BF16),
    norm_acc=((2, 8, CH), F32),
    pair_acc=((CH, 1024), F32),
    **tile_scratch("pool"),
    **tile_scratch("gateg"),
    expand_x=((CH, 1024), BF16),
    expand_pair=((CH // 2, 1024), BF16),
    expand_summed=((CH // 2, 1024), BF16),
    expand_slots=((CHIPS, 16, 128), BF16),
    **big_scratch("project", 1024, CH),
    **big_scratch("pair", CH, 1024),
    **small_scratch("bias", 512),
    **small_scratch("small", 256),
)
SEMS = 96


class Refs:
    pass


def lanes_of(ref, first, at):
    return jnp.concatenate([ref[first, at, :], ref[first + 1, at, :]], axis=1)


def map_rows(t, count=4):
    return pl.ds(t * count, count)


def cell_rows(t):
    return aligned(t * TILE, TILE, TILE)


def pad_row(row, col=0):
    return pl.multiple_of(row * PAD + col, 8)


def block_kernel(*args):
    r = Refs()
    names = IN_NAMES + ["hbm_" + n for n in LATE] + ["hbm_" + n for n in OUTS]
    names += list(LATE) + list(OUTS) + list(SCRATCH) + ["sems", "late_sems", "out_sems"]
    for name, ref in zip(names, args, strict=True):
        setattr(r, name, ref)
    me = Place()
    links = Links(r.sems)

    def late(name):
        at = list(LATE).index(name)
        return pltpu.make_async_copy(
            getattr(r, "hbm_" + name), getattr(r, name), r.late_sems.at[at]
        )

    def flush(name):
        at = list(OUTS).index(name)
        return pltpu.make_async_copy(
            getattr(r, name), getattr(r, "hbm_" + name), r.out_sems.at[at]
        )

    for name in LATE:
        late(name).start()
    gain_first = r.norm0_gain[...].astype(F32).reshape(1, CH)
    gain_second = r.norm1_gain[...].astype(F32).reshape(1, CH)
    for a in range(3):
        r.taps[a * 3 : a * 3 + 3, :] = r.w_depth[a].astype(F32)
    off = r.image.shape[0] - 1

    barrier = pltpu.get_barrier_semaphore()

    def greet(row, q, device):
        pl.semaphore_signal(barrier, inc=1, device_id=device, device_id_type=MESH)

    me.every_peer(greet)
    for up in (-1, 0, 1):
        for right in (-1, 1):
            pl.semaphore_signal(
                barrier, inc=1, device_id=me.beside(up, right), device_id_type=MESH
            )

    for side, col in ((0, 0), (1, MAP_COLS - 16)):
        rows = []
        for i in range(MAP_ROWS):
            part = r.image[i, col : col + 16, :].astype(F32)
            rows.append(part[0:1] if side == 0 else part[15:16])
        r.edge_cols[side] = jnp.concatenate(rows, axis=0).astype(BF16)

    @pl.loop(0, 4)
    def _(t):
        x = r.image[map_rows(t)].reshape(TILE, CH).astype(F32)
        unit, _ = centre(x)
        r.normed[cell_rows(t)] = (unit * gain_first).astype(BF16)

    @pl.loop(0, 4)
    def _(t):
        @pl.loop(0, 4)
        def _(c):
            e = nn(r.normed[cell_rows(t)], r.w_expand[:, aligned(c * 256, 256, 256)])
            s = gelu(e).astype(BF16).astype(F32)
            for h in range(2):
                lane = slice(h * 128, (h + 1) * 128)
                r.expanded[2 * c + h, cell_rows(t), :] = e[:, lane]
                for a in range(4):
                    at = pl.ds(pad_row(1 + t * 4 + a, 8), MAP_COLS)
                    r.spread[2 * c + h, at, :] = s[a * 64 : (a + 1) * 64, lane]

    pl.semaphore_wait(barrier, CHIPS + 5)
    halo = Halo(
        me,
        links,
        (r.image.at[0], r.image.at[off]),
        r.edge_cols,
        [r.edge_cols.at[side] for side in (0, 1, 0, 1)],
        r.edge_rows_in,
        r.edge_cols_in,
        r.edge_corners_in,
    )
    halo.start()
    late("dy").wait()
    dy_out = Exchange(me, links, r.dy, r.grid_dy)

    @pl.loop(0, LANES * 4)
    def _(n):
        c, t = lax.div(n, 4), lax.rem(n, 4)
        row = lax.rem(me.row + c, ROWS)
        for k in range(2):
            q = lax.rem(me.q + t * 2 + k, 8)

            @pl.when(row * 8 + q != me.chip)
            def _():
                push(
                    r.dy.at[row * 8 + q],
                    r.grid_dy.at[me.chip],
                    *dy_out.sems,
                    (row, q * 2 + me.core),
                )

        r.expanded[c, cell_rows(t), :] = gelu_slope(r.expanded[c, cell_rows(t), :])

    halo.end()

    up_ok = (me.row > 0).astype(F32)
    down_ok = (me.row < ROWS - 1).astype(F32)
    left_ok = (me.col > 0).astype(F32)
    right_ok = (me.col < COLS - 1).astype(F32)
    around = jnp.concatenate(
        [
            r.edge_rows_in[0].astype(F32) * up_ok,
            r.edge_rows_in[1].astype(F32) * down_ok,
            r.edge_cols_in[0].astype(F32) * left_ok,
            r.edge_cols_in[1].astype(F32) * right_ok,
            r.edge_corners_in[0].astype(F32)[8:16] * (up_ok * left_ok),
            r.edge_corners_in[1].astype(F32)[8:16] * (up_ok * right_ok),
            r.edge_corners_in[2].astype(F32)[0:8] * (down_ok * left_ok),
            r.edge_corners_in[3].astype(F32)[0:8] * (down_ok * right_ok),
        ],
        axis=0,
    )
    unit, _ = centre(around)
    around_normed = (unit * gain_first).astype(BF16)
    last = (MAP_ROWS + 1) * PAD
    for c in range(4):
        s = gelu(nn(around_normed, r.w_expand[:, c * 256 : (c + 1) * 256]))
        s = s.astype(BF16).astype(F32)
        for h in range(2):
            v = s[:, h * 128 : (h + 1) * 128]
            n = 2 * c + h
            r.spread[n, 8:72, :] = v[0:64]
            r.spread[n, last + 8 : last + 72, :] = v[64:128]
            r.spread[n, pl.ds(PAD + 7, MAP_ROWS, stride=PAD), :] = v[128:144]
            r.spread[n, pl.ds(PAD + 72, MAP_ROWS, stride=PAD), :] = v[144:160]
            r.spread[n, 7:8, :] = v[167:168]
            r.spread[n, 72:73, :] = v[175:176]
            r.spread[n, last + 7 : last + 8, :] = v[176:177]
            r.spread[n, last + 72 : last + 73, :] = v[184:185]

    def taps_of(c):
        lane = aligned(c * 128, 128, 128)
        return [r.taps[k : k + 1, lane] for k in range(9)]

    @pl.loop(0, LANES)
    def _(c):
        taps = taps_of(c)

        def block(n, total):
            sums = [None] * 4
            for row in range(6):
                view = r.spread.at[c, pl.ds(pad_row(n * 4 + row), PAD)]
                for b in range(3):
                    v = view[pl.ds(7 + b, MAP_COLS), :]
                    for a in range(3):
                        i = row - a
                        if 0 <= i < 4:
                            term = v * taps[a * 3 + b]
                            sums[i] = term if sums[i] is None else sums[i] + term
            for i in range(4):
                at = aligned((n * 4 + i) * MAP_COLS, MAP_COLS, MAP_COLS)
                r.depth[c, at, :] = sums[i]
                value = gelu(sums[i])
                r.act[c, at, :] = value.astype(BF16)
                total = total + fold(value)
            return total

        total = lax.fori_loop(0, 4, block, jnp.zeros((8, 128), F32))
        r.pool_x[pl.ds(c, 1), :] = jnp.sum(total, axis=0, keepdims=True)

    pool = TileSum(me, links, r.pool_x, r.pool_pair, r.pool_slots)
    pool.start()

    @pl.loop(0, LANES * 4)
    def _(n):
        c, t = lax.div(n, 4), lax.rem(n, 4)
        r.depth[c, cell_rows(t), :] = gelu_slope(r.depth[c, cell_rows(t), :])

    dy_out.end()
    late("w_out").wait()
    late("bias").wait()

    @pl.loop(0, 4)
    def _(t):
        dy = r.grid_dy[map_rows(t, 16)].reshape(TILE, CH)
        g = nt(dy, r.w_out[...])
        for n in range(2):
            r.grid_g[n, cell_rows(t), :] = g[:, n * 128 : (n + 1) * 128]

    for h in range(0, HEADS, 2):
        both = jnp.concatenate([r.bias[h], r.bias[h + 1]], axis=0)
        r.bias_t[:, h * 64 : (h + 2) * 64] = both.T
    for t in range(4):
        r.normed_t[:, t * TILE : (t + 1) * TILE] = r.normed[t * TILE : (t + 1) * TILE].T

    def flat(tile):
        return jnp.concatenate([tile[n : n + 1] for n in range(8)], axis=1)

    pooled = flat(pool.end()) * (1.0 / CELLS_TOTAL)
    for name in ("w_squeeze_t", "w_excite", "w_project", "w_qkv"):
        late(name).wait()
    squeezed = wide_product(pooled, r.w_squeeze_t[...], nt)
    open_part = jax.nn.sigmoid(squeezed)
    hidden = squeezed * open_part
    gate = jax.nn.sigmoid(wide_product(hidden, r.w_excite[...], nn))
    r.gate[...] = gate

    grid_out = Exchange(me, links, r.normed_two, r.grid_x)
    start_tile = lax.div(me.row, 2)

    @pl.loop(0, 4)
    def _(step):
        t = lax.rem(start_tile + step, 4)
        total = r.image[map_rows(t)].reshape(TILE, CH).astype(F32)
        for c in range(4):
            lane = slice(c * 256, (c + 1) * 256)
            gated = lanes_of(r.act, 2 * c, cell_rows(t)).astype(F32) * r.gate[:, lane]
            total = total + nn(gated.astype(BF16), r.w_project[lane, :])
        mixed = total.astype(BF16)
        r.mixed[cell_rows(t)] = mixed
        unit, _ = centre(mixed.astype(F32))
        normed = (unit * gain_second).astype(BF16)
        r.normed_two[map_rows(t, 16)] = normed.reshape(16, GROUPS, CH)
        grid_out.send_tile(t)

    grid_out.end()

    @pl.loop(0, 4)
    def _(t):
        x = r.grid_x[map_rows(t, 16)].reshape(TILE, CH)
        qkv = nn(x, r.w_qkv[...])
        for n in range(6):
            r.qkv[n, cell_rows(t), :] = qkv[:, n * 128 : (n + 1) * 128]

    head_of = lax.div(lax.broadcasted_iota(jnp.int32, (1, 128), 1), 32)
    masks_f = [(head_of == h).astype(F32) for h in range(4)]
    masks = [m.astype(BF16) for m in masks_f]
    unroll = 4

    def spread_heads(a):
        return jnp.concatenate([a * m for m in masks], axis=0)

    def own_heads(v):
        total = v[0:MEMBERS] * masks_f[0]
        for h in range(1, 4):
            total = total + v[h * MEMBERS : (h + 1) * MEMBERS] * masks_f[h]
        return total

    def put(ref, n, at, value):
        ref[n, at, :] = value.astype(BF16).astype(F32)

    def group_forward(group):
        at = pl.ds(group, MEMBERS, stride=GROUPS)
        for n in range(2):
            q, k, v = [r.qkv[part * 2 + n, at, :].astype(BF16) for part in range(3)]
            lanes = slice(n * 256, (n + 1) * 256)
            scores = nt(k, spread_heads(q)) * SCALE + r.bias_t[:, lanes]
            lifted = jnp.exp(scores - jnp.max(scores, axis=0, keepdims=True))
            probs = lifted * (1.0 / jnp.sum(lifted, axis=0, keepdims=True))
            r.probs[group, :, lanes] = probs
            put(r.att_rows, n, at, own_heads(tn(probs.astype(BF16), v)))

    def group_back(group):
        at = pl.ds(group, MEMBERS, stride=GROUPS)
        bias_parts = []
        for n in range(2):
            q, k, v = [r.qkv[part * 2 + n, at, :].astype(BF16) for part in range(3)]
            lanes = slice(n * 256, (n + 1) * 256)
            q_heads = spread_heads(q)
            g_heads = spread_heads(r.grid_g[n, at, :].astype(BF16))
            probs = r.probs[group, :, lanes]
            put(r.packed_back, 4 + n, at, nn(probs.astype(BF16), g_heads))
            grad_probs = nt(v, g_heads)
            grad_scores = probs * (
                grad_probs - jnp.sum(grad_probs * probs, axis=0, keepdims=True)
            )
            bias_parts.append(grad_scores)
            scaled = (grad_scores * SCALE).astype(BF16)
            put(r.packed_back, n, at, own_heads(tn(scaled, k)))
            put(r.packed_back, 2 + n, at, nn(scaled, q_heads))
        return bias_parts

    @pl.loop(0, GROUPS // unroll)
    def _(step):
        for n in range(unroll):
            group_forward(step * unroll + n)

    @pl.loop(0, 4)
    def _(t):
        att = lanes_of(r.att_rows, 0, cell_rows(t)).astype(BF16)
        r.att_out[map_rows(t, 16)] = att.reshape(16, GROUPS, CH)

    att_back = Exchange(me, links, r.att_out, r.att_in)
    r.bias_x[...] = jnp.zeros_like(r.bias_x)

    @pl.loop(0, GROUPS // unroll)
    def _(step):
        for n in range(2):
            att_back.send_row(lax.rem(me.row + step * 2 + n, ROWS))
        total = group_back(step * unroll)
        for n in range(1, unroll):
            total = [a + b for a, b in zip(total, group_back(step * unroll + n))]
        for n in range(2):
            r.bias_x[:, n * 256 : (n + 1) * 256] += total[n]

    def packed_tile(t):
        parts = [r.packed_back[n, cell_rows(t), :] for n in range(6)]
        return jnp.concatenate(parts, axis=1).astype(BF16)

    gn_back = Exchange(me, links, r.gn_out, r.gn_in)

    @pl.loop(0, 4)
    def _(step):
        t = lax.rem(start_tile + step, 4)
        gn = nt(packed_tile(t), r.w_qkv[...]).astype(BF16)
        r.gn_out[map_rows(t, 16)] = gn.reshape(16, GROUPS, CH)
        gn_back.send_tile(t)

    bias_sum = SmallSum(
        me, links, r.bias_x, r.bias_pair, r.bias_summed, r.bias_a, r.bias_b, r.sum_bias
    )
    bias_sum.start()
    r.pair_acc[...] = jnp.zeros_like(r.pair_acc)

    @pl.loop(0, 4)
    def _(t):
        x = r.grid_x[map_rows(t, 16)].reshape(TILE, CH)
        dy = r.grid_dy[map_rows(t, 16)].reshape(TILE, CH)
        att = r.att_out[map_rows(t, 16)].reshape(TILE, CH)
        r.pair_acc[:, : 3 * CH] += tn(x, packed_tile(t))
        r.pair_acc[:, 3 * CH :] += tn(att, dy)

    r.pair_x[...] = r.pair_acc[...].astype(BF16)

    def big(name, out):
        parts = ["x", "pair", "summed", "a", "total", "b"]
        return BigSum(me, links, *[getattr(r, name + "_" + p) for p in parts], out)

    pair_sum = big("pair", r.sum_pair)
    pair_sum.start()
    gn_back.end()

    r.norm_acc[...] = jnp.zeros_like(r.norm_acc)
    r.gate_acc[...] = jnp.zeros_like(r.gate_acc)

    @pl.loop(0, 4)
    def _(t):
        unit, rstd = centre(r.mixed[cell_rows(t)].astype(F32))
        gn = r.gn_in[map_rows(t, 16)].reshape(TILE, CH).astype(F32)
        r.norm_acc[1] += fold(gn * unit)
        dy = r.dy[map_rows(t, 16)].reshape(TILE, CH).astype(F32)
        grad = dy + norm_back(unit, rstd, gn * gain_second)
        r.grad_mixed[cell_rows(t)] = grad
        grad_b = grad.astype(BF16)
        r.grad_mixed_b[cell_rows(t)] = grad_b
        for c in range(4):
            gg = nt(grad_b, r.w_project[c * 256 : (c + 1) * 256, :])
            for h in range(2):
                n = 2 * c + h
                part = gg[:, h * 128 : (h + 1) * 128]
                r.grad_gated[n, cell_rows(t), :] = part
                r.gate_acc[n] += fold(part * r.act[n, cell_rows(t), :].astype(F32))

    for n in range(LANES):
        r.gateg_x[n : n + 1, :] = jnp.sum(r.gate_acc[n], axis=0, keepdims=True)
    gate_sum = TileSum(me, links, r.gateg_x, r.gateg_pair, r.gateg_slots)
    gate_sum.start()

    att_back.end()

    @pl.loop(0, 4)
    def _(t):
        att = r.att_in[map_rows(t, 16)].reshape(TILE, CH)
        value = r.mixed[cell_rows(t)].astype(F32) + nn(att, r.w_out[...])
        r.out_map[map_rows(t)] = value.astype(BF16).reshape(4, MAP_COLS, CH)

    flush("out_map").start()
    grad_t = r.grad_mixed_b[...].T
    for c in range(4):
        lane = slice(c * 256, (c + 1) * 256)
        product = nn(grad_t, lanes_of(r.act, 2 * c, slice(None))) * r.gate[:, lane]
        r.project_x[lane, :] = product.T.astype(BF16)
    project_sum = big("project", r.sum_project)
    grad_gate = flat(gate_sum.end())
    grad_logit = grad_gate * gate * (1.0 - gate)
    grad_hidden = wide_product(grad_logit, r.w_excite[...], nt)
    grad_squeezed = grad_hidden * (open_part * (1.0 + squeezed * (1.0 - open_part)))
    r.gate_back[...] = wide_product(grad_squeezed, r.w_squeeze_t[...], nn) * (1.0 / CELLS_TOTAL)

    @pl.loop(0, LANES)
    def _(c):
        lane = aligned(c * 128, 128, 128)
        scale, shift = r.gate[:, lane], r.gate_back[:, lane]
        for t in range(4):
            at = slice(t * TILE, (t + 1) * TILE)
            g = (r.grad_gated[c, at, :] * scale + shift) * r.depth[c, at, :]
            g = g.astype(BF16).astype(F32)
            for a in range(4):
                first = (1 + t * 4 + a) * PAD + 8
                r.grad_pre[c, first : first + MAP_COLS, :] = g[a * 64 : (a + 1) * 64]

        for side, row in ((0, 1), (1, MAP_ROWS)):
            at = pl.ds(row * PAD + 8, MAP_COLS)
            r.pre_rows[side, c] = r.grad_pre[c, at, :].astype(BF16)
        for side, col in ((0, 8), (1, 71)):
            at = pl.ds(PAD + col, MAP_ROWS, stride=PAD)
            r.pre_cols[side, c] = r.grad_pre[c, at, :].astype(BF16)

    for corner, at in enumerate((PAD + 8, PAD + 71, last - PAD + 8, last - PAD + 71)):
        cells = [r.grad_pre[c, at : at + 1, :] for c in range(LANES)]
        cells.append(jnp.zeros((8, 128), F32))
        r.pre_corners[corner] = jnp.concatenate(cells, axis=0).astype(BF16)

    pre_halo = Halo(
        me,
        links,
        (r.pre_rows.at[0], r.pre_rows.at[1]),
        r.pre_cols,
        [r.pre_corners.at[n] for n in range(4)],
        r.pre_rows_in,
        r.pre_cols_in,
        r.pre_corners_in,
    )
    pre_halo.start()

    project_sum.start()
    bias_sum.to_q()
    pair_sum.to_q()
    project_sum.to_q()
    pre_halo.end()

    @pl.loop(0, LANES)
    def _(c):
        r.grad_pre[c, 8:72, :] = r.pre_rows_in[0, c].astype(F32) * up_ok
        r.grad_pre[c, last + 8 : last + 72, :] = r.pre_rows_in[1, c].astype(F32) * down_ok
        left = r.pre_cols_in[0, c].astype(F32) * left_ok
        right = r.pre_cols_in[1, c].astype(F32) * right_ok
        r.grad_pre[c, pl.ds(PAD + 7, MAP_ROWS, stride=PAD), :] = left
        r.grad_pre[c, pl.ds(PAD + 72, MAP_ROWS, stride=PAD), :] = right

    corners = (
        (7, up_ok * left_ok),
        (72, up_ok * right_ok),
        (last + 7, down_ok * left_ok),
        (last + 72, down_ok * right_ok),
    )
    for corner, (at, ok) in enumerate(corners):
        cells = r.pre_corners_in[corner].astype(F32) * ok
        for c in range(LANES):
            r.grad_pre[c, at : at + 1, :] = cells[c : c + 1]

    r.tap_acc[...] = jnp.zeros_like(r.tap_acc)

    def depth_back(c):
        taps = taps_of(c)

        @pl.loop(0, MAP_ROWS // 2)
        def _(n):
            sums = [None] * 2
            inner = [
                r.spread[c, pl.ds(pad_row(1 + n * 2 + i, 8), MAP_COLS), :] for i in range(2)
            ]
            for b in range(3):
                parts = [None] * 3
                for row in range(4):
                    view = r.grad_pre.at[c, pl.ds(pad_row(n * 2 + row), PAD)]
                    v = view[pl.ds(7 + b, MAP_COLS), :]
                    for a in range(3):
                        i = row - a
                        if 0 <= i < 2:
                            term = v * taps[(2 - a) * 3 + 2 - b]
                            sums[i] = term if sums[i] is None else sums[i] + term
                            part = fold(v * inner[i])
                            parts[a] = part if parts[a] is None else parts[a] + part
                for a in range(3):
                    r.tap_acc[c, (2 - a) * 3 + 2 - b] += parts[a]
            for i in range(2):
                at = aligned((n * 2 + i) * MAP_COLS, MAP_COLS, MAP_COLS)
                r.grad_exp[c, at, :] = (sums[i] * r.expanded[c, at, :]).astype(BF16)

    @pl.loop(0, LANES)
    def _(c):
        depth_back(c)

    for c in range(4):
        lane = slice(c * 256, (c + 1) * 256)
        product = nn(r.normed_t[...], lanes_of(r.grad_exp, 2 * c, slice(None)))
        r.expand_x[:, lane] = product.astype(BF16)
    expand_sum = DirectSum(
        me, links, r.expand_x, r.expand_pair, r.expand_summed, r.expand_slots, r.sum_expand
    )
    expand_sum.start()
    bias_sum.to_rows()
    pair_sum.to_rows()
    expand_sum.scatter()
    project_sum.to_rows()

    @pl.loop(0, 4)
    def _(t):
        grad = None
        for c in range(4):
            lane = slice(c * 256, (c + 1) * 256)
            part = nt(lanes_of(r.grad_exp, 2 * c, cell_rows(t)), r.w_expand[:, lane])
            grad = part if grad is None else grad + part
        unit, rstd = centre(r.image[map_rows(t)].reshape(TILE, CH).astype(F32))
        r.norm_acc[0] += fold(grad * unit)
        value = r.grad_mixed[cell_rows(t)] + norm_back(unit, rstd, grad * gain_first)
        r.grad_map[map_rows(t)] = value.astype(BF16).reshape(4, MAP_COLS, CH)

    r.small_x[...] = jnp.zeros_like(r.small_x)
    for c in range(LANES):
        rows = [jnp.sum(r.tap_acc[c, k], axis=0, keepdims=True) for k in range(9)]
        r.small_x[c * 8 : c * 8 + 8, :128] = jnp.concatenate(rows[:8], axis=0)
        r.small_x[c * 8 : c * 8 + 1, 128:] = rows[8]
    for n in range(2):
        sums = jnp.sum(r.norm_acc[n], axis=0, keepdims=True)
        for c in range(2):
            at = c * 8 + 1 + n
            r.small_x[at : at + 1, 128:] = sums[:, c * 128 : (c + 1) * 128]
    small_sum = SmallSum(
        me, links, r.small_x, r.small_pair, r.small_summed, r.small_a, r.small_b, r.sum_small
    )
    flush("grad_map").start()
    small_sum.start()
    bias_sum.back_q()
    pair_sum.back_rows()
    small_sum.to_q()
    expand_sum.gather()
    project_sum.back_rows()
    pair_sum.back_q()
    small_sum.to_rows()
    bias_sum.end()
    flush("sum_bias").start()
    project_sum.back_q()
    small_sum.back_q()
    pair_sum.back_pair()
    expand_sum.back_pair()
    pair_sum.end()
    flush("sum_pair").start()
    project_sum.back_pair()
    small_sum.end()
    flush("sum_small").start()
    rows = [pooled, grad_logit, jnp.pad(hidden, ((0, 0), (0, 960)))]
    rows += [jnp.pad(grad_squeezed, ((0, 0), (0, 960))), jnp.zeros((4, 1024), F32)]
    r.gate_rows[...] = jnp.concatenate(rows, axis=0)
    flush("gate_rows").start()
    expand_sum.end()
    flush("sum_expand").start()
    project_sum.end()
    flush("sum_project").start()
    for name in OUTS:
        flush(name).wait()
    links.finish()


FINAL = dict(
    block_out=((MAP_ROWS, MAP_COLS, CH), BF16),
    grad_image=((MAP_ROWS, MAP_COLS, CH), BF16),
    grad_norm0=((1, CH), F32),
    grad_expand=((CH, 1024), F32),
    grad_depth=((3, 3, 1024), F32),
    grad_squeeze=((64, 1024), F32),
    grad_excite=((64, 1024), F32),
    grad_project=((1024, CH), F32),
    grad_norm1=((1, CH), F32),
    grad_qkv=((CH, 3 * CH), F32),
    grad_out_proj=((CH, CH), F32),
    grad_bias=((HEADS, MEMBERS, MEMBERS), F32),
)


def finish_kernel(*args):
    r = Refs()
    for name, ref in zip(list(OUTS) + list(FINAL) + ["sems"], args, strict=True):
        setattr(r, name, ref)
    copies = [
        pltpu.make_async_copy(r.out_map, r.block_out, r.sems.at[0]),
        pltpu.make_async_copy(r.grad_map, r.grad_image, r.sems.at[1]),
    ]
    for copy in copies:
        copy.start()
    r.grad_expand[...] = r.sum_expand[...].astype(F32)
    r.grad_project[...] = r.sum_project[...].astype(F32)
    r.grad_qkv[...] = r.sum_pair[:, : 3 * CH].astype(F32)
    r.grad_out_proj[...] = r.sum_pair[:, 3 * CH :].astype(F32)
    for h in range(0, HEADS, 2):
        both = r.sum_bias[:, h * 64 : (h + 2) * 64].T
        r.grad_bias[h] = both[:64]
        r.grad_bias[h + 1] = both[64:]
    for k in range(9):
        if k < 8:
            rows = [r.sum_small[c * 8 + k : c * 8 + k + 1, :128] for c in range(LANES)]
        else:
            rows = [r.sum_small[c * 8 : c * 8 + 1, 128:] for c in range(LANES)]
        r.grad_depth[k // 3, k % 3 : k % 3 + 1, :] = jnp.concatenate(rows, axis=1)
    for n, out in enumerate((r.grad_norm0, r.grad_norm1)):
        rows = [r.sum_small[c * 8 + 1 + n : c * 8 + 2 + n, 128:] for c in range(2)]
        out[...] = jnp.concatenate(rows, axis=1)
    pooled, grad_logit = r.gate_rows[0:1, :], r.gate_rows[1:2, :]
    hidden, grad_squeezed = r.gate_rows[2:3, :64], r.gate_rows[3:4, :64]
    r.grad_excite[...] = outer(hidden, grad_logit)
    r.grad_squeeze[...] = outer(grad_squeezed, pooled)
    for copy in copies:
        copy.wait()


def on_device(
    image,
    out_cotangent,
    norm0_gain,
    w_expand,
    w_depth,
    w_squeeze,
    w_excite,
    w_project,
    norm1_gain,
    w_qkv,
    w_out,
    attn_bias,
):
    vmem = pl.BlockSpec(memory_space=pltpu.VMEM)
    any_space = pl.BlockSpec(memory_space=pl.ANY)
    buffers = lambda shapes: [pltpu.VMEM(*shape) for shape in shapes.values()]
    made = pl.pallas_call(
        block_kernel,
        out_shape=[jax.ShapeDtypeStruct(*shape) for shape in OUTS.values()],
        in_specs=[vmem] * len(IN_NAMES) + [any_space] * len(LATE),
        out_specs=[any_space] * len(OUTS),
        scratch_shapes=buffers(LATE)
        + buffers(OUTS)
        + buffers(SCRATCH)
        + [pltpu.SemaphoreType.DMA((n,)) for n in (SEMS, len(LATE), len(OUTS))],
        compiler_params=pltpu.CompilerParams(
            collective_id=0, has_side_effects=True, vmem_limit_bytes=63 * 2**20
        ),
        name="block",
    )(
        image,
        norm0_gain,
        norm1_gain,
        w_depth,
        w_expand,
        out_cotangent.reshape(MEMBERS, GROUPS, CH),
        w_out,
        attn_bias,
        w_squeeze.T,
        w_excite,
        w_project,
        w_qkv,
    )
    final = pl.pallas_call(
        finish_kernel,
        out_shape=[jax.ShapeDtypeStruct(*shape) for shape in FINAL.values()],
        in_specs=[any_space] * 2 + [vmem] * (len(OUTS) - 2),
        out_specs=[any_space] * 2 + [vmem] * (len(FINAL) - 2),
        scratch_shapes=[pltpu.SemaphoreType.DMA((2,))],
        compiler_params=pltpu.CompilerParams(vmem_limit_bytes=63 * 2**20),
        name="finish",
    )(*made)
    final = dict(zip(FINAL, final))
    final["grad_norm0"] = final["grad_norm0"].reshape(CH)
    final["grad_norm1"] = final["grad_norm1"].reshape(CH)
    final["grad_squeeze"] = final["grad_squeeze"].T
    return tuple(final.values())


def solution(mesh):
    mapped = P("row", "col", None)
    return jax.shard_map(
        on_device,
        mesh=mesh,
        in_specs=(mapped, mapped) + (P(),) * 10,
        out_specs=(mapped, mapped) + (P(),) * 10,
        check_vma=False,
    )
```

time: 536 us -> 165 us (0.31); the launches traced: 526 us -> 165 us
  blocking collectives: 205 us -> 0 us
  Pallas kernels: 0 us -> 164 us
  waiting for transfers between devices: 92 us -> 0 us
  starting transfers between devices: 58.4 us -> 0 us
  local copies, waits for them, and re-layouts: 57.7 us -> 0 us
  other arithmetic: 52.7 us -> 0 us
  matrix products: 45 us -> 0 us
  between operations: 15.2 us -> 0.66 us
    psum x3 -> x0, blocking collectives: 205 us -> none  [the longest x1 71.3 us: on_device(): lax.psum((grad_norm0, grad_expand, grad_depth, grad_project, grad_norm1,...]
    pallas_call x0 -> x2, Pallas kernels: none -> 164 us  [the longest x1 128 us: on_device(): pl.pallas_call(block_kernel, out_shape=[jax.ShapeDtypeStruct(*shape) for...]
    psum x1 -> x0, waiting for transfers between devices: 77.8 us -> none  [on_device(): lax.psum((grad_norm0, grad_expand, grad_depth, grad_project, grad_norm1,...]
    dot_general x22 -> x0, matrix products: 45 us -> none  [the longest x8 20.6 us: matmul_last(): product = jnp.dot(flat_rows, right_side, preferred_element_type=jnp.float32)]
    all_to_all x4 -> x0, starting transfers between devices: 37.7 us -> none  [the longest x2 19.5 us: to_grid(): lax.all_to_all(flat_order_out(values), ('row', 'col'), split_axis=0, conc...]
    reduce_sum x8 -> x0, other arithmetic: 25.2 us -> none  [the longest x1 12.4 us: kernel_grad(): jnp.sum(window * grad_pre.astype(jnp.float32), axis=(0, 1))]
    ppermute x8 -> x0, starting transfers between devices: 20.7 us -> none  [the longest x4 11.8 us: with_halo(): lax.ppermute(tail, axis, [(i, (i + 1) % count) for i in range(ends)])]
    another operation x7 -> x0, local copies, waits for them, and re-layouts: 20.5 us -> none  [the longest x2 6.48 us: attention_back(): grad_heads = grad_att.reshape(groups, members, head_count, head_dim)]
  transfers between devices with their start and end apart: 13 -> 0, of which waited for: 7 -> 0; matrix products, arithmetic and copies ran while one was open for 15% -> 0% of each run, Pallas kernels for 0% -> 0%
where the time goes in v2:
time: 165 us
  Pallas kernels  164 us (99%)
    pallas_call x1, Pallas kernels, on_device(): pl.pallas_call(block_kernel, out_shape=[jax.ShapeDtypeStruct(*shape) for...  128 us
    pallas_call x1, Pallas kernels, on_device(): pl.pallas_call(finish_kernel, out_shape=[jax.ShapeDtypeStruct(*shape) for...  36.3 us

profile of v2, /device:TPU:1, one launch (start us, length us, event | category | flops | bytes accessed | tf_op | source)
XLA Modules:
  0.0 164.7 jit_solution(12155055627620934632)
XLA Ops:
  0.6 127.8 %block.1 = (bf16[16,64,256]{2,1,0:T(8,128)(2,1)}, bf16[16,64,256]{2,1,0:T(8,128)(2,1)}, bf16[256,1024]{1,0:T(8,128)(2,1)}, bf16[1024,256]{1,0:T(8,128)(2,1)}, bf...) custom-call(bf16[16,64,256]{2,1,0:T(8,128)(2,1)} %args_0_.4, ...), custom_call_target="tpu_custom_call" | custom-call | tf_op jit(solution)/shard_map/block/pallas_call | solution.py:1166
  128.4 36.3 %finish.1 = (bf16[16,64,256]{2,1,0:T(8,128)(2,1)}, bf16[16,64,256]{2,1,0:T(8,128)(2,1)}, f32[1,256]{1,0:T(1,128)}, f32[256,1024]{1,0:T(8,128)}, f32[3,3,1024]{2,...) custom-call(bf16[16,64,256]{2,1,0:T(8,128)(2,1)} %get-tuple-element., ...), custom_call_target="tpu_custom_call" | custom-call | tf_op jit(solution)/shard_map/finish/pallas_call | solution.py:1193

commit v3 on v2

--- a/solution.py
+++ b/solution.py
@@ -185,126 +185,64 @@
         return jnp.sum(self.slots[...], axis=0)
 
 
-class BigSum:
-    def __init__(self, me, links, x, pair_in, summed, slots_a, total_a, slots_b, out):
+class Scatter:
+    def __init__(self, me, links, x, pair_in, summed, slots):
         self.me, self.links = me, links
-        self.x, self.pair_in, self.summed, self.out = x, pair_in, summed, out
-        self.slots_a, self.total_a, self.slots_b = slots_a, total_a, slots_b
-        self.half = x.shape[0] // 2
-        self.across = x.shape[1] // 128
-        self.sems = [links.pair() for _ in range(6)]
-
-    def half_of(self, ref, core):
-        return ref.at[aligned(core * self.half, self.half, 128)]
-
-    def block(self, ref, base, q, row=None):
-        first = base + lax.div(q, self.across) * 128
-        size = 128
-        if row is not None:
-            first, size = first + row * 16, 16
-        lane = aligned(lax.rem(q, self.across) * 128, 128, 128)
-        return ref.at[aligned(first, size, 16), lane]
+        self.x, self.pair_in, self.summed, self.slots = x, pair_in, summed, slots
+        self.sems = [links.pair() for _ in range(2)]
+
+    def half_of(self, core):
+        return self.x.at[aligned(core * 128, 128, 128)]
+
+    def piece(self, row, q):
+        return self.summed.at[aligned(row * 16, 16, 16), aligned(q * 128, 128, 128)]
 
     def start(self):
-        push(
-            self.half_of(self.x, 1 - self.me.core),
-            self.pair_in,
-            *self.sems[0],
-            self.me.partner(),
-        )
+        push(self.half_of(1 - self.me.core), self.pair_in, *self.sems[0], self.me.partner())
         self.links.sent.append((self.sems[0][0], self.pair_in))
-
-    def to_q(self):
-        arrived(self.pair_in, self.sems[0][1])
-        mine = self.half_of(self.x, self.me.core)
-        for n in range(self.half // 128):
-            at = pl.ds(n * 128, 128)
-            self.summed[at] = (mine[at].astype(F32) + self.pair_in[at].astype(F32)).astype(BF16)
-        for k in range(1, 8):
-            q, device = self.me.q_peer(k)
-            push(
-                self.block(self.summed, 0, q), self.slots_a.at[self.me.q], *self.sems[1], device
-            )
-        self.links.sent.append((self.sems[1][0], self.slots_a.at[pl.ds(0, 7)]))
-
-    def to_rows(self):
-        self.slots_a[self.me.q] = self.block(self.summed, 0, self.me.q)[...]
-        arrived(self.slots_a.at[pl.ds(0, 7)], self.sems[1][1])
-        self.total_a[...] = jnp.sum(self.slots_a[...].astype(F32), axis=0).astype(BF16)
-        for k in range(1, 8):
-            row, device = self.me.row_peer(k)
-            piece = self.total_a.at[aligned(row * 16, 16, 16)]
-            push(piece, self.slots_b.at[self.me.row], *self.sems[2], device)
-        self.links.sent.append((self.sems[2][0], self.slots_b.at[pl.ds(0, 7)]))
-
-    def back_rows(self):
-        me = self.me
-        self.slots_b[me.row] = self.total_a[aligned(me.row * 16, 16, 16)]
-        arrived(self.slots_b.at[pl.ds(0, 7)], self.sems[2][1])
-        total = jnp.sum(self.slots_b[...].astype(F32), axis=0).astype(BF16)
-        piece = self.block(self.out, me.core * self.half, me.q, me.row)
-        piece[...] = total
-        for k in range(1, 8):
-            _, device = me.row_peer(k)
-            push(piece, piece, *self.sems[3], device)
-        self.links.sent.append((self.sems[3][0], self.slots_b.at[pl.ds(0, 7)]))
-
-    def back_q(self):
-        me = self.me
-        arrived(self.slots_b.at[pl.ds(0, 7)], self.sems[3][1])
-        piece = self.block(self.out, me.core * self.half, me.q)
-        for k in range(1, 8):
-            _, device = me.q_peer(k)
-            push(piece, piece, *self.sems[4], device)
-        self.links.sent.append((self.sems[4][0], self.slots_a.at[pl.ds(0, 7)]))
-
-    def back_pair(self):
-        me = self.me
-        arrived(self.slots_a.at[pl.ds(0, 7)], self.sems[4][1])
-        piece = self.half_of(self.out, me.core)
-        push(piece, piece, *self.sems[5], me.partner())
-        self.links.sent.append((self.sems[5][0], self.pair_in))
-
-    def end(self):
-        arrived(self.pair_in, self.sems[5][1])
-
-
-class DirectSum(BigSum):
-    def __init__(self, me, links, x, pair_in, summed, slots, out):
-        super().__init__(me, links, x, pair_in, summed, None, None, None, out)
-        self.slots = slots
 
     def scatter(self):
         me = self.me
         arrived(self.pair_in, self.sems[0][1])
-        mine = self.half_of(self.x, me.core)
-        for n in range(self.half // 128):
-            at = pl.ds(n * 128, 128)
-            self.summed[at] = (mine[at].astype(F32) + self.pair_in[at].astype(F32)).astype(BF16)
-
-        def send(row, q, device):
-            push(
-                self.block(self.summed, 0, q, row), self.slots.at[me.chip], *self.sems[1], device
-            )
-
-        me.every_peer(send)
-        self.slots[me.chip] = self.block(self.summed, 0, me.q, me.row)[...]
+        mine = self.half_of(me.core)
+        self.summed[...] = (mine[...].astype(F32) + self.pair_in[...].astype(F32)).astype(BF16)
+        to = self.slots.at[me.chip]
+        me.every_peer(
+            lambda row, q, device: push(self.piece(row, q), to, *self.sems[1], device)
+        )
+        self.slots[me.chip] = self.piece(me.row, me.q)[...]
+
+    def end(self):
+        arrived(self.slots.at[pl.ds(0, CHIPS - 1)], self.sems[1][1])
         self.links.sent.append((self.sems[1][0], self.slots.at[pl.ds(0, CHIPS - 1)]))
 
-    def gather(self):
-        me = self.me
-        arrived(self.slots.at[pl.ds(0, CHIPS - 1)], self.sems[1][1])
-        piece = self.block(self.out, me.core * self.half, me.q, me.row)
-        piece[...] = jnp.sum(self.slots[...].astype(F32), axis=0).astype(BF16)
-        me.every_peer(lambda row, q, device: push(piece, piece, *self.sems[2], device))
-        self.links.sent.append((self.sems[2][0], self.slots.at[pl.ds(0, CHIPS - 1)]))
+
+class Gather:
+    def __init__(self, me, links, out, like):
+        self.me, self.links, self.out, self.like = me, links, out, like
+        self.width = out.shape[1] // 8
+        self.sems = [links.pair() for _ in range(2)]
+        lane = aligned(me.q * self.width, self.width, 128)
+        self.piece = out.at[aligned(me.core * 128 + me.row * 16, 16, 16), lane]
+
+    def send(self, row, k):
+        push(self.piece, self.piece, *self.sems[0], (row, self.me.cols[k]))
+
+    def send_all(self):
+        self.me.every_peer(
+            lambda row, q, device: push(self.piece, self.piece, *self.sems[0], device)
+        )
 
     def back_pair(self):
         me = self.me
-        arrived(self.slots.at[pl.ds(0, CHIPS - 1)], self.sems[2][1])
-        piece = self.half_of(self.out, me.core)
-        push(piece, piece, *self.sems[5], me.partner())
-        self.links.sent.append((self.sems[5][0], self.pair_in))
+        arrived(self.like.at[pl.ds(0, CHIPS - 1)], self.sems[0][1])
+        self.links.sent.append((self.sems[0][0], self.like.at[pl.ds(0, CHIPS - 1)]))
+        half = self.out.at[aligned(me.core * 128, 128, 128)]
+        push(half, half, *self.sems[1], me.partner())
+        self.links.sent.append((self.sems[1][0], half))
+
+    def end(self):
+        arrived(self.out.at[pl.ds(0, 128)], self.sems[1][1])
 
 
 class SmallSum:
@@ -428,22 +366,19 @@
     out_map=((MAP_ROWS, MAP_COLS, CH), BF16),
     grad_map=((MAP_ROWS, MAP_COLS, CH), BF16),
     sum_expand=((CH, 1024), BF16),
-    sum_project=((1024, CH), BF16),
-    sum_pair=((CH, 1024), BF16),
+    sum_early=((CH, 2048), BF16),
     sum_bias=((MEMBERS, 512), F32),
-    sum_small=((64, 256), F32),
+    sum_taps=((64, 256), F32),
+    sum_norms=((8, 128), F32),
     gate_rows=((8, 1024), F32),
 )
 
 
-def big_scratch(name, rows, width):
+def big_scratch(name):
     return {
-        name + "_x": ((rows, width), BF16),
-        name + "_pair": ((rows // 2, width), BF16),
-        name + "_summed": ((rows // 2, width), BF16),
-        name + "_a": ((8, 128, 128), BF16),
-        name + "_total": ((128, 128), BF16),
-        name + "_b": ((8, 16, 128), BF16),
+        name + "_x": ((CH, 1024), BF16),
+        name + "_pair": ((CH // 2, 1024), BF16),
+        name + "_summed": ((CH // 2, 1024), BF16),
     }
 
 
@@ -511,14 +446,15 @@
     pair_acc=((CH, 1024), F32),
     **tile_scratch("pool"),
     **tile_scratch("gateg"),
-    expand_x=((CH, 1024), BF16),
-    expand_pair=((CH // 2, 1024), BF16),
-    expand_summed=((CH // 2, 1024), BF16),
+    **big_scratch("expand"),
+    **big_scratch("project"),
+    **big_scratch("pair"),
     expand_slots=((CHIPS, 16, 128), BF16),
-    **big_scratch("project", 1024, CH),
-    **big_scratch("pair", CH, 1024),
+    pair_slots=((CHIPS, 16, 128), BF16),
+    project_slots=((CHIPS, 16, 128), BF16),
     **small_scratch("bias", 512),
-    **small_scratch("small", 256),
+    **small_scratch("taps_sum", 256),
+    **tile_scratch("norms"),
 )
 SEMS = 96
 
@@ -625,23 +561,19 @@
     late("dy").wait()
     dy_out = Exchange(me, links, r.dy, r.grid_dy)
 
-    @pl.loop(0, LANES * 4)
-    def _(n):
-        c, t = lax.div(n, 4), lax.rem(n, 4)
+    @pl.loop(0, LANES)
+    def _(c):
         row = lax.rem(me.row + c, ROWS)
-        for k in range(2):
-            q = lax.rem(me.q + t * 2 + k, 8)
-
-            @pl.when(row * 8 + q != me.chip)
-            def _():
-                push(
-                    r.dy.at[row * 8 + q],
-                    r.grid_dy.at[me.chip],
-                    *dy_out.sems,
-                    (row, q * 2 + me.core),
-                )
-
-        r.expanded[c, cell_rows(t), :] = gelu_slope(r.expanded[c, cell_rows(t), :])
+        for t in range(4):
+            for k in (2 * t + 1, 2 * t):
+                if k:
+                    dy_out.send(row, k)
+            at = pl.ds(t * TILE, TILE)
+            r.expanded[c, at, :] = gelu_slope(r.expanded[c, at, :])
+
+        @pl.when(c > 0)
+        def _():
+            dy_out.send(row, 0)
 
     halo.end()
 
@@ -874,12 +806,14 @@
 
     r.pair_x[...] = r.pair_acc[...].astype(BF16)
 
-    def big(name, out):
-        parts = ["x", "pair", "summed", "a", "total", "b"]
-        return BigSum(me, links, *[getattr(r, name + "_" + p) for p in parts], out)
-
-    pair_sum = big("pair", r.sum_pair)
+    def big(name):
+        parts = ["x", "pair", "summed", "slots"]
+        return Scatter(me, links, *[getattr(r, name + "_" + p) for p in parts])
+
+    pair_sum = big("pair")
     pair_sum.start()
+    bias_sum.to_q()
+    pair_sum.scatter()
     gn_back.end()
 
     r.norm_acc[...] = jnp.zeros_like(r.norm_acc)
@@ -908,21 +842,15 @@
     gate_sum = TileSum(me, links, r.gateg_x, r.gateg_pair, r.gateg_slots)
     gate_sum.start()
 
-    att_back.end()
-
-    @pl.loop(0, 4)
-    def _(t):
-        att = r.att_in[map_rows(t, 16)].reshape(TILE, CH)
-        value = r.mixed[cell_rows(t)].astype(F32) + nn(att, r.w_out[...])
-        r.out_map[map_rows(t)] = value.astype(BF16).reshape(4, MAP_COLS, CH)
-
-    flush("out_map").start()
     grad_t = r.grad_mixed_b[...].T
     for c in range(4):
         lane = slice(c * 256, (c + 1) * 256)
         product = nn(grad_t, lanes_of(r.act, 2 * c, slice(None))) * r.gate[:, lane]
-        r.project_x[lane, :] = product.T.astype(BF16)
-    project_sum = big("project", r.sum_project)
+        r.project_x[:, lane] = product.astype(BF16)
+    project_sum = big("project")
+    project_sum.start()
+    bias_sum.to_rows()
+    project_sum.scatter()
     grad_gate = flat(gate_sum.end())
     grad_logit = grad_gate * gate * (1.0 - gate)
     grad_hidden = wide_product(grad_logit, r.w_excite[...], nt)
@@ -965,10 +893,16 @@
     )
     pre_halo.start()
 
-    project_sum.start()
-    bias_sum.to_q()
-    pair_sum.to_q()
-    project_sum.to_q()
+    att_back.end()
+
+    @pl.loop(0, 4)
+    def _(t):
+        att = r.att_in[map_rows(t, 16)].reshape(TILE, CH)
+        value = r.mixed[cell_rows(t)].astype(F32) + nn(att, r.w_out[...])
+        r.out_map[map_rows(t)] = value.astype(BF16).reshape(4, MAP_COLS, CH)
+
+    flush("out_map").start()
+    bias_sum.back_q()
     pre_halo.end()
 
     @pl.loop(0, LANES)
@@ -1020,22 +954,42 @@
                 at = aligned((n * 2 + i) * MAP_COLS, MAP_COLS, MAP_COLS)
                 r.grad_exp[c, at, :] = (sums[i] * r.expanded[c, at, :]).astype(BF16)
 
+    pair_sum.end()
+    project_sum.end()
+    early = Gather(me, links, r.sum_early, r.grid_dy)
+    for n, slots in enumerate((r.pair_slots, r.project_slots)):
+        total = jnp.sum(slots[...].astype(F32), axis=0).astype(BF16)
+        early.piece[:, n * 128 : (n + 1) * 128] = total
+
     @pl.loop(0, LANES)
     def _(c):
         depth_back(c)
+        row = lax.rem(me.row + c, ROWS)
+        for k in range(1, 8):
+            early.send(row, k)
+
+        @pl.when(c > 0)
+        def _():
+            early.send(row, 0)
 
     for c in range(4):
         lane = slice(c * 256, (c + 1) * 256)
         product = nn(r.normed_t[...], lanes_of(r.grad_exp, 2 * c, slice(None)))
         r.expand_x[:, lane] = product.astype(BF16)
-    expand_sum = DirectSum(
-        me, links, r.expand_x, r.expand_pair, r.expand_summed, r.expand_slots, r.sum_expand
+    expand_sum = big("expand")
+    expand_sum.start()
+    for c in range(LANES):
+        rows = [jnp.sum(r.tap_acc[c, k], axis=0, keepdims=True) for k in range(9)]
+        r.taps_sum_x[c * 8 : c * 8 + 8, :128] = jnp.concatenate(rows[:8], axis=0)
+        rows = [rows[8], jnp.zeros((7, 128), F32)]
+        r.taps_sum_x[c * 8 : c * 8 + 8, 128:] = jnp.concatenate(rows, axis=0)
+    parts = ["x", "pair", "summed", "a", "b"]
+    taps_sum = SmallSum(
+        me, links, *[getattr(r, "taps_sum_" + p) for p in parts], r.sum_taps
     )
-    expand_sum.start()
-    bias_sum.to_rows()
-    pair_sum.to_rows()
+    taps_sum.start()
     expand_sum.scatter()
-    project_sum.to_rows()
+    taps_sum.to_q()
 
     @pl.loop(0, 4)
     def _(t):
@@ -1049,47 +1003,36 @@
         value = r.grad_mixed[cell_rows(t)] + norm_back(unit, rstd, grad * gain_first)
         r.grad_map[map_rows(t)] = value.astype(BF16).reshape(4, MAP_COLS, CH)
 
-    r.small_x[...] = jnp.zeros_like(r.small_x)
-    for c in range(LANES):
-        rows = [jnp.sum(r.tap_acc[c, k], axis=0, keepdims=True) for k in range(9)]
-        r.small_x[c * 8 : c * 8 + 8, :128] = jnp.concatenate(rows[:8], axis=0)
-        r.small_x[c * 8 : c * 8 + 1, 128:] = rows[8]
+    flush("grad_map").start()
+    rows = []
     for n in range(2):
         sums = jnp.sum(r.norm_acc[n], axis=0, keepdims=True)
-        for c in range(2):
-            at = c * 8 + 1 + n
-            r.small_x[at : at + 1, 128:] = sums[:, c * 128 : (c + 1) * 128]
-    small_sum = SmallSum(
-        me, links, r.small_x, r.small_pair, r.small_summed, r.small_a, r.small_b, r.sum_small
-    )
-    flush("grad_map").start()
-    small_sum.start()
-    bias_sum.back_q()
-    pair_sum.back_rows()
-    small_sum.to_q()
-    expand_sum.gather()
-    project_sum.back_rows()
-    pair_sum.back_q()
-    small_sum.to_rows()
+        rows += [sums[:, :128], sums[:, 128:]]
+    r.norms_x[...] = jnp.concatenate(rows + [jnp.zeros((4, 128), F32)], axis=0)
+    norms_sum = TileSum(me, links, r.norms_x, r.norms_pair, r.norms_slots)
+    norms_sum.start()
     bias_sum.end()
     flush("sum_bias").start()
-    project_sum.back_q()
-    small_sum.back_q()
-    pair_sum.back_pair()
-    expand_sum.back_pair()
-    pair_sum.end()
-    flush("sum_pair").start()
-    project_sum.back_pair()
-    small_sum.end()
-    flush("sum_small").start()
     rows = [pooled, grad_logit, jnp.pad(hidden, ((0, 0), (0, 960)))]
     rows += [jnp.pad(grad_squeezed, ((0, 0), (0, 960))), jnp.zeros((4, 1024), F32)]
     r.gate_rows[...] = jnp.concatenate(rows, axis=0)
     flush("gate_rows").start()
+    taps_sum.to_rows()
     expand_sum.end()
+    final = Gather(me, links, r.sum_expand, r.expand_slots)
+    final.piece[...] = jnp.sum(r.expand_slots[...].astype(F32), axis=0).astype(BF16)
+    final.send_all()
+    early.back_pair()
+    taps_sum.back_q()
+    early.end()
+    flush("sum_early").start()
+    r.sum_norms[...] = norms_sum.end()
+    flush("sum_norms").start()
+    taps_sum.end()
+    flush("sum_taps").start()
+    final.back_pair()
+    final.end()
     flush("sum_expand").start()
-    project_sum.end()
-    flush("sum_project").start()
     for name in OUTS:
         flush(name).wait()
     links.finish()
@@ -1113,37 +1056,36 @@
 
 def finish_kernel(*args):
     r = Refs()
-    for name, ref in zip(list(OUTS) + list(FINAL) + ["sems"], args, strict=True):
+    for name, ref in zip(list(OUTS) + list(FINAL), args, strict=True):
         setattr(r, name, ref)
-    copies = [
-        pltpu.make_async_copy(r.out_map, r.block_out, r.sems.at[0]),
-        pltpu.make_async_copy(r.grad_map, r.grad_image, r.sems.at[1]),
-    ]
-    for copy in copies:
-        copy.start()
+    r.block_out[...] = r.out_map[...]
+    r.grad_image[...] = r.grad_map[...]
     r.grad_expand[...] = r.sum_expand[...].astype(F32)
-    r.grad_project[...] = r.sum_project[...].astype(F32)
-    r.grad_qkv[...] = r.sum_pair[:, : 3 * CH].astype(F32)
-    r.grad_out_proj[...] = r.sum_pair[:, 3 * CH :].astype(F32)
+    for n in range(8):
+        lane = slice(n * 128, (n + 1) * 128)
+        part = r.sum_early[:, n * 256 : n * 256 + 128].astype(F32)
+        if n < 6:
+            r.grad_qkv[:, lane] = part
+        else:
+            r.grad_out_proj[:, (n - 6) * 128 : (n - 5) * 128] = part
+        r.grad_project[lane, :] = r.sum_early[:, n * 256 + 128 : n * 256 + 256].astype(F32).T
     for h in range(0, HEADS, 2):
         both = r.sum_bias[:, h * 64 : (h + 2) * 64].T
         r.grad_bias[h] = both[:64]
         r.grad_bias[h + 1] = both[64:]
     for k in range(9):
         if k < 8:
-            rows = [r.sum_small[c * 8 + k : c * 8 + k + 1, :128] for c in range(LANES)]
+            rows = [r.sum_taps[c * 8 + k : c * 8 + k + 1, :128] for c in range(LANES)]
         else:
-            rows = [r.sum_small[c * 8 : c * 8 + 1, 128:] for c in range(LANES)]
+            rows = [r.sum_taps[c * 8 : c * 8 + 1, 128:] for c in range(LANES)]
         r.grad_depth[k // 3, k % 3 : k % 3 + 1, :] = jnp.concatenate(rows, axis=1)
     for n, out in enumerate((r.grad_norm0, r.grad_norm1)):
-        rows = [r.sum_small[c * 8 + 1 + n : c * 8 + 2 + n, 128:] for c in range(2)]
+        rows = [r.sum_norms[n * 2 + c : n * 2 + c + 1, :] for c in range(2)]
         out[...] = jnp.concatenate(rows, axis=1)
     pooled, grad_logit = r.gate_rows[0:1, :], r.gate_rows[1:2, :]
     hidden, grad_squeezed = r.gate_rows[2:3, :64], r.gate_rows[3:4, :64]
     r.grad_excite[...] = outer(hidden, grad_logit)
     r.grad_squeeze[...] = outer(grad_squeezed, pooled)
-    for copy in copies:
-        copy.wait()
 
 
 def on_device(
@@ -1193,9 +1135,8 @@
     final = pl.pallas_call(
         finish_kernel,
         out_shape=[jax.ShapeDtypeStruct(*shape) for shape in FINAL.values()],
-        in_specs=[any_space] * 2 + [vmem] * (len(OUTS) - 2),
-        out_specs=[any_space] * 2 + [vmem] * (len(FINAL) - 2),
-        scratch_shapes=[pltpu.SemaphoreType.DMA((2,))],
+        in_specs=[vmem] * len(OUTS),
+        out_specs=[vmem] * len(FINAL),
         compiler_params=pltpu.CompilerParams(vmem_limit_bytes=63 * 2**20),
         name="finish",
     )(*made)

time: 165 us -> 127 us (0.77)
  Pallas kernels: 164 us -> 126 us
    pallas_call x1, Pallas kernels: 36.3 us -> 4.3 us  [on_device(): pl.pallas_call(finish_kernel, out_shape=[jax.ShapeDtypeStruct(*shape) for...]
    pallas_call x1, Pallas kernels: 128 us -> 122 us  [on_device(): pl.pallas_call(block_kernel, out_shape=[jax.ShapeDtypeStruct(*shape) for...]
where the time goes in v3:
time: 127 us
  Pallas kernels  126 us (99%)
    pallas_call x1, Pallas kernels, on_device(): pl.pallas_call(block_kernel, out_shape=[jax.ShapeDtypeStruct(*shape) for...  122 us
    pallas_call x1, Pallas kernels, on_device(): pl.pallas_call(finish_kernel, out_shape=[jax.ShapeDtypeStruct(*shape) for...  4.3 us

profile of v3, /device:TPU:1, one launch (start us, length us, event | category | flops | bytes accessed | tf_op | source)
XLA Modules:
  0.0 127.1 jit_solution(9624177755723461973)
XLA Ops:
  0.6 122.2 %block.1 = (bf16[16,64,256]{2,1,0:T(8,128)(2,1)}, bf16[16,64,256]{2,1,0:T(8,128)(2,1)}, bf16[256,1024]{1,0:T(8,128)(2,1)}, bf16[256,2048]{1,0:T(8,128)(2,1)}, f3...) custom-call(bf16[16,64,256]{2,1,0:T(8,128)(2,1)} %args_0_.4, ...), custom_call_target="tpu_custom_call" | custom-call | tf_op jit(solution)/shard_map/block/pallas_call | solution.py:1108
  122.8 4.3 %finish.1 = (bf16[16,64,256]{2,1,0:T(8,128)(2,1)}, bf16[16,64,256]{2,1,0:T(8,128)(2,1)}, f32[1,256]{1,0:T(1,128)}, f32[256,1024]{1,0:T(8,128)}, f32[3,3,1024]{2,...) custom-call(bf16[16,64,256]{2,1,0:T(8,128)(2,1)} %get-tuple-element., ...), custom_call_target="tpu_custom_call" | custom-call | tf_op jit(solution)/shard_map/finish/pallas_call | solution.py:1135

commit v4 on v3

--- a/solution.py
+++ b/solution.py
@@ -434,6 +434,12 @@
     grad_gated=((LANES, CELLS, 128), F32),
     gate_acc=((LANES, 8, 128), F32),
     grad_pre=((LANES, PADDED, 128), F32),
+    slope_rows=((2, LANES, MAP_COLS, 128), BF16),
+    slope_cols=((2, LANES, 16, 128), BF16),
+    slope_corners=((4, 16, 128), BF16),
+    slope_rows_in=((2, LANES, MAP_COLS, 128), BF16),
+    slope_cols_in=((2, LANES, 16, 128), BF16),
+    slope_corners_in=((4, 16, 128), BF16),
     pre_rows=((2, LANES, MAP_COLS, 128), BF16),
     pre_cols=((2, LANES, 16, 128), BF16),
     pre_rows_in=((2, LANES, MAP_COLS, 128), BF16),
@@ -697,6 +703,38 @@
         r.normed_two[map_rows(t, 16)] = normed.reshape(16, GROUPS, CH)
         grid_out.send_tile(t)
 
+    def pack_edges(ref, width, first, rows_out, cols_out, corners_out):
+        final_row = first + (MAP_ROWS - 1) * width
+
+        @pl.loop(0, LANES)
+        def _(c):
+            for side, at in ((0, first), (1, final_row)):
+                rows_out[side, c] = ref[c, at : at + MAP_COLS, :].astype(BF16)
+            for side, at in ((0, first), (1, first + MAP_COLS - 1)):
+                cells = ref[c, pl.ds(at, MAP_ROWS, stride=width), :]
+                cols_out[side, c] = cells.astype(BF16)
+
+        ends = (first, first + MAP_COLS - 1, final_row, final_row + MAP_COLS - 1)
+        for corner, at in enumerate(ends):
+            cells = [ref[c, at : at + 1, :] for c in range(LANES)]
+            cells.append(jnp.zeros((8, 128), F32))
+            corners_out[corner] = jnp.concatenate(cells, axis=0).astype(BF16)
+
+    def edge_halo(name):
+        parts = ["rows", "cols", "corners", "rows_in", "cols_in", "corners_in"]
+        rows, cols, corners, *arriving = [getattr(r, name + "_" + p) for p in parts]
+        return Halo(
+            me,
+            links,
+            (rows.at[0], rows.at[1]),
+            cols,
+            [corners.at[n] for n in range(4)],
+            *arriving,
+        )
+
+    pack_edges(r.depth, MAP_COLS, 0, r.slope_rows, r.slope_cols, r.slope_corners)
+    slope_halo = edge_halo("slope")
+    slope_halo.start()
     grid_out.end()
 
     @pl.loop(0, 4)
@@ -709,7 +747,7 @@
     head_of = lax.div(lax.broadcasted_iota(jnp.int32, (1, 128), 1), 32)
     masks_f = [(head_of == h).astype(F32) for h in range(4)]
     masks = [m.astype(BF16) for m in masks_f]
-    unroll = 4
+    unroll = 8
 
     def spread_heads(a):
         return jnp.concatenate([a * m for m in masks], axis=0)
@@ -769,8 +807,8 @@
 
     @pl.loop(0, GROUPS // unroll)
     def _(step):
-        for n in range(2):
-            att_back.send_row(lax.rem(me.row + step * 2 + n, ROWS))
+        for n in range(4):
+            att_back.send_row(lax.rem(me.row + step * 4 + n, ROWS))
         total = group_back(step * unroll)
         for n in range(1, unroll):
             total = [a + b for a, b in zip(total, group_back(step * unroll + n))]
@@ -842,6 +880,19 @@
     gate_sum = TileSum(me, links, r.gateg_x, r.gateg_pair, r.gateg_slots)
     gate_sum.start()
 
+    @pl.loop(0, LANES)
+    def _(c):
+        scale = r.gate[:, aligned(c * 128, 128, 128)]
+        for t in range(4):
+            at = slice(t * TILE, (t + 1) * TILE)
+            g = r.grad_gated[c, at, :] * scale * r.depth[c, at, :]
+            for a in range(4):
+                first = (1 + t * 4 + a) * PAD + 8
+                r.grad_pre[c, first : first + MAP_COLS, :] = g[a * 64 : (a + 1) * 64]
+
+    pack_edges(r.grad_pre, PAD, PAD + 8, r.pre_rows, r.pre_cols, r.pre_corners)
+    pre_halo = edge_halo("pre")
+    pre_halo.start()
     grad_t = r.grad_mixed_b[...].T
     for c in range(4):
         lane = slice(c * 256, (c + 1) * 256)
@@ -851,6 +902,8 @@
     project_sum.start()
     bias_sum.to_rows()
     project_sum.scatter()
+    slope_halo.end()
+    pre_halo.end()
     grad_gate = flat(gate_sum.end())
     grad_logit = grad_gate * gate * (1.0 - gate)
     grad_hidden = wide_product(grad_logit, r.w_excite[...], nt)
@@ -859,60 +912,27 @@
 
     @pl.loop(0, LANES)
     def _(c):
-        lane = aligned(c * 128, 128, 128)
-        scale, shift = r.gate[:, lane], r.gate_back[:, lane]
-        for t in range(4):
-            at = slice(t * TILE, (t + 1) * TILE)
-            g = (r.grad_gated[c, at, :] * scale + shift) * r.depth[c, at, :]
-            g = g.astype(BF16).astype(F32)
-            for a in range(4):
-                first = (1 + t * 4 + a) * PAD + 8
-                r.grad_pre[c, first : first + MAP_COLS, :] = g[a * 64 : (a + 1) * 64]
-
-        for side, row in ((0, 1), (1, MAP_ROWS)):
-            at = pl.ds(row * PAD + 8, MAP_COLS)
-            r.pre_rows[side, c] = r.grad_pre[c, at, :].astype(BF16)
-        for side, col in ((0, 8), (1, 71)):
-            at = pl.ds(PAD + col, MAP_ROWS, stride=PAD)
-            r.pre_cols[side, c] = r.grad_pre[c, at, :].astype(BF16)
-
-    for corner, at in enumerate((PAD + 8, PAD + 71, last - PAD + 8, last - PAD + 71)):
-        cells = [r.grad_pre[c, at : at + 1, :] for c in range(LANES)]
-        cells.append(jnp.zeros((8, 128), F32))
-        r.pre_corners[corner] = jnp.concatenate(cells, axis=0).astype(BF16)
-
-    pre_halo = Halo(
-        me,
-        links,
-        (r.pre_rows.at[0], r.pre_rows.at[1]),
-        r.pre_cols,
-        [r.pre_corners.at[n] for n in range(4)],
-        r.pre_rows_in,
-        r.pre_cols_in,
-        r.pre_corners_in,
-    )
-    pre_halo.start()
-
-    att_back.end()
-
-    @pl.loop(0, 4)
-    def _(t):
-        att = r.att_in[map_rows(t, 16)].reshape(TILE, CH)
-        value = r.mixed[cell_rows(t)].astype(F32) + nn(att, r.w_out[...])
-        r.out_map[map_rows(t)] = value.astype(BF16).reshape(4, MAP_COLS, CH)
-
-    flush("out_map").start()
-    bias_sum.back_q()
-    pre_halo.end()
-
-    @pl.loop(0, LANES)
-    def _(c):
-        r.grad_pre[c, 8:72, :] = r.pre_rows_in[0, c].astype(F32) * up_ok
-        r.grad_pre[c, last + 8 : last + 72, :] = r.pre_rows_in[1, c].astype(F32) * down_ok
-        left = r.pre_cols_in[0, c].astype(F32) * left_ok
-        right = r.pre_cols_in[1, c].astype(F32) * right_ok
-        r.grad_pre[c, pl.ds(PAD + 7, MAP_ROWS, stride=PAD), :] = left
-        r.grad_pre[c, pl.ds(PAD + 72, MAP_ROWS, stride=PAD), :] = right
+        shift = r.gate_back[:, aligned(c * 128, 128, 128)]
+
+        def beside(part, slope, ok):
+            return (part.astype(F32) + shift * slope.astype(F32)) * ok
+
+        for row in range(MAP_ROWS):
+            first = (1 + row) * PAD + 8
+            at = slice(first, first + MAP_COLS)
+            slope = r.depth[c, row * MAP_COLS : (row + 1) * MAP_COLS, :]
+            value = r.grad_pre[c, at, :] + shift * slope
+            r.grad_pre[c, at, :] = value.astype(BF16).astype(F32)
+        rows = [
+            beside(r.pre_rows_in[n, c], r.slope_rows_in[n, c], ok)
+            for n, ok in enumerate((up_ok, down_ok))
+        ]
+        r.grad_pre[c, 8:72, :] = rows[0]
+        r.grad_pre[c, last + 8 : last + 72, :] = rows[1]
+        for n, (col, ok) in enumerate(((7, left_ok), (72, right_ok))):
+            r.grad_pre[c, pl.ds(PAD + col, MAP_ROWS, stride=PAD), :] = beside(
+                r.pre_cols_in[n, c], r.slope_cols_in[n, c], ok
+            )
 
     corners = (
         (7, up_ok * left_ok),
@@ -920,10 +940,17 @@
         (last + 7, down_ok * left_ok),
         (last + 72, down_ok * right_ok),
     )
+    shifts = jnp.concatenate(
+        [r.gate_back[:, c * 128 : (c + 1) * 128] for c in range(LANES)], axis=0
+    )
     for corner, (at, ok) in enumerate(corners):
-        cells = r.pre_corners_in[corner].astype(F32) * ok
+        slope = r.slope_corners_in[corner].astype(F32)[:8]
+        cells = r.pre_corners_in[corner].astype(F32)[:8] + shifts * slope
+        cells = cells * ok
         for c in range(LANES):
             r.grad_pre[c, at : at + 1, :] = cells[c : c + 1]
+
+    bias_sum.back_q()
 
     r.tap_acc[...] = jnp.zeros_like(r.tap_acc)
 
@@ -1004,6 +1031,15 @@
         r.grad_map[map_rows(t)] = value.astype(BF16).reshape(4, MAP_COLS, CH)
 
     flush("grad_map").start()
+    att_back.end()
+
+    @pl.loop(0, 4)
+    def _(t):
+        att = r.att_in[map_rows(t, 16)].reshape(TILE, CH)
+        value = r.mixed[cell_rows(t)].astype(F32) + nn(att, r.w_out[...])
+        r.out_map[map_rows(t)] = value.astype(BF16).reshape(4, MAP_COLS, CH)
+
+    flush("out_map").start()
     rows = []
     for n in range(2):
         sums = jnp.sum(r.norm_acc[n], axis=0, keepdims=True)
@@ -1056,11 +1092,30 @@
 
 def finish_kernel(*args):
     r = Refs()
-    for name, ref in zip(list(OUTS) + list(FINAL), args, strict=True):
+    names = ["hbm_" + n for n in OUTS] + ["hbm_" + n for n in FINAL]
+    names += list(OUTS) + list(FINAL)[2:] + ["in_sems", "out_sems"]
+    for name, ref in zip(names, args, strict=True):
         setattr(r, name, ref)
-    r.block_out[...] = r.out_map[...]
-    r.grad_image[...] = r.grad_map[...]
+    r.block_out, r.grad_image = r.out_map, r.grad_map
+
+    def fetch(name):
+        at = list(OUTS).index(name)
+        return pltpu.make_async_copy(getattr(r, "hbm_" + name), getattr(r, name), r.in_sems.at[at])
+
+    def flush(name):
+        at = list(FINAL).index(name)
+        return pltpu.make_async_copy(
+            getattr(r, name), getattr(r, "hbm_" + name), r.out_sems.at[at]
+        )
+
+    order = ["sum_expand", "sum_early", "out_map", "grad_map"]
+    order += ["sum_bias", "sum_taps", "sum_norms", "gate_rows"]
+    for name in order:
+        fetch(name).start()
+    fetch("sum_expand").wait()
     r.grad_expand[...] = r.sum_expand[...].astype(F32)
+    flush("grad_expand").start()
+    fetch("sum_early").wait()
     for n in range(8):
         lane = slice(n * 128, (n + 1) * 128)
         part = r.sum_early[:, n * 256 : n * 256 + 128].astype(F32)
@@ -1068,7 +1123,18 @@
             r.grad_qkv[:, lane] = part
         else:
             r.grad_out_proj[:, (n - 6) * 128 : (n - 5) * 128] = part
+    flush("grad_qkv").start()
+    flush("grad_out_proj").start()
+    for n in range(8):
+        lane = slice(n * 128, (n + 1) * 128)
         r.grad_project[lane, :] = r.sum_early[:, n * 256 + 128 : n * 256 + 256].astype(F32).T
+    flush("grad_project").start()
+    fetch("out_map").wait()
+    flush("block_out").start()
+    fetch("grad_map").wait()
+    flush("grad_image").start()
+    for name in order[4:]:
+        fetch(name).wait()
     for h in range(0, HEADS, 2):
         both = r.sum_bias[:, h * 64 : (h + 2) * 64].T
         r.grad_bias[h] = both[:64]
@@ -1086,6 +1152,12 @@
     hidden, grad_squeezed = r.gate_rows[2:3, :64], r.gate_rows[3:4, :64]
     r.grad_excite[...] = outer(hidden, grad_logit)
     r.grad_squeeze[...] = outer(grad_squeezed, pooled)
+    early = ["block_out", "grad_image", "grad_expand", "grad_qkv", "grad_out_proj", "grad_project"]
+    for name in FINAL:
+        if name not in early:
+            flush(name).start()
+    for name in FINAL:
+        flush(name).wait()
 
 
 def on_device(
@@ -1135,8 +1207,11 @@
     final = pl.pallas_call(
         finish_kernel,
         out_shape=[jax.ShapeDtypeStruct(*shape) for shape in FINAL.values()],
-        in_specs=[vmem] * len(OUTS),
-        out_specs=[vmem] * len(FINAL),
+        in_specs=[any_space] * len(OUTS),
+        out_specs=[any_space] * len(FINAL),
+        scratch_shapes=buffers(OUTS)
+        + buffers(FINAL)[2:]
+        + [pltpu.SemaphoreType.DMA((n,)) for n in (len(OUTS), len(FINAL))],
         compiler_params=pltpu.CompilerParams(vmem_limit_bytes=63 * 2**20),
         name="finish",
     )(*made)

time: 127 us -> 122 us (0.961)
  Pallas kernels: 126 us -> 121 us
    pallas_call x1, Pallas kernels: 122 us -> 118 us  [on_device(): pl.pallas_call(block_kernel, out_shape=[jax.ShapeDtypeStruct(*shape) for...]
where the time goes in v4:
time: 122 us
  Pallas kernels  121 us (99%)
    pallas_call x1, Pallas kernels, on_device(): pl.pallas_call(block_kernel, out_shape=[jax.ShapeDtypeStruct(*shape) for...  118 us
    pallas_call x1, Pallas kernels, on_device(): pl.pallas_call(finish_kernel, out_shape=[jax.ShapeDtypeStruct(*shape) for...  3.71 us

profile of v4, /device:TPU:1, one launch (start us, length us, event | category | flops | bytes accessed | tf_op | source)
XLA Modules:
  0.0 122.1 jit_solution(9442347369061676703)
XLA Ops:
  0.6 117.8 %block.1 = (bf16[16,64,256]{2,1,0:T(8,128)(2,1)}, bf16[16,64,256]{2,1,0:T(8,128)(2,1)}, bf16[256,1024]{1,0:T(8,128)(2,1)}, bf16[256,2048]{1,0:T(8,128)(2,1)}, f3...) custom-call(bf16[16,64,256]{2,1,0:T(8,128)(2,1)} %args_0_.4, ...), custom_call_target="tpu_custom_call" | custom-call | tf_op jit(solution)/shard_map/block/pallas_call | solution.py:1180
  118.4 3.7 %finish.1 = (bf16[16,64,256]{2,1,0:T(8,128)(2,1)}, bf16[16,64,256]{2,1,0:T(8,128)(2,1)}, f32[1,256]{1,0:T(1,128)}, f32[256,1024]{1,0:T(8,128)}, f32[3,3,1024]{2,...) custom-call(bf16[16,64,256]{2,1,0:T(8,128)(2,1)} %get-tuple-element., ...), custom_call_target="tpu_custom_call" | custom-call | tf_op jit(solution)/shard_map/finish/pallas_call | solution.py:1207

commit v5 on v4

--- a/solution.py
+++ b/solution.py
@@ -217,6 +217,33 @@
         self.links.sent.append((self.sems[1][0], self.slots.at[pl.ds(0, CHIPS - 1)]))
 
 
+class HalvesScatter(Scatter):
+    def __init__(self, *args):
+        super().__init__(*args)
+        self.pairs = [self.sems[0], self.links.pair()]
+
+    def start(self, n):
+        lane = pl.ds(n * 512, 512)
+        other = aligned((1 - self.me.core) * 128, 128, 128)
+        to = self.pair_in.at[:, lane]
+        push(self.x.at[other, lane], to, *self.pairs[n], self.me.partner())
+        self.links.sent.append((self.pairs[n][0], to))
+
+    def scatter(self):
+        me = self.me
+        mine = aligned(me.core * 128, 128, 128)
+        for n in range(2):
+            lane = pl.ds(n * 512, 512)
+            arrived(self.pair_in.at[:, lane], self.pairs[n][1])
+            total = self.x[mine, lane].astype(F32) + self.pair_in[:, lane].astype(F32)
+            self.summed[:, lane] = total.astype(BF16)
+        to = self.slots.at[me.chip]
+        me.every_peer(
+            lambda row, q, device: push(self.piece(row, q), to, *self.sems[1], device)
+        )
+        self.slots[me.chip] = self.piece(me.row, me.q)[...]
+
+
 class Gather:
     def __init__(self, me, links, out, like):
         self.me, self.links, self.out, self.like = me, links, out, like
@@ -352,8 +379,10 @@
             self.links.sent.append((self.sems[n][0], buf))
 
 
-IN_NAMES = ["image", "norm0_gain", "norm1_gain", "w_depth", "w_expand"]
+IN_NAMES = ["norm0_gain", "norm1_gain", "w_depth"]
 LATE = dict(
+    image=((MAP_ROWS, MAP_COLS, CH), BF16),
+    w_expand=((CH, 1024), BF16),
     dy=((MEMBERS, GROUPS, CH), BF16),
     w_out=((CH, CH), BF16),
     bias=((HEADS, MEMBERS, MEMBERS), F32),
@@ -508,10 +537,6 @@
 
     for name in LATE:
         late(name).start()
-    gain_first = r.norm0_gain[...].astype(F32).reshape(1, CH)
-    gain_second = r.norm1_gain[...].astype(F32).reshape(1, CH)
-    for a in range(3):
-        r.taps[a * 3 : a * 3 + 3, :] = r.w_depth[a].astype(F32)
     off = r.image.shape[0] - 1
 
     barrier = pltpu.get_barrier_semaphore()
@@ -526,6 +551,12 @@
                 barrier, inc=1, device_id=me.beside(up, right), device_id_type=MESH
             )
 
+    gain_first = r.norm0_gain[...].astype(F32).reshape(1, CH)
+    gain_second = r.norm1_gain[...].astype(F32).reshape(1, CH)
+    for a in range(3):
+        r.taps[a * 3 : a * 3 + 3, :] = r.w_depth[a].astype(F32)
+
+    late("image").wait()
     for side, col in ((0, 0), (1, MAP_COLS - 16)):
         rows = []
         for i in range(MAP_ROWS):
@@ -533,17 +564,18 @@
             rows.append(part[0:1] if side == 0 else part[15:16])
         r.edge_cols[side] = jnp.concatenate(rows, axis=0).astype(BF16)
 
-    @pl.loop(0, 4)
+    @pl.loop(0, 4, unroll=4)
     def _(t):
         x = r.image[map_rows(t)].reshape(TILE, CH).astype(F32)
         unit, _ = centre(x)
         r.normed[cell_rows(t)] = (unit * gain_first).astype(BF16)
 
+    late("w_expand").wait()
+
     @pl.loop(0, 4)
     def _(t):
-        @pl.loop(0, 4)
-        def _(c):
-            e = nn(r.normed[cell_rows(t)], r.w_expand[:, aligned(c * 256, 256, 256)])
+        for c in range(4):
+            e = nn(r.normed[cell_rows(t)], r.w_expand[:, c * 256 : (c + 1) * 256])
             s = gelu(e).astype(BF16).astype(F32)
             for h in range(2):
                 lane = slice(h * 128, (h + 1) * 128)
@@ -645,7 +677,7 @@
                 total = total + fold(value)
             return total
 
-        total = lax.fori_loop(0, 4, block, jnp.zeros((8, 128), F32))
+        total = lax.fori_loop(0, 4, block, jnp.zeros((8, 128), F32), unroll=2)
         r.pool_x[pl.ds(c, 1), :] = jnp.sum(total, axis=0, keepdims=True)
 
     pool = TileSum(me, links, r.pool_x, r.pool_pair, r.pool_slots)
@@ -688,7 +720,7 @@
     grid_out = Exchange(me, links, r.normed_two, r.grid_x)
     start_tile = lax.div(me.row, 2)
 
-    @pl.loop(0, 4)
+    @pl.loop(0, 4, unroll=2)
     def _(step):
         t = lax.rem(start_tile + step, 4)
         total = r.image[map_rows(t)].reshape(TILE, CH).astype(F32)
@@ -737,7 +769,7 @@
     slope_halo.start()
     grid_out.end()
 
-    @pl.loop(0, 4)
+    @pl.loop(0, 4, unroll=2)
     def _(t):
         x = r.grid_x[map_rows(t, 16)].reshape(TILE, CH)
         qkv = nn(x, r.w_qkv[...])
@@ -821,7 +853,7 @@
 
     gn_back = Exchange(me, links, r.gn_out, r.gn_in)
 
-    @pl.loop(0, 4)
+    @pl.loop(0, 4, unroll=2)
     def _(step):
         t = lax.rem(start_tile + step, 4)
         gn = nt(packed_tile(t), r.w_qkv[...]).astype(BF16)
@@ -844,9 +876,9 @@
 
     r.pair_x[...] = r.pair_acc[...].astype(BF16)
 
-    def big(name):
+    def big(name, kind=Scatter):
         parts = ["x", "pair", "summed", "slots"]
-        return Scatter(me, links, *[getattr(r, name + "_" + p) for p in parts])
+        return kind(me, links, *[getattr(r, name + "_" + p) for p in parts])
 
     pair_sum = big("pair")
     pair_sum.start()
@@ -857,7 +889,7 @@
     r.norm_acc[...] = jnp.zeros_like(r.norm_acc)
     r.gate_acc[...] = jnp.zeros_like(r.gate_acc)
 
-    @pl.loop(0, 4)
+    @pl.loop(0, 4, unroll=2)
     def _(t):
         unit, rstd = centre(r.mixed[cell_rows(t)].astype(F32))
         gn = r.gn_in[map_rows(t, 16)].reshape(TILE, CH).astype(F32)
@@ -957,7 +989,7 @@
     def depth_back(c):
         taps = taps_of(c)
 
-        @pl.loop(0, MAP_ROWS // 2)
+        @pl.loop(0, MAP_ROWS // 2, unroll=2)
         def _(n):
             sums = [None] * 2
             inner = [
@@ -999,12 +1031,13 @@
         def _():
             early.send(row, 0)
 
+    expand_sum = big("expand", HalvesScatter)
     for c in range(4):
         lane = slice(c * 256, (c + 1) * 256)
         product = nn(r.normed_t[...], lanes_of(r.grad_exp, 2 * c, slice(None)))
         r.expand_x[:, lane] = product.astype(BF16)
-    expand_sum = big("expand")
-    expand_sum.start()
+        if c % 2:
+            expand_sum.start(c // 2)
     for c in range(LANES):
         rows = [jnp.sum(r.tap_acc[c, k], axis=0, keepdims=True) for k in range(9)]
         r.taps_sum_x[c * 8 : c * 8 + 8, :128] = jnp.concatenate(rows[:8], axis=0)
@@ -1191,10 +1224,10 @@
         ),
         name="block",
     )(
-        image,
         norm0_gain,
         norm1_gain,
         w_depth,
+        image,
         w_expand,
         out_cotangent.reshape(MEMBERS, GROUPS, CH),
         w_out,

time: 122 us -> 120 us (0.984)
  Pallas kernels: 121 us -> 119 us
    pallas_call x1, Pallas kernels: 118 us -> 115 us  [on_device(): pl.pallas_call(block_kernel, out_shape=[jax.ShapeDtypeStruct(*shape) for...]
where the time goes in v5:
time: 120 us; the launch traced here: 119 us
  Pallas kernels  119 us (99%)
    pallas_call x1, Pallas kernels, on_device(): pl.pallas_call(block_kernel, out_shape=[jax.ShapeDtypeStruct(*shape) for...  115 us
    pallas_call x1, Pallas kernels, on_device(): pl.pallas_call(finish_kernel, out_shape=[jax.ShapeDtypeStruct(*shape) for...  3.71 us

profile of v5, /device:TPU:1, one launch (start us, length us, event | category | flops | bytes accessed | tf_op | source)
XLA Modules:
  0.0 119.3 jit_solution(2722891311804379786)
XLA Ops:
  0.6 114.9 %block.1 = (bf16[16,64,256]{2,1,0:T(8,128)(2,1)}, bf16[16,64,256]{2,1,0:T(8,128)(2,1)}, bf16[256,1024]{1,0:T(8,128)(2,1)}, bf16[256,2048]{1,0:T(8,128)(2,1)}, f3...) custom-call(bf16[256]{0:T(256)(128)(2,1)} %args_0_.4, bf16[256]{0:T(256)(128)(2,1)} %args_1_.4, ...), custom_call_target="tpu_custom_call" | custom-call | tf_op jit(solution)/shard_map/block/pallas_call | solution.py:1213
  115.6 3.7 %finish.1 = (bf16[16,64,256]{2,1,0:T(8,128)(2,1)}, bf16[16,64,256]{2,1,0:T(8,128)(2,1)}, f32[1,256]{1,0:T(1,128)}, f32[256,1024]{1,0:T(8,128)}, f32[3,3,1024]{2,...) custom-call(bf16[16,64,256]{2,1,0:T(8,128)(2,1)} %get-tuple-element., ...), custom_call_target="tpu_custom_call" | custom-call | tf_op jit(solution)/shard_map/finish/pallas_call | solution.py:1240

commit v6 on v5

--- a/solution.py
+++ b/solution.py
@@ -677,7 +677,7 @@
                 total = total + fold(value)
             return total
 
-        total = lax.fori_loop(0, 4, block, jnp.zeros((8, 128), F32), unroll=2)
+        total = lax.fori_loop(0, 4, block, jnp.zeros((8, 128), F32), unroll=4)
         r.pool_x[pl.ds(c, 1), :] = jnp.sum(total, axis=0, keepdims=True)
 
     pool = TileSum(me, links, r.pool_x, r.pool_pair, r.pool_slots)
@@ -720,7 +720,7 @@
     grid_out = Exchange(me, links, r.normed_two, r.grid_x)
     start_tile = lax.div(me.row, 2)
 
-    @pl.loop(0, 4, unroll=2)
+    @pl.loop(0, 4, unroll=4)
     def _(step):
         t = lax.rem(start_tile + step, 4)
         total = r.image[map_rows(t)].reshape(TILE, CH).astype(F32)
@@ -769,7 +769,7 @@
     slope_halo.start()
     grid_out.end()
 
-    @pl.loop(0, 4, unroll=2)
+    @pl.loop(0, 4, unroll=4)
     def _(t):
         x = r.grid_x[map_rows(t, 16)].reshape(TILE, CH)
         qkv = nn(x, r.w_qkv[...])
@@ -853,7 +853,7 @@
 
     gn_back = Exchange(me, links, r.gn_out, r.gn_in)
 
-    @pl.loop(0, 4, unroll=2)
+    @pl.loop(0, 4, unroll=4)
     def _(step):
         t = lax.rem(start_tile + step, 4)
         gn = nt(packed_tile(t), r.w_qkv[...]).astype(BF16)
@@ -889,7 +889,7 @@
     r.norm_acc[...] = jnp.zeros_like(r.norm_acc)
     r.gate_acc[...] = jnp.zeros_like(r.gate_acc)
 
-    @pl.loop(0, 4, unroll=2)
+    @pl.loop(0, 4, unroll=4)
     def _(t):
         unit, rstd = centre(r.mixed[cell_rows(t)].astype(F32))
         gn = r.gn_in[map_rows(t, 16)].reshape(TILE, CH).astype(F32)
@@ -989,7 +989,7 @@
     def depth_back(c):
         taps = taps_of(c)
 
-        @pl.loop(0, MAP_ROWS // 2, unroll=2)
+        @pl.loop(0, MAP_ROWS // 2, unroll=4)
         def _(n):
             sums = [None] * 2
             inner = [

time: 120 us -> 119 us (level)
  no operation moved by 1% of the time
where the time goes in v6:
time: 119 us
  Pallas kernels  118 us (99%)
    pallas_call x1, Pallas kernels, on_device(): pl.pallas_call(block_kernel, out_shape=[jax.ShapeDtypeStruct(*shape) for...  115 us
    pallas_call x1, Pallas kernels, on_device(): pl.pallas_call(finish_kernel, out_shape=[jax.ShapeDtypeStruct(*shape) for...  3.71 us

profile of v6, /device:TPU:1, one launch (start us, length us, event | category | flops | bytes accessed | tf_op | source)
XLA Modules:
  0.0 119.0 jit_solution(15806395217844313678)
XLA Ops:
  0.6 114.5 %block.1 = (bf16[16,64,256]{2,1,0:T(8,128)(2,1)}, bf16[16,64,256]{2,1,0:T(8,128)(2,1)}, bf16[256,1024]{1,0:T(8,128)(2,1)}, bf16[256,2048]{1,0:T(8,128)(2,1)}, f3...) custom-call(bf16[256]{0:T(256)(128)(2,1)} %args_0_.4, bf16[256]{0:T(256)(128)(2,1)} %args_1_.4, ...), custom_call_target="tpu_custom_call" | custom-call | tf_op jit(solution)/shard_map/block/pallas_call | solution.py:1213
  115.2 3.7 %finish.1 = (bf16[16,64,256]{2,1,0:T(8,128)(2,1)}, bf16[16,64,256]{2,1,0:T(8,128)(2,1)}, f32[1,256]{1,0:T(1,128)}, f32[256,1024]{1,0:T(8,128)}, f32[3,3,1024]{2,...) custom-call(bf16[16,64,256]{2,1,0:T(8,128)(2,1)} %get-tuple-element., ...), custom_call_target="tpu_custom_call" | custom-call | tf_op jit(solution)/shard_map/finish/pallas_call | solution.py:1240
